TPU v7x, 32 devices: a whole 2x2x4 slice. The times are simulated.
32 devices in a mesh: dp: 2 (over x), expert: 4 (over z), tensor: 4 (over y, core).
Axes of the slice: x: 2, y: 2, z: 4, core: 2. Of those that a mesh axis runs over, the one named last changes fastest.
Arguments:
- tokens: bfloat16 [192, 3072], P(('dp', 'expert', 'tensor')), parts along dimension 0, may hold values from -200 to 200
- norm_gain: float32 [3072], replicated, may hold values from 0.1 to 1.9
- router: bfloat16 [3072, 4], replicated, may hold values from -0.109375 to 0.109375
- up_weight: bfloat16 [4, 3072, 16384], P('expert', None, 'tensor'), may hold values from -0.109375 to 0.109375
- down_weight: bfloat16 [4, 3072, 16384], P('expert', None, 'tensor'), may hold values from -0.046875 to 0.046875
- expert_ids: int32 [192, 2], P(('dp', 'expert', 'tensor')), parts along dimension 0, may hold values from 0 to 3, as said below
- bin_slots: int32 [192, 2], P(('dp', 'expert', 'tensor')), parts along dimension 0, may hold values from 0 to 14, as said below
- kept_mask: int32 [192, 2], P(('dp', 'expert', 'tensor')), parts along dimension 0, may hold values from 0 to 1, as said below
- grad_out: bfloat16 [192, 3072], P(('dp', 'expert', 'tensor')), parts along dimension 0, may hold values from -6 to 6
Outputs:
- mixed: bfloat16 [192, 3072], P(('dp', 'expert', 'tensor')), parts along dimension 0
- grad_tokens: bfloat16 [192, 3072], P(('dp', 'expert', 'tensor')), parts along dimension 0
There are 2 independent parts, one for each index of `dp`. A program takes and returns all parts, laid end to end along the dimension named above; an argument that names none is the same for every part. Nothing has to cross between parts.
Inputs may be any that keep to these rules, and one draw needn't show every extreme that they name: `expert_ids`: each token names 2 different experts. `bin_slots`: in each group the choices are taken in order of token, first choice before second; a choice is kept while its expert has fewer than 15 kept choices of the group and then holds the number of kept choices of that group and expert before it; a dropped choice holds 0. In every group some expert receives 15 kept choices. `kept_mask`: follows the rule stated for bin_slots.
All inputs are finite; a program needn't handle non-finite values.
Results may differ from a plain program's by a relative error of at most 0.0069.
Values may be sent and summed in bfloat16 or wider, within the bound.
No kernel may reach another device: no remote copies, remote signals or barrier semaphores. Data moves between devices by JAX's collectives and lax.ppermute only.
A program may use at most 128 MiB of HBM per device.

v0:
```python
import jax
import jax.numpy as jnp
from jax import lax
from jax.sharding import PartitionSpec as P

D = 3072
GCAP = 15


root_two_pi = 0.7978845608028654
cubic_term = 0.044715


def gelu_tanh(inputs):
    return (
        0.5
        * inputs
        * (1.0 + jnp.tanh(root_two_pi * (inputs + cubic_term * inputs * inputs * inputs)))
    )


def gelu_slope(inputs):
    inner_tanh = jnp.tanh(root_two_pi * (inputs + cubic_term * inputs * inputs * inputs))
    return 0.5 * (1.0 + inner_tanh) + 0.5 * inputs * (
        1.0 - inner_tanh * inner_tanh
    ) * root_two_pi * (1.0 + 3.0 * cubic_term * inputs * inputs)


def gate_values(normed, router, expert_ids):
    logits = jnp.dot(normed, router, preferred_element_type=jnp.float32)
    choose = (
        expert_ids[:, :, None] == jnp.arange(router.shape[1], dtype=jnp.int32)[None, None, :]
    ).astype(jnp.float32)
    picked = jnp.sum(choose * logits[:, None, :], axis=2)
    first_gate = 1.0 / (1.0 + jnp.exp(picked[:, 1] - picked[:, 0]))
    second_gate = 1.0 / (1.0 + jnp.exp(picked[:, 0] - picked[:, 1]))
    return (jnp.stack([first_gate, second_gate], axis=1), choose)


def shards(
    tokens, norm_gain, router, up_weight, down_weight, expert_ids, bin_slots, kept_mask, grad_out
):
    tok_rows = tokens.shape[0]
    experts = router.shape[1]
    sources = lax.axis_size("expert")
    my_expert = lax.axis_index("expert")
    widened = tokens.astype(jnp.float32)
    meansq = jnp.mean(widened * widened, axis=1, keepdims=True)
    inverse = lax.rsqrt(meansq + 1e-06)
    normed = (widened * inverse * norm_gain).astype(jnp.bfloat16)
    gate_pair, choose = gate_values(normed, router, expert_ids)
    kept_float = kept_mask.astype(jnp.float32)
    table_ids, table_slots, table_kept = (
        lax.all_gather(expert_ids, "expert", axis=0, tiled=True),
        lax.all_gather(bin_slots, "expert", axis=0, tiled=True),
        lax.all_gather(kept_mask, "expert", axis=0, tiled=True),
    )
    accepts = (table_ids == my_expert) & (table_kept == 1)
    slot_range = jnp.arange(GCAP, dtype=jnp.int32)
    placed = jnp.sum(
        ((table_slots[None, :, :] == slot_range[:, None, None]) & accepts[None, :, :]).astype(
            jnp.float32
        ),
        axis=2,
    ).astype(jnp.bfloat16)
    weighted = (
        (kept_float * gate_pair)[:, :, None] * grad_out.astype(jnp.float32)[:, None, :]
    ).astype(jnp.bfloat16)
    target = expert_ids * GCAP + bin_slots
    rows_all = jnp.arange(experts * GCAP, dtype=jnp.int32)
    matches = (
        (rows_all[:, None, None] == target[None, :, :]) & (kept_mask[None, :, :] == 1)
    ).astype(jnp.bfloat16)
    fill_in = jnp.dot(jnp.sum(matches, axis=2), normed, preferred_element_type=jnp.float32)
    fill_grad = jnp.einsum("rjk,jkd->rd", matches, weighted, preferred_element_type=jnp.float32)
    stacked = jnp.stack([fill_in, fill_grad], axis=1).reshape(experts, GCAP, 2, D)
    summed = lax.psum_scatter(
        stacked.astype(jnp.bfloat16), "expert", scatter_dimension=0, tiled=True
    ).astype(jnp.float32)
    bin_pair = summed[0].astype(jnp.bfloat16)
    weight_in = up_weight[0]
    weight_out = down_weight[0]
    contract = (((1,), (1,)), ((), ()))
    segment = lax.all_gather(bin_pair, "tensor", axis=0, tiled=True)
    front_part = jnp.dot(segment[:, 0], weight_in, preferred_element_type=jnp.float32)
    rear_part = jnp.dot(segment[:, 1], weight_out, preferred_element_type=jnp.float32)
    gathered = jnp.stack([front_part, rear_part], axis=1)
    hidden = gathered[:, 0]
    active = gelu_tanh(hidden).astype(jnp.bfloat16)
    back_hidden = (gathered[:, 1] * gelu_slope(hidden)).astype(jnp.bfloat16)
    forward_part = lax.dot_general(active, weight_out, contract, preferred_element_type=jnp.float32)
    backward_part = lax.dot_general(
        back_hidden, weight_in, contract, preferred_element_type=jnp.float32
    )
    result = lax.psum_scatter(
        jnp.stack([forward_part, backward_part], axis=1), "tensor", scatter_dimension=0, tiled=True
    )
    out_pair = result.astype(jnp.bfloat16).reshape(GCAP, 2 * D)
    reply = lax.dot_general(
        placed, out_pair, (((0,), (0,)), ((), ())), preferred_element_type=jnp.float32
    ).astype(jnp.bfloat16)
    reply = reply.reshape(sources, tok_rows, 2 * D)
    answers = lax.all_to_all(reply, "expert", split_axis=0, concat_axis=0, tiled=True)
    chosen = jnp.einsum(
        "jke,ejd->jkd",
        choose.astype(jnp.bfloat16),
        answers[:, :, :D],
        preferred_element_type=jnp.float32,
    )
    mixed = jnp.sum(gate_pair[:, :, None] * chosen, axis=1).astype(jnp.bfloat16)
    gate_grad = jnp.sum(grad_out.astype(jnp.float32)[:, None, :] * chosen, axis=2)
    spread = gate_pair[:, 0] * gate_pair[:, 1] * (gate_grad[:, 0] - gate_grad[:, 1])
    logit_grad = jnp.stack([spread, -spread], axis=1)
    router_grad = jnp.sum(logit_grad[:, :, None] * choose, axis=1)
    normed_grad = jnp.sum(answers[:, :, D:].astype(jnp.float32), axis=0) + jnp.dot(
        router_grad, router.astype(jnp.float32).T, precision=lax.Precision.HIGHEST
    )
    upstream = normed_grad * norm_gain
    grad_tokens = inverse * (
        upstream - widened * inverse * inverse * jnp.mean(upstream * widened, axis=1, keepdims=True)
    )
    return (mixed, grad_tokens.astype(jnp.bfloat16))


def solution(mesh):
    placed = (
        P(("dp", "expert", "tensor"), None),
        P(),
        P(),
        P("expert", None, "tensor"),
        P("expert", None, "tensor"),
        P(("dp", "expert", "tensor"), None),
        P(("dp", "expert", "tensor"), None),
        P(("dp", "expert", "tensor"), None),
        P(("dp", "expert", "tensor"), None),
    )
    return jax.shard_map(
        shards,
        mesh=mesh,
        in_specs=placed,
        out_specs=(P(("dp", "expert", "tensor"), None), P(("dp", "expert", "tensor"), None)),
        check_vma=False,
    )
```

profile of v0, /device:TPU:0, one launch (start us, length us, event | category | flops | bytes accessed | tf_op | source)
XLA Modules:
  0.0 172.3 jit_solution(16565069379719774276)
XLA Ops:
  7.2 0.8 copy.87
  8.7 0.8 convert_element_type.69
  9.5 0.9 fusion.59
  10.4 0.8 copy.82
  11.2 1.0 fusion.69
  12.4 0.7 multiply_add_fusion.1
  14.0 1.1 fusion.25
  15.3 1.7 copy.89
  17.0 1.2 dynamic-slice
  18.2 1.2 dynamic-slice.2
  19.4 12.9 %all-gather.3 = s32[4,6,2]{1,2,0:T(2,128)S(1)} all-gather(s32[1,6,2]{1,2,0:T(2,128)} %bitcast.71), channel_id=1, replica_groups=mesh['dp'=2,'expert'=4,'tensor'=4] {'expert'}, dimensions={0}, use_global_device_ids=true | all-gather | bytes 240 | tf_op jit(solution)/shard_map/all_gather | solution.py:56
  32.3 8.2 %all-gather.2 = s32[4,6,2]{1,2,0:T(2,128)S(1)} all-gather(s32[1,6,2]{1,2,0:T(2,128)} %bitcast.70), channel_id=1, replica_groups=mesh['dp'=2,'expert'=4,'tensor'=4] {'expert'}, dimensions={0}, use_global_device_ids=true | all-gather | bytes 240 | tf_op jit(solution)/shard_map/all_gather | solution.py:54
  40.6 9.7 %all-gather.1 = s32[4,6,2]{1,2,0:T(2,128)S(1)} all-gather(s32[1,6,2]{1,2,0:T(2,128)} %bitcast.72), channel_id=1, replica_groups=mesh['dp'=2,'expert'=4,'tensor'=4] {'expert'}, dimensions={0}, use_global_device_ids=true | all-gather | bytes 240 | tf_op jit(solution)/shard_map/all_gather | solution.py:55
  51.1 11.4 %all-reduce.5.cloned.1.call-done = bf16[4,15,2,3072]{3,2,1,0:T(2,128)(2,1)} async-done(((bf16[4,15,2,3072]{3,2,1,0:T(2,128)(2,1)}), bf16[4,15,2,3072]{3,2,1,0:T(2,128)(2,1)}) %all-reduce.5.cloned.1.call-update) | async-done | bytes 737296
  62.4 1.7 dynamic-slice_bitcast_fusion
  64.1 8.3 %all-gather = bf16[1,60,2,3072]{3,2,0,1:T(2,128)(2,1)S(1)} all-gather(bf16[1,15,2,3072]{3,2,0,1:T(2,128)(2,1)S(1)} %dynamic-slice_bitcast_fusion), channel_id=2, replica_groups=mesh['dp'=2,'expert'=4,'tensor'=4] {'tensor'}, dimensions={1}, use_global_device_ids=true | all-gather | bytes 921600 | tf_op jit(solution)/shard_map/all_gather | solution.py:84
  72.6 10.5 %fusion.6 = f32[60,4096]{1,0:T(8,128)S(1)} fusion(bf16[1,3072,4096]{2,1,0:T(8,128)(2,1)} %param.12, bf16[60,2,3072]{2,0,1:T(8,128)(2,1)S(1)} %bitcast.66), kind=kOutput, calls=%fused_computation.6 | convolution fusion | flops 1509949440 | bytes 26542080 | tf_op jit(solution)/shard_map/dot_general | solution.py:85
  83.1 20.1 %fusion.16 = f32[60,1,3072]{2,0,1:T(8,128)S(1)} fusion(bf16[1,3072,4096]{2,1,0:T(8,128)(2,1)} %param.12, bf16[1,3072,4096]{2,1,0:T(8,128)(2,1)} %param.13, f32[60,4096]{1,0:T(8,128)S(1)} %fusion.6, bf16[60,2,3072]{2,0,1:T(8,128)(2,1)S(1)} %bitcast.67), kind=kOutput, calls=%fused_computation.11 | convolution fusion | flops 3024568320 | bytes 52510720 | tf_op jit(solution)/shard_map/dot_general | solution.py:92
  103.2 12.5 %fusion.21 = f32[60,1,3072]{2,0,1:T(8,128)S(1)} fusion(bf16[1,3072,4096]{2,1,0:T(8,128)(2,1)} %param.13, f32[60,4096]{1,0:T(8,128)S(1)} %fusion.6), kind=kOutput, calls=%fused_computation.12 | convolution fusion | flops 1512161280 | bytes 26886144 | tf_op jit(solution)/shard_map/dot_general | solution.py:91
  115.8 1.1 copy.92
  117.0 30.5 %all-reduce.6 = bf16[60,2,3072]{2,1,0:T(2,128)(2,1)S(1)} all-reduce(f32[60,2,3072]{2,1,0:T(2,128)S(1)} %copy.92), channel_id=4, replica_groups=mesh['dp'=2,'expert'=4,'tensor'=4] {'tensor'}, use_global_device_ids=true, to_apply=%region_5.0.clone | all-reduce | flops 368640 | bytes 2211840
  148.2 14.8 %all_to_all.5 = bf16[4,6,6144]{2,1,0:T(8,128)(2,1)S(1)} all-to-all(bf16[4,6,6144]{2,1,0:T(8,128)(2,1)S(1)} %reshape.48), channel_id=1, replica_groups=mesh['dp'=2,'expert'=4,'tensor'=4] {'expert'}, dimensions={0} | all-to-all | bytes 589824 | tf_op jit(solution)/shard_map/all_to_all | solution.py:103
  163.0 1.1 multiply_reduce_fusion
  164.8 0.7 fusion.58
  (39 shorter events, 3.7 us)
Async XLA Ops:
  7.2 4.0 %copy-start = (bf16[3072,4]{0,1:T(4,128)(2,1)S(1)}, bf16[3072,4]{0,1:T(4,128)(2,1)}, u32[]{:S(2)}) copy-start(bf16[3072,4]{0,1:T(4,128)(2,1)} %param.11) | copy-start | bytes 73732
  7.2 55.3 %all-reduce.5.cloned.1.call-start = ((), (), s32[]{:S(2)}) async-start(), calls=%async_computation.1 | async-start | bytes 1474560
  103.2 61.2 %copy-start.1 = (bf16[6,3072]{1,0:T(8,128)(2,1)S(1)}, bf16[6,3072]{1,0:T(8,128)(2,1)}, u32[]{:S(2)}) copy-start(bf16[6,3072]{1,0:T(8,128)(2,1)} %param.9) | copy-start | bytes 110596
  103.2 61.2 %copy-start.2 = (f32[3072]{0:T(1024)S(1)}, f32[3072]{0:T(1024)}, u32[]{:S(2)}) copy-start(f32[3072]{0:T(1024)} %param.10) | copy-start | bytes 36868
Sparse Core Ops, SparseCore 0:
  17.1 45.3 all-reduce.4
where the time goes:
time: 173 us; the launch traced here: 172 us
  blocking collectives  84.4 us (49%)
  matrix products  47.2 us (27%)
  between operations  14.9 us (9%)
  waiting for transfers between devices  11.4 us (7%)
  local copies, waits for them, and re-layouts  9.49 us (5%)
  other arithmetic  4.92 us (3%)
    unnamed x1, blocking collectives  30.5 us
    dot_general x1, matrix products, shards(): lax.dot_general(back_hidden, weight_in, contract, preferred_element_type=...  20.1 us
    all_to_all x1, blocking collectives, shards(): lax.all_to_all(reply, 'expert', split_axis=0, concat_axis=0, tiled=True)  14.8 us
    all_gather x1, blocking collectives, shards(): lax.all_gather(kept_mask, 'expert', axis=0, tiled=True)  12.9 us
    dot_general x1, matrix products, shards(): lax.dot_general(active, weight_out, contract, preferred_element_type=jnp....  12.5 us
    unnamed x2, waiting for transfers between devices  11.4 us
    dot_general x1, matrix products, shards(): jnp.dot(segment[:, 0], weight_in, preferred_element_type=jnp.float32)  10.5 us
    all_gather x1, blocking collectives, shards(): lax.all_gather(bin_slots, 'expert', axis=0, tiled=True)  9.74 us
  transfers between devices with their start and end apart: 1, of which 1 were waited for; matrix products, arithmetic and copies ran while one was open for 2% of the time, Pallas kernels for 0%

commit v1 on v0

v1 whole, which is shorter than its diff:
```python
import functools

import jax
import jax.numpy as jnp
from jax import lax
from jax.experimental import pallas as pl
from jax.experimental.pallas import tpu as pltpu
from jax.sharding import PartitionSpec as P

GCAP = 15
SLOTS = 16
PAD = 8
LANES = 128
CHUNK = 512

root_two_pi = 0.7978845608028654
cubic_term = 0.044715

VM = pl.BlockSpec(memory_space=pltpu.VMEM)
SM = pl.BlockSpec(memory_space=pltpu.SMEM)


def gelu_both(v):
    t = jnp.tanh(root_two_pi * (v + cubic_term * v * v * v))
    value = 0.5 * v * (1.0 + t)
    slope = 0.5 * (1.0 + t) + 0.5 * v * (1.0 - t * t) * root_two_pi * (
        1.0 + 3.0 * cubic_term * v * v
    )
    return value, slope


def column(ref, choice, rows):
    row = lax.broadcasted_iota(jnp.int32, (rows, LANES), 0)
    out = jnp.zeros((rows, LANES), jnp.int32)
    for r in range(rows):
        out = jnp.where(row == r, ref[choice, r], out)
    return out


def pack_kernel(ids, slots, kept, tok, grad, gain, router, *outs):
    messages, gates_ref = outs[:-1], outs[-1]
    rows, width = tok.shape
    experts = router.shape[0]
    me = lax.axis_index("expert")
    x = tok[...].astype(jnp.float32)
    g = grad[...].astype(jnp.float32)
    inverse = lax.rsqrt(jnp.mean(x * x, axis=1, keepdims=True) + 1e-06)
    normed = (x * inverse * gain[...]).astype(jnp.bfloat16)
    wide = normed.astype(jnp.float32)
    id0, id1 = column(ids, 0, rows), column(ids, 1, rows)
    slot0, slot1 = column(slots, 0, rows), column(slots, 1, rows)
    kept0, kept1 = column(kept, 0, rows), column(kept, 1, rows)
    pick0 = jnp.zeros((rows, LANES), jnp.float32)
    pick1 = jnp.zeros((rows, LANES), jnp.float32)
    for e in range(experts):
        logit = jnp.sum(wide * router[e : e + 1, :].astype(jnp.float32), axis=1, keepdims=True)
        pick0 = jnp.where(id0 == e, logit, pick0)
        pick1 = jnp.where(id1 == e, logit, pick1)
    gate0 = 1.0 / (1.0 + jnp.exp(pick1 - pick0))
    gate1 = 1.0 / (1.0 + jnp.exp(pick0 - pick1))
    gates_ref[0, ...] = gate0
    gates_ref[1, ...] = gate1
    for k, out in enumerate(messages):
        expert = me ^ k
        take0 = (id0 == expert) & (kept0 == 1)
        take1 = (id1 == expert) & (kept1 == 1)
        gate = jnp.where(take0, gate0, jnp.where(take1, gate1, 0.0))
        slot = jnp.where(take0, slot0, jnp.where(take1, slot1, -1))
        out[:, : 2 * width] = jnp.zeros((PAD, 2 * width), jnp.bfloat16)
        out[:, 2 * width :] = jnp.full((PAD, LANES), -1.0, jnp.bfloat16)
        out[0:rows, :width] = normed
        out[0:rows, width : 2 * width] = (gate[:, 0:1] * g).astype(jnp.bfloat16)
        out[0:rows, 2 * width :] = slot.astype(jnp.float32).astype(jnp.bfloat16)


def bin_kernel(width, *refs):
    messages, (bins, placed_ref) = refs[:-2], refs[-2:]
    rows = jnp.concatenate([m[...].astype(jnp.float32) for m in messages], axis=0)
    lane = lax.broadcasted_iota(jnp.int32, (rows.shape[0], LANES), 1).astype(jnp.float32)
    placed = jnp.where(rows[:, 2 * width :] == lane, 1.0, 0.0)
    placed_ref[...] = placed
    onehot = placed.T[:SLOTS].astype(jnp.bfloat16)
    packed = rows[:, : 2 * width].astype(jnp.bfloat16)
    filled = jnp.dot(onehot, packed, preferred_element_type=jnp.float32).astype(jnp.bfloat16)
    bins[0:SLOTS, :] = filled[:, :width]
    bins[SLOTS : 2 * SLOTS, :] = filled[:, width:]


def expert_kernel(groups, *refs):
    bins = refs[:groups]
    up, down, keep, send, x, g, acc_out, acc_back = refs[groups:]
    step = pl.program_id(0)
    rows = groups * SLOTS

    @pl.when(step == 0)
    def _():
        x[...] = jnp.zeros_like(x)
        g[...] = jnp.zeros_like(g)
        for j in range(groups):
            x[j * SLOTS : (j + 1) * SLOTS, :] = bins[j][0:SLOTS, :]
            g[j * SLOTS : (j + 1) * SLOTS, :] = bins[j][SLOTS : 2 * SLOTS, :]
        acc_out[...] = jnp.zeros_like(acc_out)
        acc_back[...] = jnp.zeros_like(acc_back)

    w_in, w_out = up[0], down[0]
    hidden = jnp.dot(x[...], w_in, preferred_element_type=jnp.float32)[:rows]
    back_act = jnp.dot(g[...], w_out, preferred_element_type=jnp.float32)[:rows]
    value, slope = gelu_both(hidden)
    active = value.astype(jnp.bfloat16)
    back_hidden = (back_act * slope).astype(jnp.bfloat16)
    over = (((1,), (1,)), ((), ()))
    acc_out[...] += lax.dot_general(w_out, active, over, preferred_element_type=jnp.float32)
    acc_back[...] += lax.dot_general(w_in, back_hidden, over, preferred_element_type=jnp.float32)

    @pl.when(step == pl.num_programs(0) - 1)
    def _():
        width = x.shape[1]
        for c in range(0, width, 512):
            for half, acc in ((0, acc_out), (1, acc_back)):
                part = acc[c : c + 512, :].T.astype(jnp.bfloat16)
                for j in range(groups):
                    to = send if j % 2 else keep
                    at = (j // 2) * 2 * SLOTS + half * SLOTS
                    to[at : at + SLOTS, c : c + 512] = part[j * SLOTS : (j + 1) * SLOTS]


def sum_reply_kernel(n_parts, *refs):
    parts, placed, replies = refs[:n_parts], refs[n_parts], refs[n_parts + 1 :]
    width = parts[0].shape[1]
    total = parts[0][0 : 2 * SLOTS, :].astype(jnp.float32)
    for p in parts[1:]:
        total = total + p[0 : 2 * SLOTS, :].astype(jnp.float32)
    total = total.astype(jnp.bfloat16)
    onehot = placed[...][:, :SLOTS].astype(jnp.bfloat16)
    for half in (0, 1):
        rows = total[half * SLOTS : (half + 1) * SLOTS, :]
        spread = jnp.dot(onehot, rows, preferred_element_type=jnp.float32)
        for k, out in enumerate(replies):
            out[:, half * width : (half + 1) * width] = spread[k * PAD : (k + 1) * PAD].astype(
                jnp.bfloat16
            )


def finish_kernel(ids, tok, grad, gain, router, gates, *refs):
    replies, (mixed, grad_tokens) = refs[:-2], refs[-2:]
    rows, width = tok.shape
    experts = router.shape[0]
    me = lax.axis_index("expert")
    x = tok[...].astype(jnp.float32)
    g = grad[...].astype(jnp.float32)
    inverse = lax.rsqrt(jnp.mean(x * x, axis=1, keepdims=True) + 1e-06)
    id0, id1 = column(ids, 0, rows), column(ids, 1, rows)
    gate0, gate1 = gates[0][:, 0:1], gates[1][:, 0:1]
    chosen0 = jnp.zeros((rows, width), jnp.float32)
    chosen1 = jnp.zeros((rows, width), jnp.float32)
    back = jnp.zeros((rows, width), jnp.float32)
    for k, reply in enumerate(replies):
        expert = me ^ k
        row = reply[0:rows, :].astype(jnp.float32)
        chosen0 = jnp.where(id0[:, 0:1] == expert, row[:, :width], chosen0)
        chosen1 = jnp.where(id1[:, 0:1] == expert, row[:, :width], chosen1)
        back = back + row[:, width:]
    mixed[...] = (gate0 * chosen0 + gate1 * chosen1).astype(jnp.bfloat16)
    grad0 = jnp.sum(g * chosen0, axis=1, keepdims=True)
    grad1 = jnp.sum(g * chosen1, axis=1, keepdims=True)
    spread = gate0 * gate1 * (grad0 - grad1)
    for e in range(experts):
        line = router[e : e + 1, :].astype(jnp.float32)
        weight = jnp.where(id0[:, 0:1] == e, spread, 0.0) - jnp.where(
            id1[:, 0:1] == e, spread, 0.0
        )
        back = back + weight * line
    upstream = back * gain[...]
    mean = jnp.mean(upstream * x, axis=1, keepdims=True)
    grad_tokens[...] = (inverse * (upstream - x * inverse * inverse * mean)).astype(jnp.bfloat16)


def call(body, out_shape, in_specs, args, **kwargs):
    out_specs = jax.tree.map(lambda _: VM, out_shape)
    return pl.pallas_call(
        body, out_shape=out_shape, in_specs=in_specs, out_specs=out_specs, **kwargs
    )(*args)


def shards(
    tokens, norm_gain, router, up_weight, down_weight, expert_ids, bin_slots, kept_mask, grad_out
):
    rows, width = tokens.shape
    hidden = up_weight.shape[2]
    experts = lax.axis_size("expert")
    groups = lax.axis_size("tensor")
    bf16, f32 = jnp.bfloat16, jnp.float32

    def swap(array, axis, mask):
        n = lax.axis_size(axis)
        return lax.ppermute(array, axis, [(i, i ^ mask) for i in range(n)])

    ids, slots, kept = expert_ids.T, bin_slots.T, kept_mask.T
    gain, lines = norm_gain.reshape(1, width), router.T

    message = jax.ShapeDtypeStruct((PAD, 2 * width + LANES), bf16)
    *messages, gates = call(
        pack_kernel,
        [message] * experts + [jax.ShapeDtypeStruct((2, rows, LANES), f32)],
        [SM] * 3 + [VM] * 4,
        (ids, slots, kept, tokens, grad_out, gain, lines),
    )
    arrived = [messages[0]] + [swap(messages[k], "expert", k) for k in range(1, experts)]

    own, placed = call(
        functools.partial(bin_kernel, width),
        [
            jax.ShapeDtypeStruct((2 * SLOTS, width), bf16),
            jax.ShapeDtypeStruct((experts * PAD, LANES), f32),
        ],
        [VM] * experts,
        arrived,
    )

    bins = {0: own}
    mask = groups // 2
    while mask:
        bins.update({j | mask: swap(b, "tensor", mask) for j, b in bins.items()})
        mask //= 2

    tall = max(groups * SLOTS, 128)
    chunk = min(CHUNK, hidden)
    half = jax.ShapeDtypeStruct((groups * SLOTS, width), bf16)
    whole = pl.BlockSpec((2 * SLOTS, width), lambda i: (0, 0))
    weight = pl.BlockSpec((1, width, chunk), lambda i: (0, 0, i))
    keep, send = pl.pallas_call(
        functools.partial(expert_kernel, groups),
        out_shape=[half, half],
        grid=(hidden // chunk,),
        in_specs=[whole] * groups + [weight] * 2,
        out_specs=[pl.BlockSpec(half.shape, lambda i: (0, 0))] * 2,
        scratch_shapes=[
            pltpu.VMEM((tall, width), bf16),
            pltpu.VMEM((tall, width), bf16),
            pltpu.VMEM((width, groups * SLOTS), f32),
            pltpu.VMEM((width, groups * SLOTS), f32),
        ],
        compiler_params=pltpu.CompilerParams(vmem_limit_bytes=48 * 2**20),
    )(*[bins[j] for j in range(groups)], up_weight, down_weight)

    got = swap(send, "tensor", 1)
    mask = 2
    left = {2 * i: slice(2 * SLOTS * i, 2 * SLOTS * (i + 1)) for i in range(groups // 2)}
    sums = {
        j: (keep[s].astype(f32) + got[s].astype(f32)) for j, s in left.items() if j
    }
    firsts = [keep, got]
    while mask < groups:
        going = {j: sums[j].astype(bf16) for j in sums if j & mask}
        came = {j ^ mask: swap(a, "tensor", mask) for j, a in going.items()}
        for j, a in came.items():
            if j == 0:
                firsts.append(a)
            else:
                sums[j] = sums[j] + a.astype(f32)
        sums = {j: a for j, a in sums.items() if not j & mask}
        mask *= 2

    replies = call(
        functools.partial(sum_reply_kernel, len(firsts)),
        [jax.ShapeDtypeStruct((PAD, 2 * width), bf16)] * experts,
        [VM] * (len(firsts) + 1),
        (*firsts, placed),
    )
    answers = [replies[0]] + [swap(replies[k], "expert", k) for k in range(1, experts)]

    result = jax.ShapeDtypeStruct((rows, width), bf16)
    mixed, grad_tokens = call(
        finish_kernel,
        [result, result],
        [SM] + [VM] * (5 + experts),
        (ids, tokens, grad_out, gain, lines, gates, *answers),
    )
    return mixed, grad_tokens


def solution(mesh):
    split = P(("dp", "expert", "tensor"), None)
    weights = P("expert", None, "tensor")
    return jax.shard_map(
        shards,
        mesh=mesh,
        in_specs=(split, P(), P(), weights, weights, split, split, split, split),
        out_specs=(split, split),
        check_vma=False,
    )
```

time: 173 us -> 79.3 us (0.46)
  blocking collectives: 84.4 us -> 0 us
  matrix products: 47.2 us -> 0 us
  Pallas kernels: 0 us -> 33.7 us
  waiting for transfers between devices: 11.4 us -> 28.3 us
  between operations: 14.9 us -> 0.68 us
  starting transfers between devices: 0.04 us -> 13.3 us
  local copies, waits for them, and re-layouts: 9.49 us -> 2.98 us
  other arithmetic: 4.92 us -> 0.05 us
    dot_general x9 -> x0, matrix products: 47.2 us -> none  [the longest x1 20.1 us: shards(): lax.dot_general(back_hidden, weight_in, contract, preferred_element_type=...]
    all_gather x4 -> x0, blocking collectives: 39.1 us -> none  [the longest x1 12.9 us: shards(): lax.all_gather(kept_mask, 'expert', axis=0, tiled=True)]
    pallas_call x0 -> x5, Pallas kernels: none -> 33.7 us  [the longest x1 25.4 us: shards(): pl.pallas_call(functools.partial(expert_kernel, groups), out_shape=[half,...]
    unnamed x1 -> x0, blocking collectives: 30.5 us -> none
    ppermute x0 -> x11, waiting for transfers between devices: none -> 28.3 us  [swap(): return lax.ppermute(array, axis, [(i, i ^ mask) for i in range(n)])]
    all_to_all x1 -> x0, blocking collectives: 14.8 us -> none  [shards(): lax.all_to_all(reply, 'expert', split_axis=0, concat_axis=0, tiled=True)]
    ppermute x0 -> x11, starting transfers between devices: none -> 13.3 us  [swap(): return lax.ppermute(array, axis, [(i, i ^ mask) for i in range(n)])]
    unnamed x2 -> x0, waiting for transfers between devices: 11.4 us -> none
  transfers between devices with their start and end apart: 1 -> 11, of which waited for: 1 -> 8; matrix products, arithmetic and copies ran while one was open for 2% -> 0% of each run, Pallas kernels for 0% -> 0%
where the time goes in v1:
time: 79.3 us; the launch traced here: 79 us
  Pallas kernels  33.7 us (42%)
  waiting for transfers between devices  28.3 us (36%)
  starting transfers between devices  13.3 us (17%)
  local copies, waits for them, and re-layouts  2.98 us (4%)
    ppermute x11, waiting for transfers between devices, swap(): return lax.ppermute(array, axis, [(i, i ^ mask) for i in range(n)])  28.3 us
    pallas_call x1, Pallas kernels, shards(): pl.pallas_call(functools.partial(expert_kernel, groups), out_shape=[half,...  25.4 us
    ppermute x11, starting transfers between devices, swap(): return lax.ppermute(array, axis, [(i, i ^ mask) for i in range(n)])  13.3 us
    pallas_call x4, Pallas kernels, call(): pl.pallas_call(body, out_shape=out_shape, in_specs=in_specs, out_specs=ou...  8.22 us
    unnamed x20, local copies, waits for them, and re-layouts  2.98 us
  transfers between devices with their start and end apart: 11, of which 8 were waited for; matrix products, arithmetic and copies ran while one was open for 0% of the time, Pallas kernels for 0%

profile of v1, /device:TPU:0, one launch (start us, length us, event | category | flops | bytes accessed | tf_op | source)
XLA Modules:
  0.0 79.0 jit_solution(12452419125242143036)
XLA Ops:
  0.6 1.9 %shard_map.104 = (bf16[8,6272]{1,0:T(8,128)(2,1)}, bf16[8,6272]{1,0:T(8,128)(2,1)}, bf16[8,6272]{1,0:T(8,128)(2,1)}, bf16[8,6272]{1,0:T(8,128)(2,1)}, f32[2,6,128]{2,1,0:T(8,128)}) custom-call(s32[2,6]{1,0:T(2,128)} %bitcast.9, s32[2,6]{1,0:T(2,128)} %bitcast.11, s32[2,6]{1,0:T(2,128)} %bitcast.12, bf16[6,3072]{1,0:T(8,128)(2,1)} %tok.3, ...), custom_call_target="tpu_custom_call" | custom-call | tf_op jit(solution)/shard_map/pallas_call | solution.py:180
  2.5 3.0 %collective-permute-start = (bf16[8,6272]{1,0:T(8,128)(2,1)}, bf16[8,6272]{1,0:T(8,128)(2,1)S(1)}, u32[]{:S(2)}, u32[]{:S(2)}) collective-permute-start(bf16[8,6272]{1,0:T(8,128)(2,1)} %get-tuple-element.17), channel_id=1, source_target_pairs={{0,4},{4,0},{8,12},{12,8},{1,5},{5,1},{9,13},{13,9},{2,6},{6,2},{1... | collective-permute-start | bytes 301064 | tf_op jit(solution)/shard_map/ppermute | solution.py:196
  5.5 2.6 %collective-permute-start.1 = (bf16[8,6272]{1,0:T(8,128)(2,1)}, bf16[8,6272]{1,0:T(8,128)(2,1)S(1)}, u32[]{:S(2)}, u32[]{:S(2)}) collective-permute-start(bf16[8,6272]{1,0:T(8,128)(2,1)} %get-tuple-element.18), channel_id=1, source_target_pairs={{0,8},{4,12},{8,0},{12,4},{1,9},{5,13},{9,1},{13,5},{2,10},{6,14},... | collective-permute-start | bytes 301064 | tf_op jit(solution)/shard_map/ppermute | solution.py:196
  8.1 0.5 collective-permute-done.refs_1_
  8.6 7.7 %collective-permute-done.1.refs_2_ = bf16[8,6272]{1,0:T(8,128)(2,1)S(1)} collective-permute-done((bf16[8,6272]{1,0:T(8,128)(2,1)}, bf16[8,6272]{1,0:T(8,128)(2,1)S(1)}, u32[]{:S(2)}, u32[]{:S(2)}) %collective-permute-start.1) | collective-permute-done | bytes 100384 | tf_op jit(solution)/shard_map/ppermute | solution.py:196
  16.3 0.6 copy-done.5
  17.0 2.0 %shard_map.105 = (bf16[32,3072]{1,0:T(8,128)(2,1)}, f32[32,128]{1,0:T(8,128)}) custom-call(bf16[8,6272]{1,0:T(8,128)(2,1)} %get-tuple-element.16.refs_0_, bf16[8,6272]{1,0:T(8,128)(2,1)} %copy-done.4, bf16[8,6272]{1,0:T(8,128)(2,1)} %copy-done.5, bf16[8,6272]{1,0:T(8,128)(2,1)} %copy-done.6), custom_call_target="tpu_custom_call" | custom-call | tf_op jit(solution)/shard_map/pallas_call | solution.py:180
  19.0 1.5 %collective-permute-start.4 = (bf16[32,3072]{1,0:T(8,128)(2,1)}, bf16[32,3072]{1,0:T(8,128)(2,1)S(1)}, u32[]{:S(2)}, u32[]{:S(2)}) collective-permute-start(bf16[32,3072]{1,0:T(8,128)(2,1)} %get-tuple-element.20.refs_0_), channel_id=1, source_target_pairs={{0,2},{1,3},{2,0},{3,1},{4,6},{5,7},{6,4},{7,5},{8,10},{9,11},{10,... | collective-permute-start | bytes 589832 | tf_op jit(solution)/shard_map/ppermute | solution.py:196
  20.5 4.4 %collective-permute-done.4.refs_2_ = bf16[32,3072]{1,0:T(8,128)(2,1)S(1)} collective-permute-done((bf16[32,3072]{1,0:T(8,128)(2,1)}, bf16[32,3072]{1,0:T(8,128)(2,1)S(1)}, u32[]{:S(2)}, u32[]{:S(2)}) %collective-permute-start.4) | collective-permute-done | bytes 196640 | tf_op jit(solution)/shard_map/ppermute | solution.py:196
  24.9 1.4 %collective-permute-done.5.refs_3_ = bf16[32,3072]{1,0:T(8,128)(2,1)S(1)} collective-permute-done((bf16[32,3072]{1,0:T(8,128)(2,1)S(1)}, bf16[32,3072]{1,0:T(8,128)(2,1)S(1)}, u32[]{:S(2)}, u32[]{:S(2)}) %collective-permute-start.5) | collective-permute-done | bytes 196640 | tf_op jit(solution)/shard_map/ppermute | solution.py:196
  26.3 0.9 %copy-done.1 = bf16[32,3072]{1,0:T(8,128)(2,1)S(1)} copy-done((bf16[32,3072]{1,0:T(8,128)(2,1)S(1)}, bf16[32,3072]{1,0:T(8,128)(2,1)}, u32[]{:S(2)}) %copy-start.1) | copy-done | bytes 196632
  27.3 25.4 %shard_map.106 = (bf16[64,3072]{1,0:T(8,128)(2,1)S(1)}, bf16[64,3072]{1,0:T(8,128)(2,1)S(1)}) custom-call(bf16[32,3072]{1,0:T(8,128)(2,1)S(1)} %copy-done.1, bf16[32,3072]{1,0:T(8,128)(2,1)S(1)} %collective-permute-done.3.refs_1_, bf16[32,3072]{1,0:T(8,128)(2,1)S(1)} %collective-permute-done.4.refs_2_, bf16[32,3072]{1,0:T(8,128)(2,1)S(1)} %collective-permute-done.5.refs_3_, ...), custom_call_target="tpu_custom_call" | custom-call | tf_op jit(solution)/shard_map/pallas_call | solution.py:231
  52.9 1.6 %collective-permute-done.6.refs_1_ = bf16[64,3072]{1,0:T(8,128)(2,1)S(1)} collective-permute-done((bf16[64,3072]{1,0:T(8,128)(2,1)S(1)}, bf16[64,3072]{1,0:T(8,128)(2,1)S(1)}, u32[]{:S(2)}, u32[]{:S(2)}) %collective-permute-start.6) | collective-permute-done | bytes 393248 | tf_op jit(solution)/shard_map/ppermute | solution.py:196
  54.6 1.6 %collective-permute-start.7 = (bf16[32,3072]{1,0:T(8,128)(2,1)S(1)}, bf16[32,3072]{1,0:T(8,128)(2,1)S(1)}, u32[]{:S(2)}, u32[]{:S(2)}) collective-permute-start(bf16[32,3072]{1,0:T(8,128)(2,1)S(1)} %add_convert_fusion), channel_id=1, source_target_pairs={{0,2},{1,3},{2,0},{3,1},{4,6},{5,7},{6,4},{7,5},{8,10},{9,11},{10,... | collective-permute-start | bytes 589832 | tf_op jit(solution)/shard_map/ppermute | solution.py:196
  56.1 5.4 %collective-permute-done.7.refs_2_ = bf16[32,3072]{1,0:T(8,128)(2,1)S(1)} collective-permute-done((bf16[32,3072]{1,0:T(8,128)(2,1)S(1)}, bf16[32,3072]{1,0:T(8,128)(2,1)S(1)}, u32[]{:S(2)}, u32[]{:S(2)}) %collective-permute-start.7) | collective-permute-done | bytes 196640 | tf_op jit(solution)/shard_map/ppermute | solution.py:196
  61.6 0.7 copy-done.3
  62.2 2.2 %shard_map.107 = (bf16[8,6144]{1,0:T(8,128)(2,1)}, bf16[8,6144]{1,0:T(8,128)(2,1)}, bf16[8,6144]{1,0:T(8,128)(2,1)}, bf16[8,6144]{1,0:T(8,128)(2,1)}) custom-call(bf16[64,3072]{1,0:T(8,128)(2,1)} %copy-done, bf16[64,3072]{1,0:T(8,128)(2,1)} %copy-done.2, bf16[32,3072]{1,0:T(8,128)(2,1)} %copy-done.3, f32[32,128]{1,0:T(8,128)} %get-tuple-element.23.refs_3_), custom_call_target="tpu_custom_call" | custom-call | tf_op jit(solution)/shard_map/pallas_call | solution.py:180
  64.4 1.6 %collective-permute-start.8 = (bf16[8,6144]{1,0:T(8,128)(2,1)}, bf16[8,6144]{1,0:T(8,128)(2,1)S(1)}, u32[]{:S(2)}, u32[]{:S(2)}) collective-permute-start(bf16[8,6144]{1,0:T(8,128)(2,1)} %get-tuple-element.25), channel_id=1, source_target_pairs={{0,4},{4,0},{8,12},{12,8},{1,5},{5,1},{9,13},{13,9},{2,6},{6,2},{1... | collective-permute-start | bytes 294920 | tf_op jit(solution)/shard_map/ppermute | solution.py:196
  66.0 1.5 %collective-permute-start.9 = (bf16[8,6144]{1,0:T(8,128)(2,1)}, bf16[8,6144]{1,0:T(8,128)(2,1)S(1)}, u32[]{:S(2)}, u32[]{:S(2)}) collective-permute-start(bf16[8,6144]{1,0:T(8,128)(2,1)} %get-tuple-element.26), channel_id=1, source_target_pairs={{0,8},{4,12},{8,0},{12,4},{1,9},{5,13},{9,1},{13,5},{2,10},{6,14},... | collective-permute-start | bytes 294920 | tf_op jit(solution)/shard_map/ppermute | solution.py:196
  67.5 1.3 %collective-permute-start.10 = (bf16[8,6144]{1,0:T(8,128)(2,1)}, bf16[8,6144]{1,0:T(8,128)(2,1)S(1)}, u32[]{:S(2)}, u32[]{:S(2)}) collective-permute-start(bf16[8,6144]{1,0:T(8,128)(2,1)} %get-tuple-element.27), channel_id=1, source_target_pairs={{0,12},{4,8},{8,4},{12,0},{1,13},{5,9},{9,5},{13,1},{2,14},{6,10},... | collective-permute-start | bytes 294920 | tf_op jit(solution)/shard_map/ppermute | solution.py:196
  68.8 1.4 %collective-permute-done.8.refs_1_ = bf16[8,6144]{1,0:T(8,128)(2,1)S(1)} collective-permute-done((bf16[8,6144]{1,0:T(8,128)(2,1)}, bf16[8,6144]{1,0:T(8,128)(2,1)S(1)}, u32[]{:S(2)}, u32[]{:S(2)}) %collective-permute-start.8) | collective-permute-done | bytes 98336 | tf_op jit(solution)/shard_map/ppermute | solution.py:196
  70.2 5.9 %collective-permute-done.9.refs_2_ = bf16[8,6144]{1,0:T(8,128)(2,1)S(1)} collective-permute-done((bf16[8,6144]{1,0:T(8,128)(2,1)}, bf16[8,6144]{1,0:T(8,128)(2,1)S(1)}, u32[]{:S(2)}, u32[]{:S(2)}) %collective-permute-start.9) | collective-permute-done | bytes 98336 | tf_op jit(solution)/shard_map/ppermute | solution.py:196
  76.1 0.6 copy-done.8
  76.8 2.2 %shard_map.108 = (bf16[6,3072]{1,0:T(8,128)(2,1)}, bf16[6,3072]{1,0:T(8,128)(2,1)}) custom-call(s32[2,6]{1,0:T(2,128)} %bitcast.10, bf16[6,3072]{1,0:T(8,128)(2,1)} %tok.3, bf16[6,3072]{1,0:T(8,128)(2,1)} %grad.3, f32[1,3072]{1,0:T(1,128)} %bitcast.8, bf16[4,3072]{1,0:T(4,128)(2,1)} %bitcast.6, f32[2,6,128]{2,1,0:T(8,128)} %get-tuple-element.15.gates, ...), custom_call_target="tpu_custom_call" | custom-call | tf_op jit(solution)/shard_map/pallas_call | solution.py:180
  (24 shorter events, 0.4 us)
Async XLA Ops:
  2.5 6.1 %collective-permute-start = (bf16[8,6272]{1,0:T(8,128)(2,1)}, bf16[8,6272]{1,0:T(8,128)(2,1)S(1)}, u32[]{:S(2)}, u32[]{:S(2)}) collective-permute-start(bf16[8,6272]{1,0:T(8,128)(2,1)} %get-tuple-element.17), channel_id=1, source_target_pairs={{0,4},{4,0},{8,12},{12,8},{1,5},{5,1},{9,13},{13,9},{2,6},{6,2},{1... | collective-permute-start | bytes 301064 | tf_op jit(solution)/shard_map/ppermute | solution.py:196
  5.5 10.8 %collective-permute-start.1 = (bf16[8,6272]{1,0:T(8,128)(2,1)}, bf16[8,6272]{1,0:T(8,128)(2,1)S(1)}, u32[]{:S(2)}, u32[]{:S(2)}) collective-permute-start(bf16[8,6272]{1,0:T(8,128)(2,1)} %get-tuple-element.18), channel_id=1, source_target_pairs={{0,8},{4,12},{8,0},{12,4},{1,9},{5,13},{9,1},{13,5},{2,10},{6,14},... | collective-permute-start | bytes 301064 | tf_op jit(solution)/shard_map/ppermute | solution.py:196
  8.1 8.2 %collective-permute-start.2 = (bf16[8,6272]{1,0:T(8,128)(2,1)}, bf16[8,6272]{1,0:T(8,128)(2,1)S(1)}, u32[]{:S(2)}, u32[]{:S(2)}) collective-permute-start(bf16[8,6272]{1,0:T(8,128)(2,1)} %get-tuple-element.19), channel_id=1, source_target_pairs={{0,12},{4,8},{8,4},{12,0},{1,13},{5,9},{9,5},{13,1},{2,14},{6,10},... | collective-permute-start | bytes 301064 | tf_op jit(solution)/shard_map/ppermute | solution.py:196
  8.6 7.7 %copy-start.4 = (bf16[8,6272]{1,0:T(8,128)(2,1)}, bf16[8,6272]{1,0:T(8,128)(2,1)S(1)}, u32[]{:S(2)}) copy-start(bf16[8,6272]{1,0:T(8,128)(2,1)S(1)} %collective-permute-done.refs_1_) | copy-start | bytes 301060
  16.3 0.6 copy-start.5
  16.3 0.7 copy-start.6
  19.0 5.9 %collective-permute-start.4 = (bf16[32,3072]{1,0:T(8,128)(2,1)}, bf16[32,3072]{1,0:T(8,128)(2,1)S(1)}, u32[]{:S(2)}, u32[]{:S(2)}) collective-permute-start(bf16[32,3072]{1,0:T(8,128)(2,1)} %get-tuple-element.20.refs_0_), channel_id=1, source_target_pairs={{0,2},{1,3},{2,0},{3,1},{4,6},{5,7},{6,4},{7,5},{8,10},{9,11},{10,... | collective-permute-start | bytes 589832 | tf_op jit(solution)/shard_map/ppermute | solution.py:196
  20.5 4.4 %collective-permute-start.3 = (bf16[32,3072]{1,0:T(8,128)(2,1)}, bf16[32,3072]{1,0:T(8,128)(2,1)S(1)}, u32[]{:S(2)}, u32[]{:S(2)}) collective-permute-start(bf16[32,3072]{1,0:T(8,128)(2,1)} %get-tuple-element.20.refs_0_), channel_id=1, source_target_pairs={{0,1},{1,0},{2,3},{3,2},{4,5},{5,4},{6,7},{7,6},{8,9},{9,8},{10,11... | collective-permute-start | bytes 589832 | tf_op jit(solution)/shard_map/ppermute | solution.py:196
  24.9 1.4 %collective-permute-start.5 = (bf16[32,3072]{1,0:T(8,128)(2,1)S(1)}, bf16[32,3072]{1,0:T(8,128)(2,1)S(1)}, u32[]{:S(2)}, u32[]{:S(2)}) collective-permute-start(bf16[32,3072]{1,0:T(8,128)(2,1)S(1)} %collective-permute-done.4.refs_2_), channel_id=1, source_target_pairs={{0,1},{1,0},{2,3},{3,2},{4,5},{5,4},{6,7},{7,6},{8,9},{9,8},{10,11... | collective-permute-start | bytes 589832 | tf_op jit(solution)/shard_map/ppermute | solution.py:196
  26.3 0.9 %copy-start.1 = (bf16[32,3072]{1,0:T(8,128)(2,1)S(1)}, bf16[32,3072]{1,0:T(8,128)(2,1)}, u32[]{:S(2)}) copy-start(bf16[32,3072]{1,0:T(8,128)(2,1)} %get-tuple-element.20.refs_0_) | copy-start | bytes 589828
  52.7 8.9 %copy-start = (bf16[64,3072]{1,0:T(8,128)(2,1)}, bf16[64,3072]{1,0:T(8,128)(2,1)S(1)}, u32[]{:S(2)}) copy-start(bf16[64,3072]{1,0:T(8,128)(2,1)S(1)} %get-tuple-element.21.refs_0_) | copy-start | bytes 1179652
  52.7 1.8 %collective-permute-start.6 = (bf16[64,3072]{1,0:T(8,128)(2,1)S(1)}, bf16[64,3072]{1,0:T(8,128)(2,1)S(1)}, u32[]{:S(2)}, u32[]{:S(2)}) collective-permute-start(bf16[64,3072]{1,0:T(8,128)(2,1)S(1)} %get-tuple-element.22), channel_id=1, source_target_pairs={{0,1},{1,0},{2,3},{3,2},{4,5},{5,4},{6,7},{7,6},{8,9},{9,8},{10,11... | collective-permute-start | bytes 1179656 | tf_op jit(solution)/shard_map/ppermute | solution.py:196
  54.5 7.1 %copy-start.2 = (bf16[64,3072]{1,0:T(8,128)(2,1)}, bf16[64,3072]{1,0:T(8,128)(2,1)S(1)}, u32[]{:S(2)}) copy-start(bf16[64,3072]{1,0:T(8,128)(2,1)S(1)} %collective-permute-done.6.refs_1_) | copy-start | bytes 1179652
  54.6 7.0 %collective-permute-start.7 = (bf16[32,3072]{1,0:T(8,128)(2,1)S(1)}, bf16[32,3072]{1,0:T(8,128)(2,1)S(1)}, u32[]{:S(2)}, u32[]{:S(2)}) collective-permute-start(bf16[32,3072]{1,0:T(8,128)(2,1)S(1)} %add_convert_fusion), channel_id=1, source_target_pairs={{0,2},{1,3},{2,0},{3,1},{4,6},{5,7},{6,4},{7,5},{8,10},{9,11},{10,... | collective-permute-start | bytes 589832 | tf_op jit(solution)/shard_map/ppermute | solution.py:196
  61.6 0.7 copy-start.3
  64.4 5.8 %collective-permute-start.8 = (bf16[8,6144]{1,0:T(8,128)(2,1)}, bf16[8,6144]{1,0:T(8,128)(2,1)S(1)}, u32[]{:S(2)}, u32[]{:S(2)}) collective-permute-start(bf16[8,6144]{1,0:T(8,128)(2,1)} %get-tuple-element.25), channel_id=1, source_target_pairs={{0,4},{4,0},{8,12},{12,8},{1,5},{5,1},{9,13},{13,9},{2,6},{6,2},{1... | collective-permute-start | bytes 294920 | tf_op jit(solution)/shard_map/ppermute | solution.py:196
  66.0 10.1 %collective-permute-start.9 = (bf16[8,6144]{1,0:T(8,128)(2,1)}, bf16[8,6144]{1,0:T(8,128)(2,1)S(1)}, u32[]{:S(2)}, u32[]{:S(2)}) collective-permute-start(bf16[8,6144]{1,0:T(8,128)(2,1)} %get-tuple-element.26), channel_id=1, source_target_pairs={{0,8},{4,12},{8,0},{12,4},{1,9},{5,13},{9,1},{13,5},{2,10},{6,14},... | collective-permute-start | bytes 294920 | tf_op jit(solution)/shard_map/ppermute | solution.py:196
  67.5 8.7 %collective-permute-start.10 = (bf16[8,6144]{1,0:T(8,128)(2,1)}, bf16[8,6144]{1,0:T(8,128)(2,1)S(1)}, u32[]{:S(2)}, u32[]{:S(2)}) collective-permute-start(bf16[8,6144]{1,0:T(8,128)(2,1)} %get-tuple-element.27), channel_id=1, source_target_pairs={{0,12},{4,8},{8,4},{12,0},{1,13},{5,9},{9,5},{13,1},{2,14},{6,10},... | collective-permute-start | bytes 294920 | tf_op jit(solution)/shard_map/ppermute | solution.py:196
  70.2 5.9 %copy-start.7 = (bf16[8,6144]{1,0:T(8,128)(2,1)}, bf16[8,6144]{1,0:T(8,128)(2,1)S(1)}, u32[]{:S(2)}) copy-start(bf16[8,6144]{1,0:T(8,128)(2,1)S(1)} %collective-permute-done.8.refs_1_) | copy-start | bytes 294916
  76.1 0.6 copy-start.8
  76.1 0.7 copy-start.9

commit v2 on v1

v2 whole, which is shorter than its diff:
```python
import functools

import jax
import jax.numpy as jnp
from jax import lax
from jax.experimental import pallas as pl
from jax.experimental.pallas import tpu as pltpu
from jax.sharding import PartitionSpec as P

GCAP = 15
SLOTS = 16
PAD = 8
LANES = 128
STEP = 512
SMALL = 4 * 2**20
FIELD = 32

root_two_pi = 0.7978845608028654
cubic_term = 0.044715

VM = pl.BlockSpec(memory_space=pltpu.VMEM)
SM = pl.BlockSpec(memory_space=pltpu.SMEM)
FAR = pl.BlockSpec(memory_space=pltpu.HBM)


def layout(rows, width):
    spare = PAD - rows
    pieces = -(-rows // spare)
    tail = 2 * width // (pieces + 1)
    return pieces, tail, 2 * width - tail


def gelu_both(v):
    t = jnp.tanh(root_two_pi * (v + cubic_term * v * v * v))
    value = 0.5 * v * (1.0 + t)
    slope = 0.5 * (1.0 + t) + 0.5 * v * (1.0 - t * t) * root_two_pi * (
        1.0 + 3.0 * cubic_term * v * v
    )
    return value, slope


def column(ref, choice, rows):
    row = lax.broadcasted_iota(jnp.int32, (rows, LANES), 0)
    out = jnp.zeros((rows, LANES), jnp.int32)
    for r in range(rows):
        out = jnp.where(row == r, ref[choice, r], out)
    return out


def pack_kernel(ids, slots, kept, tok, grad, gain, router, *outs):
    messages, gates_ref = outs[:-1], outs[-1]
    rows, width = tok.shape
    experts = router.shape[0]
    pieces, tail, head = layout(rows, width)
    me = lax.axis_index("expert")
    x = tok[...].astype(jnp.float32)
    g = grad[...].astype(jnp.float32)
    inverse = lax.rsqrt(jnp.mean(x * x, axis=1, keepdims=True) + 1e-06)
    normed = (x * inverse * gain[...]).astype(jnp.bfloat16)
    wide = normed.astype(jnp.float32)
    id0, id1 = column(ids, 0, rows), column(ids, 1, rows)
    pick0 = jnp.zeros((rows, LANES), jnp.float32)
    pick1 = jnp.zeros((rows, LANES), jnp.float32)
    for e in range(experts):
        logit = jnp.sum(wide * router[e : e + 1, :].astype(jnp.float32), axis=1, keepdims=True)
        pick0 = jnp.where(id0 == e, logit, pick0)
        pick1 = jnp.where(id1 == e, logit, pick1)
    gate0 = 1.0 / (1.0 + jnp.exp(pick1 - pick0))
    gate1 = 1.0 / (1.0 + jnp.exp(pick0 - pick1))
    gates_ref[...] = jnp.zeros_like(gates_ref)
    gates_ref[0:rows, :] = gate0
    gates_ref[PAD : PAD + rows, :] = gate1
    row = lax.broadcasted_iota(jnp.int32, (PAD, LANES), 0)
    field = lax.broadcasted_iota(jnp.int32, (PAD, LANES), 1) // FIELD
    for k, out in enumerate(messages):
        expert = me ^ k
        gate = jnp.where(id0 == expert, gate0, jnp.where(id1 == expert, gate1, 0.0))
        weighted = (gate[:, 0:1] * g).astype(jnp.bfloat16).astype(jnp.float32)
        low = []
        for first in range(0, rows, pieces):
            last = [weighted[r : r + 1, width - tail :] for r in range(first, min(first + pieces, rows))]
            last += [jnp.zeros((1, tail), jnp.float32)] * (pieces - len(last))
            low.append(jnp.concatenate(last, axis=1))
        high = jnp.concatenate([wide, weighted[:, : width - tail]], axis=1)
        out[:, :head] = jnp.concatenate([high] + low, axis=0).astype(jnp.bfloat16)
        table = jnp.full((PAD, LANES), -1, jnp.int32)
        for r in range(rows):
            hit0 = (ids[0, r] == expert) & (kept[0, r] == 1)
            hit1 = (ids[1, r] == expert) & (kept[1, r] == 1)
            slot = jnp.where(hit0, slots[0, r], jnp.where(hit1, slots[1, r], -1))
            here = (row == r) & (field == 0)
            there = (row == rows + r // pieces) & (field == 1 + r % pieces)
            table = jnp.where(here | there, slot, table)
        out[:, head:] = table.astype(jnp.float32).astype(jnp.bfloat16)


def bin_kernel(rows, width, done, *refs):
    del done
    messages, (bins, placed_ref) = refs[:-2], refs[-2:]
    pieces, tail, head = layout(rows, width)
    arrived = jnp.concatenate([m[...].astype(jnp.float32) for m in messages], axis=0)
    lane = lax.broadcasted_iota(jnp.int32, (arrived.shape[0], LANES), 1) % FIELD
    placed = jnp.where(arrived[:, head:] == lane.astype(jnp.float32), 1.0, 0.0)
    placed_ref[...] = placed
    onehot = placed.T.astype(jnp.bfloat16)
    packed = arrived[:, :head].astype(jnp.bfloat16)
    first = jnp.dot(onehot[:SLOTS], packed, preferred_element_type=jnp.float32)
    bins[0:SLOTS, :] = first[:, :width].astype(jnp.bfloat16)
    bins[SLOTS : 2 * SLOTS, : width - tail] = first[:, width:].astype(jnp.bfloat16)
    rest = 0.0
    for p in range(pieces):
        which = onehot[(p + 1) * FIELD : (p + 1) * FIELD + SLOTS]
        rest += jnp.dot(
            which, packed[:, p * tail : (p + 1) * tail], preferred_element_type=jnp.float32
        )
    bins[SLOTS : 2 * SLOTS, width - tail :] = rest.astype(jnp.bfloat16)


def load_kernel(start, after, weight, out, done, sem):
    copy = pltpu.make_async_copy(weight.at[0, :, pl.ds(start, out.shape[1])], out, sem)
    copy.start()
    done[...] = after[0:8, :]
    copy.wait()


def expert_kernel(groups, *refs):
    pairs = refs[: groups // 2]
    up_a, up_b, down_hbm, keep, send, x, g, active, back_hidden, slope, down, sems = refs[
        groups // 2 :
    ]
    rows = groups * SLOTS
    width, early = up_a.shape
    hidden = early + up_b.shape[1]
    block = width // sems.shape[0]
    over = (((1,), (1,)), ((), ()))

    def fetch(i):
        at = pl.ds(i * block, block)
        return pltpu.make_async_copy(down_hbm.at[0, at, :], down.at[at, :], sems.at[i])

    for i in range(sems.shape[0]):
        fetch(i).start()
    x[...] = jnp.zeros_like(x)
    g[...] = jnp.zeros_like(g)
    for j in range(groups):
        pair, at = pairs[j % (groups // 2)], j // (groups // 2) * 2 * SLOTS
        x[j * SLOTS : (j + 1) * SLOTS, :] = pair[at : at + SLOTS, :]
        g[j * SLOTS : (j + 1) * SLOTS, :] = pair[at + SLOTS : at + 2 * SLOTS, :]

    def deliver(total, at, side):
        part = total.T.astype(jnp.bfloat16)
        for j in range(groups):
            to = send if j % 2 else keep
            row = (j // 2) * 2 * SLOTS + side * SLOTS
            to[row : row + SLOTS, at] = part[j * SLOTS : (j + 1) * SLOTS]

    taken = lax.axis_index("expert") >= 0

    @pl.when(taken)
    def _():
        for f in range(0, hidden, STEP):
            part, c = (up_a, f) if f < early else (up_b, f - early)
            v = jnp.dot(x[...], part[:, c : c + STEP], preferred_element_type=jnp.float32)
            value, rise = gelu_both(v[:rows])
            active[:, f : f + STEP] = value.astype(jnp.bfloat16)
            slope[:, f : f + STEP] = rise

    for i in range(sems.shape[0]):

        @pl.when(taken)
        def _(i=i):
            fetch(i).wait()
            for d in range(i * block, (i + 1) * block, STEP):
                total = lax.dot_general(
                    down[d : d + STEP, :], active[...], over, preferred_element_type=jnp.float32
                )
                deliver(total, slice(d, d + STEP), 0)

    for f in range(0, hidden, STEP):
        v = jnp.dot(g[...], down[:, f : f + STEP], preferred_element_type=jnp.float32)[:rows]
        back_hidden[:, f : f + STEP] = (v * slope[:, f : f + STEP]).astype(jnp.bfloat16)
    for d in range(0, width, STEP):
        total = lax.dot_general(
            up_a[d : d + STEP, :],
            back_hidden[:, :early],
            over,
            preferred_element_type=jnp.float32,
        )
        total += lax.dot_general(
            up_b[d : d + STEP, :],
            back_hidden[:, early:],
            over,
            preferred_element_type=jnp.float32,
        )
        deliver(total, slice(d, d + STEP), 1)


def join_kernel(done, a, b, out):
    del done
    out[0 : 2 * SLOTS, :] = a[...]
    out[2 * SLOTS :, :] = b[...]


def add_kernel(a, b, out):
    total = a[...].astype(jnp.float32) + b[...].astype(jnp.float32)
    out[...] = total.astype(jnp.bfloat16)


def reply_kernel(rows, n_parts, *refs):
    parts, placed, replies = refs[:n_parts], refs[n_parts], refs[n_parts + 1 :]
    width = parts[0].shape[1]
    pieces, tail, head = layout(rows, width)
    total = parts[0][0 : 2 * SLOTS, :].astype(jnp.float32)
    for p in parts[1:]:
        total = total + p[0 : 2 * SLOTS, :].astype(jnp.float32)
    total = total.astype(jnp.bfloat16)
    both = jnp.concatenate([total[:SLOTS], total[SLOTS:]], axis=1)
    onehot = placed[...].astype(jnp.bfloat16)
    for p in range(pieces):
        at = slice(p * tail, (p + 1) * tail)
        which = onehot[:, (p + 1) * FIELD : (p + 1) * FIELD + SLOTS]
        spread = jnp.dot(onehot[:, :SLOTS], both[:, at], preferred_element_type=jnp.float32)
        spread += jnp.dot(which, both[:, head:], preferred_element_type=jnp.float32)
        for k, out in enumerate(replies):
            out[:, at] = spread[k * PAD : (k + 1) * PAD].astype(jnp.bfloat16)


def finish_kernel(ids, tok, grad, gain, router, gates, *refs):
    replies, (mixed, grad_tokens) = refs[:-2], refs[-2:]
    rows, width = tok.shape
    experts = router.shape[0]
    pieces, tail, head = layout(rows, width)
    me = lax.axis_index("expert")
    x = tok[...].astype(jnp.float32)
    g = grad[...].astype(jnp.float32)
    inverse = lax.rsqrt(jnp.mean(x * x, axis=1, keepdims=True) + 1e-06)
    id0, id1 = column(ids, 0, rows)[:, 0:1], column(ids, 1, rows)[:, 0:1]
    gate0, gate1 = gates[0:rows, 0:1], gates[PAD : PAD + rows, 0:1]
    chosen0 = jnp.zeros((rows, width), jnp.float32)
    chosen1 = jnp.zeros((rows, width), jnp.float32)
    back = jnp.zeros((PAD, head), jnp.float32)
    for k, reply in enumerate(replies):
        expert = me ^ k
        answer = reply[...].astype(jnp.float32)
        chosen0 = jnp.where(id0 == expert, answer[:rows, :width], chosen0)
        chosen1 = jnp.where(id1 == expert, answer[:rows, :width], chosen1)
        back = back + answer
    rest = []
    for r in range(rows):
        p = r % pieces
        rest.append(back[rows + r // pieces : rows + r // pieces + 1, p * tail : (p + 1) * tail])
    back = jnp.concatenate([back[:rows, width:], jnp.concatenate(rest, axis=0)], axis=1)
    mixed[...] = (gate0 * chosen0 + gate1 * chosen1).astype(jnp.bfloat16)
    grad0 = jnp.sum(g * chosen0, axis=1, keepdims=True)
    grad1 = jnp.sum(g * chosen1, axis=1, keepdims=True)
    spread = gate0 * gate1 * (grad0 - grad1)
    for e in range(experts):
        line = router[e : e + 1, :].astype(jnp.float32)
        weight = jnp.where(id0 == e, spread, 0.0) - jnp.where(id1 == e, spread, 0.0)
        back = back + weight * line
    upstream = back * gain[...]
    mean = jnp.mean(upstream * x, axis=1, keepdims=True)
    grad_tokens[...] = (inverse * (upstream - x * inverse * inverse * mean)).astype(jnp.bfloat16)


def near(array):
    return pltpu.with_memory_space_constraint(array, pltpu.VMEM)


def far(array):
    return pltpu.with_memory_space_constraint(array, pltpu.HBM)


def call(body, out_shape, in_specs, args, limit=SMALL):
    return pl.pallas_call(
        body,
        out_shape=out_shape,
        in_specs=in_specs,
        out_specs=[VM] * len(out_shape),
        compiler_params=pltpu.CompilerParams(vmem_limit_bytes=limit),
    )(*args)


def shards(
    tokens, norm_gain, router, up_weight, down_weight, expert_ids, bin_slots, kept_mask, grad_out
):
    rows, width = tokens.shape
    hidden = up_weight.shape[2]
    experts = lax.axis_size("expert")
    groups = lax.axis_size("tensor")
    bf16, f32 = jnp.bfloat16, jnp.float32
    pieces, tail, head = layout(rows, width)

    def swap(array, axis, mask):
        n = lax.axis_size(axis)
        return lax.ppermute(array, axis, [(i, i ^ mask) for i in range(n)])

    ids, slots, kept = expert_ids.T, bin_slots.T, kept_mask.T
    gain, lines = norm_gain.reshape(1, width), router.T

    *messages, gates = call(
        pack_kernel,
        [pltpu.VMEM((PAD, head + LANES), bf16)] * experts
        + [pltpu.VMEM((2 * PAD, LANES), f32)],
        [SM] * 3 + [VM] * 4,
        (ids, slots, kept, tokens, grad_out, gain, lines),
        limit=None,
    )
    arrived = [messages[0]] + [swap(messages[k], "expert", k) for k in range(1, experts)]

    def load(start, stop, after):
        return pl.pallas_call(
            functools.partial(load_kernel, start),
            out_shape=[pltpu.VMEM((width, stop - start), bf16), pltpu.VMEM((8, LANES), f32)],
            in_specs=[VM, FAR],
            out_specs=[VM, VM],
            scratch_shapes=[pltpu.SemaphoreType.DMA],
            compiler_params=pltpu.CompilerParams(vmem_limit_bytes=2**20),
            cost_estimate=pl.CostEstimate(
                flops=0, bytes_accessed=width * (stop - start) * 4, transcendentals=0
            ),
        )(after, far(up_weight))

    early = max(STEP, hidden * 5 // 8 // STEP * STEP)
    up_a, done = load(0, early, near(gates))

    own, placed = call(
        functools.partial(bin_kernel, rows, width),
        [pltpu.VMEM((2 * SLOTS, width), bf16), pltpu.VMEM((experts * PAD, LANES), f32)],
        [VM] * (1 + experts),
        [near(a) for a in (done, *arrived)],
    )
    up_b, done = load(early, hidden, near(placed))

    mask = groups // 2
    pair = call(
        join_kernel,
        [pltpu.VMEM((4 * SLOTS, width), bf16)],
        [VM] * 3,
        [near(a) for a in (done, own, swap(own, "tensor", mask))],
    )[0]
    bins = {0: pair}
    mask //= 2
    while mask:
        bins.update({j | mask: swap(b, "tensor", mask) for j, b in bins.items()})
        mask //= 2

    tall = max(groups * SLOTS, 128)
    short = groups * SLOTS
    keep, send = pl.pallas_call(
        functools.partial(expert_kernel, groups),
        out_shape=[pltpu.VMEM((short, width), bf16)] * 2,
        in_specs=[VM] * (groups // 2 + 2) + [FAR],
        out_specs=[VM] * 2,
        scratch_shapes=[
            pltpu.VMEM((tall, width), bf16),
            pltpu.VMEM((tall, width), bf16),
            pltpu.VMEM((short, hidden), bf16),
            pltpu.VMEM((short, hidden), bf16),
            pltpu.VMEM((short, hidden), f32),
            pltpu.VMEM((width, hidden), bf16),
            pltpu.SemaphoreType.DMA((3,)),
        ],
        compiler_params=pltpu.CompilerParams(vmem_limit_bytes=32 * 2**20),
    )(*[near(bins[j]) for j in range(groups // 2)], near(up_a), near(up_b), far(down_weight))

    got = swap(send, "tensor", 1)
    piece = pltpu.VMEM((2 * SLOTS, width), bf16)
    firsts, sums = [keep, got], {}
    for i in range(1, groups // 2):
        at = slice(2 * SLOTS * i, 2 * SLOTS * (i + 1))
        sums[2 * i] = (keep[at].astype(f32) + got[at].astype(f32)).astype(bf16)
    mask = 2
    while mask < groups:
        came = {j ^ mask: swap(a, "tensor", mask) for j, a in sums.items() if j & mask}
        sums = {j: a for j, a in sums.items() if not j & mask}
        for j, a in came.items():
            if j == 0:
                firsts.append(a)
            else:
                sums[j] = call(add_kernel, [piece], [VM] * 2, (near(sums[j]), near(a)))[0]
        mask *= 2

    replies = call(
        functools.partial(reply_kernel, rows, len(firsts)),
        [pltpu.VMEM((PAD, head), bf16)] * experts,
        [VM] * (len(firsts) + 1),
        [near(a) for a in (*firsts, placed)],
    )
    answers = [replies[0]] + [swap(replies[k], "expert", k) for k in range(1, experts)]

    result = jax.ShapeDtypeStruct((rows, width), bf16)
    mixed, grad_tokens = call(
        finish_kernel,
        [result, result],
        [SM] + [VM] * (5 + experts),
        (ids, tokens, grad_out, gain, lines, near(gates), *[near(a) for a in answers]),
    )
    return mixed, grad_tokens


def solution(mesh):
    split = P(("dp", "expert", "tensor"), None)
    weights = P("expert", None, "tensor")
    return jax.shard_map(
        shards,
        mesh=mesh,
        in_specs=(split, P(), P(), weights, weights, split, split, split, split),
        out_specs=(split, split),
        check_vma=False,
    )
```

time: 79.3 us -> 64.6 us (0.81)
  waiting for transfers between devices: 28.3 us -> 15.6 us
  local copies, waits for them, and re-layouts: 2.98 us -> 0.02 us
    ppermute x11 -> x10, waiting for transfers between devices: 28.3 us -> 15.6 us  [swap(): return lax.ppermute(array, axis, [(i, i ^ mask) for i in range(n)])]
    unnamed x20 -> x10, local copies, waits for them, and re-layouts: 2.98 us -> 0.02 us
    pallas_call x5 -> x8, Pallas kernels: 33.7 us -> 34.4 us  [the longest x1 21.7 us: shards(): pl.pallas_call(functools.partial(expert_kernel, groups), out_shape=[pltpu...]
    ppermute x11 -> x10, starting transfers between devices: 13.3 us -> 13.6 us  [swap(): return lax.ppermute(array, axis, [(i, i ^ mask) for i in range(n)])]
  transfers between devices with their start and end apart: 11 -> 10, of which waited for: 8 -> 8; matrix products, arithmetic and copies ran while one was open for 0% -> 0% of each run, Pallas kernels for 0% -> 14%
where the time goes in v2:
time: 64.6 us; the launch traced here: 64.3 us
  Pallas kernels  34.4 us (53%)
  waiting for transfers between devices  15.6 us (24%)
  starting transfers between devices  13.6 us (21%)
  between operations  0.74 us (1%)
    pallas_call x1, Pallas kernels, shards(): pl.pallas_call(functools.partial(expert_kernel, groups), out_shape=[pltpu...  21.7 us
    ppermute x10, waiting for transfers between devices, swap(): return lax.ppermute(array, axis, [(i, i ^ mask) for i in range(n)])  15.6 us
    ppermute x10, starting transfers between devices, swap(): return lax.ppermute(array, axis, [(i, i ^ mask) for i in range(n)])  13.6 us
    pallas_call x2, Pallas kernels, load(): pl.pallas_call(functools.partial(load_kernel, start), out_shape=[pltpu.VM...  9.17 us
    pallas_call x5, Pallas kernels, call(): pl.pallas_call(body, out_shape=out_shape, in_specs=in_specs, out_specs=[V...  3.51 us
  transfers between devices with their start and end apart: 10, of which 8 were waited for; matrix products, arithmetic and copies ran while one was open for 0% of the time, Pallas kernels for 14%

profile of v2, /device:TPU:0, one launch (start us, length us, event | category | flops | bytes accessed | tf_op | source)
XLA Modules:
  0.0 64.3 jit_solution(11958216411798028432)
XLA Ops:
  0.6 1.3 %shard_map.104 = (bf16[8,4736]{1,0:T(8,128)(2,1)S(1)}, bf16[8,4736]{1,0:T(8,128)(2,1)S(1)}, bf16[8,4736]{1,0:T(8,128)(2,1)S(1)}, bf16[8,4736]{1,0:T(8,128)(2,1)S(1)}, f32[16,128]{1,0:T(8,128)S(1)}) custom-call(s32[2,6]{1,0:T(2,128)} %bitcast.9, s32[2,6]{1,0:T(2,128)} %bitcast.11, s32[2,6]{1,0:T(2,128)} %bitcast.12, bf16[6,3072]{1,0:T(8,128)(2,1)} %tok.3, ...), custom_call_target="tpu_custom_call" | custom-call | tf_op jit(solution)/shard_map/pallas_call | solution.py:275
  1.9 3.1 %collective-permute-start = (bf16[8,4736]{1,0:T(8,128)(2,1)S(1)}, bf16[8,4736]{1,0:T(8,128)(2,1)S(1)}, u32[]{:S(2)}, u32[]{:S(2)}) collective-permute-start(bf16[8,4736]{1,0:T(8,128)(2,1)S(1)} %get-tuple-element.22), channel_id=1, source_target_pairs={{0,4},{4,0},{8,12},{12,8},{1,5},{5,1},{9,13},{13,9},{2,6},{6,2},{1... | collective-permute-start | bytes 227336 | tf_op jit(solution)/shard_map/ppermute | solution.py:296
  5.0 2.6 %collective-permute-start.1 = (bf16[8,4736]{1,0:T(8,128)(2,1)S(1)}, bf16[8,4736]{1,0:T(8,128)(2,1)S(1)}, u32[]{:S(2)}, u32[]{:S(2)}) collective-permute-start(bf16[8,4736]{1,0:T(8,128)(2,1)S(1)} %get-tuple-element.23), channel_id=1, source_target_pairs={{0,8},{4,12},{8,0},{12,4},{1,9},{5,13},{9,1},{13,5},{2,10},{6,14},... | collective-permute-start | bytes 227336 | tf_op jit(solution)/shard_map/ppermute | solution.py:296
  7.6 5.5 %shard_map.105 = (bf16[3072,2560]{1,0:T(8,128)(2,1)S(1)}, f32[8,128]{1,0:T(8,128)S(1)}) custom-call(f32[16,128]{1,0:T(8,128)S(1)} %get-tuple-element.19.after.gates, bf16[1,3072,4096]{2,1,0:T(8,128)(2,1)} %weight.3), custom_call_target="tpu_custom_call" | custom-call | bytes 31457280 | tf_op jit(solution)/shard_map/pallas_call | solution.py:312
  13.1 0.8 %collective-permute-done.2.refs_3_ = bf16[8,4736]{1,0:T(8,128)(2,1)S(1)} collective-permute-done((bf16[8,4736]{1,0:T(8,128)(2,1)S(1)}, bf16[8,4736]{1,0:T(8,128)(2,1)S(1)}, u32[]{:S(2)}, u32[]{:S(2)}) %collective-permute-start.2) | collective-permute-done | bytes 75808 | tf_op jit(solution)/shard_map/ppermute | solution.py:296
  13.9 0.3 shard_map.106
  14.1 1.6 %collective-permute-start.3 = (bf16[32,3072]{1,0:T(8,128)(2,1)S(1)}, bf16[32,3072]{1,0:T(8,128)(2,1)S(1)}, u32[]{:S(2)}, u32[]{:S(2)}) collective-permute-start(bf16[32,3072]{1,0:T(8,128)(2,1)S(1)} %get-tuple-element.27.a), channel_id=1, source_target_pairs={{0,2},{1,3},{2,0},{3,1},{4,6},{5,7},{6,4},{7,5},{8,10},{9,11},{10,... | collective-permute-start | bytes 589832 | tf_op jit(solution)/shard_map/ppermute | solution.py:296
  15.7 3.7 %shard_map.107 = (bf16[3072,1536]{1,0:T(8,128)(2,1)S(1)}, f32[8,128]{1,0:T(8,128)S(1)}) custom-call(f32[32,128]{1,0:T(8,128)S(1)} %get-tuple-element.25.after.refs_3_, bf16[1,3072,4096]{2,1,0:T(8,128)(2,1)} %weight.3), custom_call_target="tpu_custom_call" | custom-call | bytes 18874368 | tf_op jit(solution)/shard_map/pallas_call | solution.py:312
  19.4 0.5 collective-permute-done.3.b
  19.9 0.1 collective-permute-start.4
  20.0 1.7 %collective-permute-done.4.refs_1_ = bf16[64,3072]{1,0:T(8,128)(2,1)S(1)} collective-permute-done((bf16[64,3072]{1,0:T(8,128)(2,1)S(1)}, bf16[64,3072]{1,0:T(8,128)(2,1)S(1)}, u32[]{:S(2)}, u32[]{:S(2)}) %collective-permute-start.4) | collective-permute-done | bytes 393248 | tf_op jit(solution)/shard_map/ppermute | solution.py:296
  21.7 21.7 %shard_map.109 = (bf16[64,3072]{1,0:T(8,128)(2,1)S(1)}, bf16[64,3072]{1,0:T(8,128)(2,1)S(1)}) custom-call(bf16[64,3072]{1,0:T(8,128)(2,1)S(1)} %shard_map.108.refs_0_, bf16[64,3072]{1,0:T(8,128)(2,1)S(1)} %collective-permute-done.4.refs_1_, bf16[3072,2560]{1,0:T(8,128)(2,1)S(1)} %get-tuple-element.28.refs_2_, ...), custom_call_target="tpu_custom_call" | custom-call | tf_op jit(solution)/shard_map/pallas_call | solution.py:350
  43.4 0.2 collective-permute-start.5
  43.6 1.6 %collective-permute-done.5.refs_1_ = bf16[64,3072]{1,0:T(8,128)(2,1)S(1)} collective-permute-done((bf16[64,3072]{1,0:T(8,128)(2,1)S(1)}, bf16[64,3072]{1,0:T(8,128)(2,1)S(1)}, u32[]{:S(2)}, u32[]{:S(2)}) %collective-permute-start.5) | collective-permute-done | bytes 393248 | tf_op jit(solution)/shard_map/ppermute | solution.py:296
  45.2 1.6 %collective-permute-start.6 = (bf16[32,3072]{1,0:T(8,128)(2,1)S(1)}, bf16[32,3072]{1,0:T(8,128)(2,1)S(1)}, u32[]{:S(2)}, u32[]{:S(2)}) collective-permute-start(bf16[32,3072]{1,0:T(8,128)(2,1)S(1)} %add_convert_fusion), channel_id=1, source_target_pairs={{0,2},{1,3},{2,0},{3,1},{4,6},{5,7},{6,4},{7,5},{8,10},{9,11},{10,... | collective-permute-start | bytes 589832 | tf_op jit(solution)/shard_map/ppermute | solution.py:296
  46.8 5.4 %collective-permute-done.6.refs_2_ = bf16[32,3072]{1,0:T(8,128)(2,1)S(1)} collective-permute-done((bf16[32,3072]{1,0:T(8,128)(2,1)S(1)}, bf16[32,3072]{1,0:T(8,128)(2,1)S(1)}, u32[]{:S(2)}, u32[]{:S(2)}) %collective-permute-start.6) | collective-permute-done | bytes 196640 | tf_op jit(solution)/shard_map/ppermute | solution.py:296
  52.3 0.4 shard_map.110
  52.6 1.3 %collective-permute-start.7 = (bf16[8,4608]{1,0:T(8,128)(2,1)S(1)}, bf16[8,4608]{1,0:T(8,128)(2,1)S(1)}, u32[]{:S(2)}, u32[]{:S(2)}) collective-permute-start(bf16[8,4608]{1,0:T(8,128)(2,1)S(1)} %get-tuple-element.33), channel_id=1, source_target_pairs={{0,4},{4,0},{8,12},{12,8},{1,5},{5,1},{9,13},{13,9},{2,6},{6,2},{1... | collective-permute-start | bytes 221192 | tf_op jit(solution)/shard_map/ppermute | solution.py:296
  53.9 2.6 %collective-permute-start.8 = (bf16[8,4608]{1,0:T(8,128)(2,1)S(1)}, bf16[8,4608]{1,0:T(8,128)(2,1)S(1)}, u32[]{:S(2)}, u32[]{:S(2)}) collective-permute-start(bf16[8,4608]{1,0:T(8,128)(2,1)S(1)} %get-tuple-element.34), channel_id=1, source_target_pairs={{0,8},{4,12},{8,0},{12,4},{1,9},{5,13},{9,1},{13,5},{2,10},{6,14},... | collective-permute-start | bytes 221192 | tf_op jit(solution)/shard_map/ppermute | solution.py:296
  56.5 0.6 collective-permute-start.9
  57.1 0.7 %collective-permute-done.7.refs_1_ = bf16[8,4608]{1,0:T(8,128)(2,1)S(1)} collective-permute-done((bf16[8,4608]{1,0:T(8,128)(2,1)S(1)}, bf16[8,4608]{1,0:T(8,128)(2,1)S(1)}, u32[]{:S(2)}, u32[]{:S(2)}) %collective-permute-start.7) | collective-permute-done | bytes 73760 | tf_op jit(solution)/shard_map/ppermute | solution.py:296
  57.8 3.4 %collective-permute-done.8.refs_2_ = bf16[8,4608]{1,0:T(8,128)(2,1)S(1)} collective-permute-done((bf16[8,4608]{1,0:T(8,128)(2,1)S(1)}, bf16[8,4608]{1,0:T(8,128)(2,1)S(1)}, u32[]{:S(2)}, u32[]{:S(2)}) %collective-permute-start.8) | collective-permute-done | bytes 73760 | tf_op jit(solution)/shard_map/ppermute | solution.py:296
  61.1 1.6 %collective-permute-done.9.refs_3_ = bf16[8,4608]{1,0:T(8,128)(2,1)S(1)} collective-permute-done((bf16[8,4608]{1,0:T(8,128)(2,1)S(1)}, bf16[8,4608]{1,0:T(8,128)(2,1)S(1)}, u32[]{:S(2)}, u32[]{:S(2)}) %collective-permute-start.9) | collective-permute-done | bytes 73760 | tf_op jit(solution)/shard_map/ppermute | solution.py:296
  62.8 1.6 %shard_map.111 = (bf16[6,3072]{1,0:T(8,128)(2,1)}, bf16[6,3072]{1,0:T(8,128)(2,1)}) custom-call(s32[2,6]{1,0:T(2,128)S(1)} %bitcast.10, bf16[6,3072]{1,0:T(8,128)(2,1)S(1)} %copy-done, bf16[6,3072]{1,0:T(8,128)(2,1)S(1)} %copy-done.1, f32[1,3072]{1,0:T(1,128)S(1)} %bitcast.8, bf16[4,3072]{1,0:T(4,128)(2,1)S(1)} %bitcast.6, ...), custom_call_target="tpu_custom_call" | custom-call | tf_op jit(solution)/shard_map/pallas_call | solution.py:275
  (15 shorter events, 0.1 us)
Async XLA Ops:
  1.9 11.2 %collective-permute-start = (bf16[8,4736]{1,0:T(8,128)(2,1)S(1)}, bf16[8,4736]{1,0:T(8,128)(2,1)S(1)}, u32[]{:S(2)}, u32[]{:S(2)}) collective-permute-start(bf16[8,4736]{1,0:T(8,128)(2,1)S(1)} %get-tuple-element.22), channel_id=1, source_target_pairs={{0,4},{4,0},{8,12},{12,8},{1,5},{5,1},{9,13},{13,9},{2,6},{6,2},{1... | collective-permute-start | bytes 227336 | tf_op jit(solution)/shard_map/ppermute | solution.py:296
  5.0 8.1 %collective-permute-start.1 = (bf16[8,4736]{1,0:T(8,128)(2,1)S(1)}, bf16[8,4736]{1,0:T(8,128)(2,1)S(1)}, u32[]{:S(2)}, u32[]{:S(2)}) collective-permute-start(bf16[8,4736]{1,0:T(8,128)(2,1)S(1)} %get-tuple-element.23), channel_id=1, source_target_pairs={{0,8},{4,12},{8,0},{12,4},{1,9},{5,13},{9,1},{13,5},{2,10},{6,14},... | collective-permute-start | bytes 227336 | tf_op jit(solution)/shard_map/ppermute | solution.py:296
  7.6 6.3 %collective-permute-start.2 = (bf16[8,4736]{1,0:T(8,128)(2,1)S(1)}, bf16[8,4736]{1,0:T(8,128)(2,1)S(1)}, u32[]{:S(2)}, u32[]{:S(2)}) collective-permute-start(bf16[8,4736]{1,0:T(8,128)(2,1)S(1)} %get-tuple-element.24), channel_id=1, source_target_pairs={{0,12},{4,8},{8,4},{12,0},{1,13},{5,9},{9,5},{13,1},{2,14},{6,10},... | collective-permute-start | bytes 227336 | tf_op jit(solution)/shard_map/ppermute | solution.py:296
  14.1 5.7 %collective-permute-start.3 = (bf16[32,3072]{1,0:T(8,128)(2,1)S(1)}, bf16[32,3072]{1,0:T(8,128)(2,1)S(1)}, u32[]{:S(2)}, u32[]{:S(2)}) collective-permute-start(bf16[32,3072]{1,0:T(8,128)(2,1)S(1)} %get-tuple-element.27.a), channel_id=1, source_target_pairs={{0,2},{1,3},{2,0},{3,1},{4,6},{5,7},{6,4},{7,5},{8,10},{9,11},{10,... | collective-permute-start | bytes 589832 | tf_op jit(solution)/shard_map/ppermute | solution.py:296
  19.9 1.8 %collective-permute-start.4 = (bf16[64,3072]{1,0:T(8,128)(2,1)S(1)}, bf16[64,3072]{1,0:T(8,128)(2,1)S(1)}, u32[]{:S(2)}, u32[]{:S(2)}) collective-permute-start(bf16[64,3072]{1,0:T(8,128)(2,1)S(1)} %shard_map.108.refs_0_), channel_id=1, source_target_pairs={{0,1},{1,0},{2,3},{3,2},{4,5},{5,4},{6,7},{7,6},{8,9},{9,8},{10,11... | collective-permute-start | bytes 1179656 | tf_op jit(solution)/shard_map/ppermute | solution.py:296
  21.7 41.0 %copy-start = (bf16[6,3072]{1,0:T(8,128)(2,1)S(1)}, bf16[6,3072]{1,0:T(8,128)(2,1)}, u32[]{:S(2)}) copy-start(bf16[6,3072]{1,0:T(8,128)(2,1)} %tok.3) | copy-start | bytes 110596
  21.7 41.0 %copy-start.1 = (bf16[6,3072]{1,0:T(8,128)(2,1)S(1)}, bf16[6,3072]{1,0:T(8,128)(2,1)}, u32[]{:S(2)}) copy-start(bf16[6,3072]{1,0:T(8,128)(2,1)} %grad.3) | copy-start | bytes 110596
  21.7 41.0 %copy-start.2 = (bf16[3072,4]{0,1:T(4,128)(2,1)S(1)}, bf16[3072,4]{0,1:T(4,128)(2,1)}, u32[]{:S(2)}) copy-start(bf16[3072,4]{0,1:T(4,128)(2,1)} %param.11) | copy-start | bytes 73732
  21.7 41.0 %copy-start.3 = (f32[3072]{0:T(1024)S(1)}, f32[3072]{0:T(1024)}, u32[]{:S(2)}) copy-start(f32[3072]{0:T(1024)} %param.10) | copy-start | bytes 36868
  21.7 41.0 %copy-start.4 = (s32[6,2]{0,1:T(2,128)S(1)}, s32[6,2]{0,1:T(2,128)}, u32[]{:S(2)}) copy-start(s32[6,2]{0,1:T(2,128)} %param.14) | copy-start | bytes 148
  43.4 1.8 %collective-permute-start.5 = (bf16[64,3072]{1,0:T(8,128)(2,1)S(1)}, bf16[64,3072]{1,0:T(8,128)(2,1)S(1)}, u32[]{:S(2)}, u32[]{:S(2)}) collective-permute-start(bf16[64,3072]{1,0:T(8,128)(2,1)S(1)} %get-tuple-element.31), channel_id=1, source_target_pairs={{0,1},{1,0},{2,3},{3,2},{4,5},{5,4},{6,7},{7,6},{8,9},{9,8},{10,11... | collective-permute-start | bytes 1179656 | tf_op jit(solution)/shard_map/ppermute | solution.py:296
  45.2 7.0 %collective-permute-start.6 = (bf16[32,3072]{1,0:T(8,128)(2,1)S(1)}, bf16[32,3072]{1,0:T(8,128)(2,1)S(1)}, u32[]{:S(2)}, u32[]{:S(2)}) collective-permute-start(bf16[32,3072]{1,0:T(8,128)(2,1)S(1)} %add_convert_fusion), channel_id=1, source_target_pairs={{0,2},{1,3},{2,0},{3,1},{4,6},{5,7},{6,4},{7,5},{8,10},{9,11},{10,... | collective-permute-start | bytes 589832 | tf_op jit(solution)/shard_map/ppermute | solution.py:296
  52.6 5.2 %collective-permute-start.7 = (bf16[8,4608]{1,0:T(8,128)(2,1)S(1)}, bf16[8,4608]{1,0:T(8,128)(2,1)S(1)}, u32[]{:S(2)}, u32[]{:S(2)}) collective-permute-start(bf16[8,4608]{1,0:T(8,128)(2,1)S(1)} %get-tuple-element.33), channel_id=1, source_target_pairs={{0,4},{4,0},{8,12},{12,8},{1,5},{5,1},{9,13},{13,9},{2,6},{6,2},{1... | collective-permute-start | bytes 221192 | tf_op jit(solution)/shard_map/ppermute | solution.py:296
  53.9 7.3 %collective-permute-start.8 = (bf16[8,4608]{1,0:T(8,128)(2,1)S(1)}, bf16[8,4608]{1,0:T(8,128)(2,1)S(1)}, u32[]{:S(2)}, u32[]{:S(2)}) collective-permute-start(bf16[8,4608]{1,0:T(8,128)(2,1)S(1)} %get-tuple-element.34), channel_id=1, source_target_pairs={{0,8},{4,12},{8,0},{12,4},{1,9},{5,13},{9,1},{13,5},{2,10},{6,14},... | collective-permute-start | bytes 221192 | tf_op jit(solution)/shard_map/ppermute | solution.py:296
  56.5 6.3 %collective-permute-start.9 = (bf16[8,4608]{1,0:T(8,128)(2,1)S(1)}, bf16[8,4608]{1,0:T(8,128)(2,1)S(1)}, u32[]{:S(2)}, u32[]{:S(2)}) collective-permute-start(bf16[8,4608]{1,0:T(8,128)(2,1)S(1)} %get-tuple-element.35), channel_id=1, source_target_pairs={{0,12},{4,8},{8,4},{12,0},{1,13},{5,9},{9,5},{13,1},{2,14},{6,10},... | collective-permute-start | bytes 221192 | tf_op jit(solution)/shard_map/ppermute | solution.py:296

commit v3 on v2

--- a/solution.py
+++ b/solution.py
@@ -125,9 +125,9 @@
 
 def expert_kernel(groups, *refs):
     pairs = refs[: groups // 2]
-    up_a, up_b, down_hbm, keep, send, x, g, active, back_hidden, slope, down, sems = refs[
-        groups // 2 :
-    ]
+    (up_a_in, up_b_in, down_hbm, keep, send, up_a, up_b) = refs[groups // 2 : groups // 2 + 7]
+    x, g, active, back_hidden, slope, down, sems = refs[groups // 2 + 7 :]
+    del up_a_in, up_b_in
     rows = groups * SLOTS
     width, early = up_a.shape
     hidden = early + up_b.shape[1]
@@ -138,17 +138,20 @@
         at = pl.ds(i * block, block)
         return pltpu.make_async_copy(down_hbm.at[0, at, :], down.at[at, :], sems.at[i])
 
+    def columns(f):
+        return (up_a, f) if f < early else (up_b, f - early)
+
     for i in range(sems.shape[0]):
         fetch(i).start()
     x[...] = jnp.zeros_like(x)
     g[...] = jnp.zeros_like(g)
+    back_hidden[...] = jnp.zeros_like(back_hidden)
     for j in range(groups):
         pair, at = pairs[j % (groups // 2)], j // (groups // 2) * 2 * SLOTS
         x[j * SLOTS : (j + 1) * SLOTS, :] = pair[at : at + SLOTS, :]
         g[j * SLOTS : (j + 1) * SLOTS, :] = pair[at + SLOTS : at + 2 * SLOTS, :]
 
-    def deliver(total, at, side):
-        part = total.T.astype(jnp.bfloat16)
+    def deliver(part, at, side):
         for j in range(groups):
             to = send if j % 2 else keep
             row = (j // 2) * 2 * SLOTS + side * SLOTS
@@ -159,11 +162,20 @@
     @pl.when(taken)
     def _():
         for f in range(0, hidden, STEP):
-            part, c = (up_a, f) if f < early else (up_b, f - early)
+            part, c = columns(f)
             v = jnp.dot(x[...], part[:, c : c + STEP], preferred_element_type=jnp.float32)
             value, rise = gelu_both(v[:rows])
             active[:, f : f + STEP] = value.astype(jnp.bfloat16)
             slope[:, f : f + STEP] = rise
+
+    waiting = [(d, f) for d in range(0, width, STEP) for f in range(0, hidden, STEP)]
+    share = -(-len(waiting) * 2 * STEP // (2 * width + hidden))
+
+    def turn(count):
+        for _ in range(min(count, len(waiting))):
+            d, f = waiting.pop()
+            part, c = columns(f)
+            part[d : d + STEP, c : c + STEP] = part[d : d + STEP, c : c + STEP].T
 
     for i in range(sems.shape[0]):
 
@@ -174,25 +186,27 @@
                 total = lax.dot_general(
                     down[d : d + STEP, :], active[...], over, preferred_element_type=jnp.float32
                 )
-                deliver(total, slice(d, d + STEP), 0)
-
-    for f in range(0, hidden, STEP):
-        v = jnp.dot(g[...], down[:, f : f + STEP], preferred_element_type=jnp.float32)[:rows]
-        back_hidden[:, f : f + STEP] = (v * slope[:, f : f + STEP]).astype(jnp.bfloat16)
+                deliver(total.T.astype(jnp.bfloat16), slice(d, d + STEP), 0)
+                turn(share)
+
+    @pl.when(taken)
+    def _():
+        for f in range(0, hidden, STEP):
+            v = jnp.dot(g[...], down[:, f : f + STEP], preferred_element_type=jnp.float32)[:rows]
+            back_hidden[0:rows, f : f + STEP] = (v * slope[:, f : f + STEP]).astype(jnp.bfloat16)
+            turn(-(-share // 2))
+        turn(len(waiting))
+
     for d in range(0, width, STEP):
-        total = lax.dot_general(
-            up_a[d : d + STEP, :],
-            back_hidden[:, :early],
-            over,
-            preferred_element_type=jnp.float32,
-        )
-        total += lax.dot_general(
-            up_b[d : d + STEP, :],
-            back_hidden[:, early:],
-            over,
-            preferred_element_type=jnp.float32,
-        )
-        deliver(total, slice(d, d + STEP), 1)
+        total = 0.0
+        for f in range(0, hidden, STEP):
+            part, c = columns(f)
+            total += jnp.dot(
+                back_hidden[:, f : f + STEP],
+                part[d : d + STEP, c : c + STEP],
+                preferred_element_type=jnp.float32,
+            )
+        deliver(total.astype(jnp.bfloat16), slice(d, d + STEP), 1)
 
 
 def join_kernel(done, a, b, out):
@@ -347,16 +361,18 @@
 
     tall = max(groups * SLOTS, 128)
     short = groups * SLOTS
-    keep, send = pl.pallas_call(
+    keep, send, _, _ = pl.pallas_call(
         functools.partial(expert_kernel, groups),
-        out_shape=[pltpu.VMEM((short, width), bf16)] * 2,
+        out_shape=[pltpu.VMEM((short, width), bf16)] * 2
+        + [pltpu.VMEM(up_a.shape, bf16), pltpu.VMEM(up_b.shape, bf16)],
+        input_output_aliases={groups // 2: 2, groups // 2 + 1: 3},
         in_specs=[VM] * (groups // 2 + 2) + [FAR],
-        out_specs=[VM] * 2,
+        out_specs=[VM] * 4,
         scratch_shapes=[
             pltpu.VMEM((tall, width), bf16),
             pltpu.VMEM((tall, width), bf16),
             pltpu.VMEM((short, hidden), bf16),
-            pltpu.VMEM((short, hidden), bf16),
+            pltpu.VMEM((tall, hidden), bf16),
             pltpu.VMEM((short, hidden), f32),
             pltpu.VMEM((width, hidden), bf16),
             pltpu.SemaphoreType.DMA((3,)),

time: 64.6 us -> 61.3 us (0.949)
  Pallas kernels: 34.4 us -> 31 us
    pallas_call x1, Pallas kernels: 21.7 us -> 18.4 us  [shards(): pl.pallas_call(functools.partial(expert_kernel, groups), out_shape=[pltpu...]
  transfers between devices with their start and end apart: 10 -> 10, of which waited for: 8 -> 8; matrix products, arithmetic and copies ran while one was open for 0% -> 0% of each run, Pallas kernels for 14% -> 15%
where the time goes in v3:
time: 61.3 us; the launch traced here: 61 us
  Pallas kernels  31 us (51%)
  waiting for transfers between devices  15.6 us (25%)
  starting transfers between devices  13.6 us (22%)
  between operations  0.74 us (1%)
    pallas_call x1, Pallas kernels, shards(): pl.pallas_call(functools.partial(expert_kernel, groups), out_shape=[pltpu...  18.4 us
    ppermute x10, waiting for transfers between devices, swap(): return lax.ppermute(array, axis, [(i, i ^ mask) for i in range(n)])  15.6 us
    ppermute x10, starting transfers between devices, swap(): return lax.ppermute(array, axis, [(i, i ^ mask) for i in range(n)])  13.6 us
    pallas_call x2, Pallas kernels, load(): pl.pallas_call(functools.partial(load_kernel, start), out_shape=[pltpu.VM...  9.17 us
    pallas_call x5, Pallas kernels, call(): pl.pallas_call(body, out_shape=out_shape, in_specs=in_specs, out_specs=[V...  3.51 us
  transfers between devices with their start and end apart: 10, of which 8 were waited for; matrix products, arithmetic and copies ran while one was open for 0% of the time, Pallas kernels for 15%

profile of v3, /device:TPU:0, one launch (start us, length us, event | category | flops | bytes accessed | tf_op | source)
XLA Modules:
  0.0 61.0 jit_solution(17997656664189421744)
XLA Ops:
  0.6 1.3 %shard_map.104 = (bf16[8,4736]{1,0:T(8,128)(2,1)S(1)}, bf16[8,4736]{1,0:T(8,128)(2,1)S(1)}, bf16[8,4736]{1,0:T(8,128)(2,1)S(1)}, bf16[8,4736]{1,0:T(8,128)(2,1)S(1)}, f32[16,128]{1,0:T(8,128)S(1)}) custom-call(s32[2,6]{1,0:T(2,128)} %bitcast.9, s32[2,6]{1,0:T(2,128)} %bitcast.11, s32[2,6]{1,0:T(2,128)} %bitcast.12, bf16[6,3072]{1,0:T(8,128)(2,1)} %tok.3, ...), custom_call_target="tpu_custom_call" | custom-call | tf_op jit(solution)/shard_map/pallas_call | solution.py:289
  1.9 3.1 %collective-permute-start = (bf16[8,4736]{1,0:T(8,128)(2,1)S(1)}, bf16[8,4736]{1,0:T(8,128)(2,1)S(1)}, u32[]{:S(2)}, u32[]{:S(2)}) collective-permute-start(bf16[8,4736]{1,0:T(8,128)(2,1)S(1)} %get-tuple-element.22), channel_id=1, source_target_pairs={{0,4},{4,0},{8,12},{12,8},{1,5},{5,1},{9,13},{13,9},{2,6},{6,2},{1... | collective-permute-start | bytes 227336 | tf_op jit(solution)/shard_map/ppermute | solution.py:310
  5.0 2.6 %collective-permute-start.1 = (bf16[8,4736]{1,0:T(8,128)(2,1)S(1)}, bf16[8,4736]{1,0:T(8,128)(2,1)S(1)}, u32[]{:S(2)}, u32[]{:S(2)}) collective-permute-start(bf16[8,4736]{1,0:T(8,128)(2,1)S(1)} %get-tuple-element.23), channel_id=1, source_target_pairs={{0,8},{4,12},{8,0},{12,4},{1,9},{5,13},{9,1},{13,5},{2,10},{6,14},... | collective-permute-start | bytes 227336 | tf_op jit(solution)/shard_map/ppermute | solution.py:310
  7.6 5.5 %shard_map.105 = (bf16[3072,2560]{1,0:T(8,128)(2,1)S(1)}, f32[8,128]{1,0:T(8,128)S(1)}) custom-call(f32[16,128]{1,0:T(8,128)S(1)} %get-tuple-element.19.after.gates, bf16[1,3072,4096]{2,1,0:T(8,128)(2,1)} %weight.3), custom_call_target="tpu_custom_call" | custom-call | bytes 31457280 | tf_op jit(solution)/shard_map/pallas_call | solution.py:326
  13.1 0.8 %collective-permute-done.2.refs_3_ = bf16[8,4736]{1,0:T(8,128)(2,1)S(1)} collective-permute-done((bf16[8,4736]{1,0:T(8,128)(2,1)S(1)}, bf16[8,4736]{1,0:T(8,128)(2,1)S(1)}, u32[]{:S(2)}, u32[]{:S(2)}) %collective-permute-start.2) | collective-permute-done | bytes 75808 | tf_op jit(solution)/shard_map/ppermute | solution.py:310
  13.9 0.3 shard_map.106
  14.1 1.6 %collective-permute-start.3 = (bf16[32,3072]{1,0:T(8,128)(2,1)S(1)}, bf16[32,3072]{1,0:T(8,128)(2,1)S(1)}, u32[]{:S(2)}, u32[]{:S(2)}) collective-permute-start(bf16[32,3072]{1,0:T(8,128)(2,1)S(1)} %get-tuple-element.27.a), channel_id=1, source_target_pairs={{0,2},{1,3},{2,0},{3,1},{4,6},{5,7},{6,4},{7,5},{8,10},{9,11},{10,... | collective-permute-start | bytes 589832 | tf_op jit(solution)/shard_map/ppermute | solution.py:310
  15.7 3.7 %shard_map.107 = (bf16[3072,1536]{1,0:T(8,128)(2,1)S(1)}, f32[8,128]{1,0:T(8,128)S(1)}) custom-call(f32[32,128]{1,0:T(8,128)S(1)} %get-tuple-element.25.after.refs_3_, bf16[1,3072,4096]{2,1,0:T(8,128)(2,1)} %weight.3), custom_call_target="tpu_custom_call" | custom-call | bytes 18874368 | tf_op jit(solution)/shard_map/pallas_call | solution.py:326
  19.4 0.5 collective-permute-done.3.b
  19.9 0.1 collective-permute-start.4
  20.0 1.7 %collective-permute-done.4.refs_1_ = bf16[64,3072]{1,0:T(8,128)(2,1)S(1)} collective-permute-done((bf16[64,3072]{1,0:T(8,128)(2,1)S(1)}, bf16[64,3072]{1,0:T(8,128)(2,1)S(1)}, u32[]{:S(2)}, u32[]{:S(2)}) %collective-permute-start.4) | collective-permute-done | bytes 393248 | tf_op jit(solution)/shard_map/ppermute | solution.py:310
  21.7 18.4 %shard_map.109 = (bf16[64,3072]{1,0:T(8,128)(2,1)S(1)}, bf16[64,3072]{1,0:T(8,128)(2,1)S(1)}, bf16[3072,2560]{1,0:T(8,128)(2,1)S(1)}, bf16[3072,1536]{1,0:T(8,128)(2,1)S(1)}) custom-call(bf16[64,3072]{1,0:T(8,128)(2,1)S(1)} %shard_map.108.refs_0_, bf16[64,3072]{1,0:T(8,128)(2,1)S(1)} %collective-permute-done.4.refs_1_, ...), custom_call_target="tpu_custom_call", output_to_operand_aliasing={{2}: (2, {}), {3}: (3, {})} | custom-call | tf_op jit(solution)/shard_map/pallas_call | solution.py:364
  40.1 0.2 collective-permute-start.5
  40.3 1.6 %collective-permute-done.5.refs_1_ = bf16[64,3072]{1,0:T(8,128)(2,1)S(1)} collective-permute-done((bf16[64,3072]{1,0:T(8,128)(2,1)S(1)}, bf16[64,3072]{1,0:T(8,128)(2,1)S(1)}, u32[]{:S(2)}, u32[]{:S(2)}) %collective-permute-start.5) | collective-permute-done | bytes 393248 | tf_op jit(solution)/shard_map/ppermute | solution.py:310
  41.9 1.6 %collective-permute-start.6 = (bf16[32,3072]{1,0:T(8,128)(2,1)S(1)}, bf16[32,3072]{1,0:T(8,128)(2,1)S(1)}, u32[]{:S(2)}, u32[]{:S(2)}) collective-permute-start(bf16[32,3072]{1,0:T(8,128)(2,1)S(1)} %add_convert_fusion), channel_id=1, source_target_pairs={{0,2},{1,3},{2,0},{3,1},{4,6},{5,7},{6,4},{7,5},{8,10},{9,11},{10,... | collective-permute-start | bytes 589832 | tf_op jit(solution)/shard_map/ppermute | solution.py:310
  43.5 5.4 %collective-permute-done.6.refs_2_ = bf16[32,3072]{1,0:T(8,128)(2,1)S(1)} collective-permute-done((bf16[32,3072]{1,0:T(8,128)(2,1)S(1)}, bf16[32,3072]{1,0:T(8,128)(2,1)S(1)}, u32[]{:S(2)}, u32[]{:S(2)}) %collective-permute-start.6) | collective-permute-done | bytes 196640 | tf_op jit(solution)/shard_map/ppermute | solution.py:310
  48.9 0.4 shard_map.110
  49.3 1.3 %collective-permute-start.7 = (bf16[8,4608]{1,0:T(8,128)(2,1)S(1)}, bf16[8,4608]{1,0:T(8,128)(2,1)S(1)}, u32[]{:S(2)}, u32[]{:S(2)}) collective-permute-start(bf16[8,4608]{1,0:T(8,128)(2,1)S(1)} %get-tuple-element.33), channel_id=1, source_target_pairs={{0,4},{4,0},{8,12},{12,8},{1,5},{5,1},{9,13},{13,9},{2,6},{6,2},{1... | collective-permute-start | bytes 221192 | tf_op jit(solution)/shard_map/ppermute | solution.py:310
  50.6 2.5 %collective-permute-start.8 = (bf16[8,4608]{1,0:T(8,128)(2,1)S(1)}, bf16[8,4608]{1,0:T(8,128)(2,1)S(1)}, u32[]{:S(2)}, u32[]{:S(2)}) collective-permute-start(bf16[8,4608]{1,0:T(8,128)(2,1)S(1)} %get-tuple-element.34), channel_id=1, source_target_pairs={{0,8},{4,12},{8,0},{12,4},{1,9},{5,13},{9,1},{13,5},{2,10},{6,14},... | collective-permute-start | bytes 221192 | tf_op jit(solution)/shard_map/ppermute | solution.py:310
  53.1 0.6 collective-permute-start.9
  53.7 0.7 %collective-permute-done.7.refs_1_ = bf16[8,4608]{1,0:T(8,128)(2,1)S(1)} collective-permute-done((bf16[8,4608]{1,0:T(8,128)(2,1)S(1)}, bf16[8,4608]{1,0:T(8,128)(2,1)S(1)}, u32[]{:S(2)}, u32[]{:S(2)}) %collective-permute-start.7) | collective-permute-done | bytes 73760 | tf_op jit(solution)/shard_map/ppermute | solution.py:310
  54.4 3.4 %collective-permute-done.8.refs_2_ = bf16[8,4608]{1,0:T(8,128)(2,1)S(1)} collective-permute-done((bf16[8,4608]{1,0:T(8,128)(2,1)S(1)}, bf16[8,4608]{1,0:T(8,128)(2,1)S(1)}, u32[]{:S(2)}, u32[]{:S(2)}) %collective-permute-start.8) | collective-permute-done | bytes 73760 | tf_op jit(solution)/shard_map/ppermute | solution.py:310
  57.9 1.5 %collective-permute-done.9.refs_3_ = bf16[8,4608]{1,0:T(8,128)(2,1)S(1)} collective-permute-done((bf16[8,4608]{1,0:T(8,128)(2,1)S(1)}, bf16[8,4608]{1,0:T(8,128)(2,1)S(1)}, u32[]{:S(2)}, u32[]{:S(2)}) %collective-permute-start.9) | collective-permute-done | bytes 73760 | tf_op jit(solution)/shard_map/ppermute | solution.py:310
  59.4 1.6 %shard_map.111 = (bf16[6,3072]{1,0:T(8,128)(2,1)}, bf16[6,3072]{1,0:T(8,128)(2,1)}) custom-call(s32[2,6]{1,0:T(2,128)S(1)} %bitcast.10, bf16[6,3072]{1,0:T(8,128)(2,1)S(1)} %copy-done, bf16[6,3072]{1,0:T(8,128)(2,1)S(1)} %copy-done.1, f32[1,3072]{1,0:T(1,128)S(1)} %bitcast.8, bf16[4,3072]{1,0:T(4,128)(2,1)S(1)} %bitcast.6, ...), custom_call_target="tpu_custom_call" | custom-call | tf_op jit(solution)/shard_map/pallas_call | solution.py:289
  (15 shorter events, 0.1 us)
Async XLA Ops:
  1.9 11.2 %collective-permute-start = (bf16[8,4736]{1,0:T(8,128)(2,1)S(1)}, bf16[8,4736]{1,0:T(8,128)(2,1)S(1)}, u32[]{:S(2)}, u32[]{:S(2)}) collective-permute-start(bf16[8,4736]{1,0:T(8,128)(2,1)S(1)} %get-tuple-element.22), channel_id=1, source_target_pairs={{0,4},{4,0},{8,12},{12,8},{1,5},{5,1},{9,13},{13,9},{2,6},{6,2},{1... | collective-permute-start | bytes 227336 | tf_op jit(solution)/shard_map/ppermute | solution.py:310
  5.0 8.1 %collective-permute-start.1 = (bf16[8,4736]{1,0:T(8,128)(2,1)S(1)}, bf16[8,4736]{1,0:T(8,128)(2,1)S(1)}, u32[]{:S(2)}, u32[]{:S(2)}) collective-permute-start(bf16[8,4736]{1,0:T(8,128)(2,1)S(1)} %get-tuple-element.23), channel_id=1, source_target_pairs={{0,8},{4,12},{8,0},{12,4},{1,9},{5,13},{9,1},{13,5},{2,10},{6,14},... | collective-permute-start | bytes 227336 | tf_op jit(solution)/shard_map/ppermute | solution.py:310
  7.6 6.3 %collective-permute-start.2 = (bf16[8,4736]{1,0:T(8,128)(2,1)S(1)}, bf16[8,4736]{1,0:T(8,128)(2,1)S(1)}, u32[]{:S(2)}, u32[]{:S(2)}) collective-permute-start(bf16[8,4736]{1,0:T(8,128)(2,1)S(1)} %get-tuple-element.24), channel_id=1, source_target_pairs={{0,12},{4,8},{8,4},{12,0},{1,13},{5,9},{9,5},{13,1},{2,14},{6,10},... | collective-permute-start | bytes 227336 | tf_op jit(solution)/shard_map/ppermute | solution.py:310
  14.1 5.7 %collective-permute-start.3 = (bf16[32,3072]{1,0:T(8,128)(2,1)S(1)}, bf16[32,3072]{1,0:T(8,128)(2,1)S(1)}, u32[]{:S(2)}, u32[]{:S(2)}) collective-permute-start(bf16[32,3072]{1,0:T(8,128)(2,1)S(1)} %get-tuple-element.27.a), channel_id=1, source_target_pairs={{0,2},{1,3},{2,0},{3,1},{4,6},{5,7},{6,4},{7,5},{8,10},{9,11},{10,... | collective-permute-start | bytes 589832 | tf_op jit(solution)/shard_map/ppermute | solution.py:310
  19.9 1.8 %collective-permute-start.4 = (bf16[64,3072]{1,0:T(8,128)(2,1)S(1)}, bf16[64,3072]{1,0:T(8,128)(2,1)S(1)}, u32[]{:S(2)}, u32[]{:S(2)}) collective-permute-start(bf16[64,3072]{1,0:T(8,128)(2,1)S(1)} %shard_map.108.refs_0_), channel_id=1, source_target_pairs={{0,1},{1,0},{2,3},{3,2},{4,5},{5,4},{6,7},{7,6},{8,9},{9,8},{10,11... | collective-permute-start | bytes 1179656 | tf_op jit(solution)/shard_map/ppermute | solution.py:310
  21.7 37.7 %copy-start = (bf16[6,3072]{1,0:T(8,128)(2,1)S(1)}, bf16[6,3072]{1,0:T(8,128)(2,1)}, u32[]{:S(2)}) copy-start(bf16[6,3072]{1,0:T(8,128)(2,1)} %tok.3) | copy-start | bytes 110596
  21.7 37.7 %copy-start.1 = (bf16[6,3072]{1,0:T(8,128)(2,1)S(1)}, bf16[6,3072]{1,0:T(8,128)(2,1)}, u32[]{:S(2)}) copy-start(bf16[6,3072]{1,0:T(8,128)(2,1)} %grad.3) | copy-start | bytes 110596
  21.7 37.7 %copy-start.2 = (bf16[3072,4]{0,1:T(4,128)(2,1)S(1)}, bf16[3072,4]{0,1:T(4,128)(2,1)}, u32[]{:S(2)}) copy-start(bf16[3072,4]{0,1:T(4,128)(2,1)} %param.11) | copy-start | bytes 73732
  21.7 37.7 %copy-start.3 = (f32[3072]{0:T(1024)S(1)}, f32[3072]{0:T(1024)}, u32[]{:S(2)}) copy-start(f32[3072]{0:T(1024)} %param.10) | copy-start | bytes 36868
  21.7 37.7 %copy-start.4 = (s32[6,2]{0,1:T(2,128)S(1)}, s32[6,2]{0,1:T(2,128)}, u32[]{:S(2)}) copy-start(s32[6,2]{0,1:T(2,128)} %param.14) | copy-start | bytes 148
  40.1 1.8 %collective-permute-start.5 = (bf16[64,3072]{1,0:T(8,128)(2,1)S(1)}, bf16[64,3072]{1,0:T(8,128)(2,1)S(1)}, u32[]{:S(2)}, u32[]{:S(2)}) collective-permute-start(bf16[64,3072]{1,0:T(8,128)(2,1)S(1)} %get-tuple-element.31), channel_id=1, source_target_pairs={{0,1},{1,0},{2,3},{3,2},{4,5},{5,4},{6,7},{7,6},{8,9},{9,8},{10,11... | collective-permute-start | bytes 1179656 | tf_op jit(solution)/shard_map/ppermute | solution.py:310
  41.9 7.0 %collective-permute-start.6 = (bf16[32,3072]{1,0:T(8,128)(2,1)S(1)}, bf16[32,3072]{1,0:T(8,128)(2,1)S(1)}, u32[]{:S(2)}, u32[]{:S(2)}) collective-permute-start(bf16[32,3072]{1,0:T(8,128)(2,1)S(1)} %add_convert_fusion), channel_id=1, source_target_pairs={{0,2},{1,3},{2,0},{3,1},{4,6},{5,7},{6,4},{7,5},{8,10},{9,11},{10,... | collective-permute-start | bytes 589832 | tf_op jit(solution)/shard_map/ppermute | solution.py:310
  49.3 5.1 %collective-permute-start.7 = (bf16[8,4608]{1,0:T(8,128)(2,1)S(1)}, bf16[8,4608]{1,0:T(8,128)(2,1)S(1)}, u32[]{:S(2)}, u32[]{:S(2)}) collective-permute-start(bf16[8,4608]{1,0:T(8,128)(2,1)S(1)} %get-tuple-element.33), channel_id=1, source_target_pairs={{0,4},{4,0},{8,12},{12,8},{1,5},{5,1},{9,13},{13,9},{2,6},{6,2},{1... | collective-permute-start | bytes 221192 | tf_op jit(solution)/shard_map/ppermute | solution.py:310
  50.6 7.3 %collective-permute-start.8 = (bf16[8,4608]{1,0:T(8,128)(2,1)S(1)}, bf16[8,4608]{1,0:T(8,128)(2,1)S(1)}, u32[]{:S(2)}, u32[]{:S(2)}) collective-permute-start(bf16[8,4608]{1,0:T(8,128)(2,1)S(1)} %get-tuple-element.34), channel_id=1, source_target_pairs={{0,8},{4,12},{8,0},{12,4},{1,9},{5,13},{9,1},{13,5},{2,10},{6,14},... | collective-permute-start | bytes 221192 | tf_op jit(solution)/shard_map/ppermute | solution.py:310
  53.1 6.3 %collective-permute-start.9 = (bf16[8,4608]{1,0:T(8,128)(2,1)S(1)}, bf16[8,4608]{1,0:T(8,128)(2,1)S(1)}, u32[]{:S(2)}, u32[]{:S(2)}) collective-permute-start(bf16[8,4608]{1,0:T(8,128)(2,1)S(1)} %get-tuple-element.35), channel_id=1, source_target_pairs={{0,12},{4,8},{8,4},{12,0},{1,13},{5,9},{9,5},{13,1},{2,14},{6,10},... | collective-permute-start | bytes 221192 | tf_op jit(solution)/shard_map/ppermute | solution.py:310

commit v4 on v3

--- a/solution.py
+++ b/solution.py
@@ -124,38 +124,32 @@
 
 
 def expert_kernel(groups, *refs):
-    pairs = refs[: groups // 2]
-    (up_a_in, up_b_in, down_hbm, keep, send, up_a, up_b) = refs[groups // 2 : groups // 2 + 7]
-    x, g, active, back_hidden, slope, down, sems = refs[groups // 2 + 7 :]
-    del up_a_in, up_b_in
+    bins, refs = refs[:groups], refs[groups:]
+    _, _, down_hbm, up_a, up_b = refs[:5]
+    outs, refs = refs[5 : 5 + groups], refs[5 + groups :]
+    x, g, active, back_hidden, slope, down, sems = refs
     rows = groups * SLOTS
     width, early = up_a.shape
     hidden = early + up_b.shape[1]
-    block = width // sems.shape[0]
+    edges = [0, width // 3, width * 2 // 3, width]
     over = (((1,), (1,)), ((), ()))
 
     def fetch(i):
-        at = pl.ds(i * block, block)
+        at = pl.ds(edges[i], edges[i + 1] - edges[i])
         return pltpu.make_async_copy(down_hbm.at[0, at, :], down.at[at, :], sems.at[i])
 
     def columns(f):
         return (up_a, f) if f < early else (up_b, f - early)
 
-    for i in range(sems.shape[0]):
+    for i in range(len(edges) - 1):
         fetch(i).start()
-    x[...] = jnp.zeros_like(x)
-    g[...] = jnp.zeros_like(g)
-    back_hidden[...] = jnp.zeros_like(back_hidden)
     for j in range(groups):
-        pair, at = pairs[j % (groups // 2)], j // (groups // 2) * 2 * SLOTS
-        x[j * SLOTS : (j + 1) * SLOTS, :] = pair[at : at + SLOTS, :]
-        g[j * SLOTS : (j + 1) * SLOTS, :] = pair[at + SLOTS : at + 2 * SLOTS, :]
+        x[j * SLOTS : (j + 1) * SLOTS, :] = bins[j][0:SLOTS, :]
+        g[j * SLOTS : (j + 1) * SLOTS, :] = bins[j][SLOTS : 2 * SLOTS, :]
 
     def deliver(part, at, side):
-        for j in range(groups):
-            to = send if j % 2 else keep
-            row = (j // 2) * 2 * SLOTS + side * SLOTS
-            to[row : row + SLOTS, at] = part[j * SLOTS : (j + 1) * SLOTS]
+        for j, out in enumerate(outs):
+            out[side * SLOTS : (side + 1) * SLOTS, at] = part[j * SLOTS : (j + 1) * SLOTS]
 
     taken = lax.axis_index("expert") >= 0
 
@@ -177,12 +171,12 @@
             part, c = columns(f)
             part[d : d + STEP, c : c + STEP] = part[d : d + STEP, c : c + STEP].T
 
-    for i in range(sems.shape[0]):
+    for i in range(len(edges) - 1):
 
         @pl.when(taken)
         def _(i=i):
             fetch(i).wait()
-            for d in range(i * block, (i + 1) * block, STEP):
+            for d in range(edges[i], edges[i + 1], STEP):
                 total = lax.dot_general(
                     down[d : d + STEP, :], active[...], over, preferred_element_type=jnp.float32
                 )
@@ -209,10 +203,9 @@
         deliver(total.astype(jnp.bfloat16), slice(d, d + STEP), 1)
 
 
-def join_kernel(done, a, b, out):
+def join_kernel(done, rows, out):
     del done
-    out[0 : 2 * SLOTS, :] = a[...]
-    out[2 * SLOTS :, :] = b[...]
+    out[...] = rows[...]
 
 
 def add_kernel(a, b, out):
@@ -224,9 +217,9 @@
     parts, placed, replies = refs[:n_parts], refs[n_parts], refs[n_parts + 1 :]
     width = parts[0].shape[1]
     pieces, tail, head = layout(rows, width)
-    total = parts[0][0 : 2 * SLOTS, :].astype(jnp.float32)
+    total = parts[0][...].astype(jnp.float32)
     for p in parts[1:]:
-        total = total + p[0 : 2 * SLOTS, :].astype(jnp.float32)
+        total = total + p[...].astype(jnp.float32)
     total = total.astype(jnp.bfloat16)
     both = jnp.concatenate([total[:SLOTS], total[SLOTS:]], axis=1)
     onehot = placed[...].astype(jnp.bfloat16)
@@ -347,13 +340,13 @@
     up_b, done = load(early, hidden, near(placed))
 
     mask = groups // 2
-    pair = call(
+    far_rows = call(
         join_kernel,
-        [pltpu.VMEM((4 * SLOTS, width), bf16)],
-        [VM] * 3,
-        [near(a) for a in (done, own, swap(own, "tensor", mask))],
+        [pltpu.VMEM((2 * SLOTS, width), bf16)],
+        [VM] * 2,
+        [near(a) for a in (done, swap(own, "tensor", mask))],
     )[0]
-    bins = {0: pair}
+    bins = {0: own, mask: far_rows}
     mask //= 2
     while mask:
         bins.update({j | mask: swap(b, "tensor", mask) for j, b in bins.items()})
@@ -361,13 +354,13 @@
 
     tall = max(groups * SLOTS, 128)
     short = groups * SLOTS
-    keep, send, _, _ = pl.pallas_call(
+    _, _, *sums = pl.pallas_call(
         functools.partial(expert_kernel, groups),
-        out_shape=[pltpu.VMEM((short, width), bf16)] * 2
-        + [pltpu.VMEM(up_a.shape, bf16), pltpu.VMEM(up_b.shape, bf16)],
-        input_output_aliases={groups // 2: 2, groups // 2 + 1: 3},
-        in_specs=[VM] * (groups // 2 + 2) + [FAR],
-        out_specs=[VM] * 4,
+        out_shape=[pltpu.VMEM(up_a.shape, bf16), pltpu.VMEM(up_b.shape, bf16)]
+        + [pltpu.VMEM((2 * SLOTS, width), bf16)] * groups,
+        input_output_aliases={groups: 0, groups + 1: 1},
+        in_specs=[VM] * (groups + 2) + [FAR],
+        out_specs=[VM] * (groups + 2),
         scratch_shapes=[
             pltpu.VMEM((tall, width), bf16),
             pltpu.VMEM((tall, width), bf16),
@@ -378,14 +371,14 @@
             pltpu.SemaphoreType.DMA((3,)),
         ],
         compiler_params=pltpu.CompilerParams(vmem_limit_bytes=32 * 2**20),
-    )(*[near(bins[j]) for j in range(groups // 2)], near(up_a), near(up_b), far(down_weight))
-
-    got = swap(send, "tensor", 1)
+    )(*[near(bins[j]) for j in range(groups)], near(up_a), near(up_b), far(down_weight))
+
     piece = pltpu.VMEM((2 * SLOTS, width), bf16)
-    firsts, sums = [keep, got], {}
-    for i in range(1, groups // 2):
-        at = slice(2 * SLOTS * i, 2 * SLOTS * (i + 1))
-        sums[2 * i] = (keep[at].astype(f32) + got[at].astype(f32)).astype(bf16)
+    firsts = [sums[0], swap(sums[1], "tensor", 1)]
+    sums = {
+        j: (sums[j].astype(f32) + swap(sums[j + 1], "tensor", 1).astype(f32)).astype(bf16)
+        for j in range(2, groups, 2)
+    }
     mask = 2
     while mask < groups:
         came = {j ^ mask: swap(a, "tensor", mask) for j, a in sums.items() if j & mask}

time: 61.3 us -> 60.6 us (0.989)
  waiting for transfers between devices: 15.6 us -> 14.6 us
    ppermute x10 -> x12, waiting for transfers between devices: 15.6 us -> 14.6 us  [swap(): return lax.ppermute(array, axis, [(i, i ^ mask) for i in range(n)])]
    ppermute x10 -> x12, starting transfers between devices: 13.6 us -> 14 us  [swap(): return lax.ppermute(array, axis, [(i, i ^ mask) for i in range(n)])]
  transfers between devices with their start and end apart: 10 -> 12, of which waited for: 8 -> 8; matrix products, arithmetic and copies ran while one was open for 0% -> 0% of each run, Pallas kernels for 15% -> 15%
where the time goes in v4:
time: 60.6 us; the launch traced here: 60.3 us
  Pallas kernels  30.9 us (51%)
  waiting for transfers between devices  14.6 us (24%)
  starting transfers between devices  14 us (23%)
  between operations  0.74 us (1%)
    pallas_call x1, Pallas kernels, shards(): pl.pallas_call(functools.partial(expert_kernel, groups), out_shape=[pltpu...  18.2 us
    ppermute x12, waiting for transfers between devices, swap(): return lax.ppermute(array, axis, [(i, i ^ mask) for i in range(n)])  14.6 us
    ppermute x12, starting transfers between devices, swap(): return lax.ppermute(array, axis, [(i, i ^ mask) for i in range(n)])  14 us
    pallas_call x2, Pallas kernels, load(): pl.pallas_call(functools.partial(load_kernel, start), out_shape=[pltpu.VM...  9.17 us
    pallas_call x5, Pallas kernels, call(): pl.pallas_call(body, out_shape=out_shape, in_specs=in_specs, out_specs=[V...  3.5 us
  transfers between devices with their start and end apart: 12, of which 8 were waited for; matrix products, arithmetic and copies ran while one was open for 0% of the time, Pallas kernels for 15%

profile of v4, /device:TPU:0, one launch (start us, length us, event | category | flops | bytes accessed | tf_op | source)
XLA Modules:
  0.0 60.3 jit_solution(13899989488142834845)
XLA Ops:
  0.6 1.3 %shard_map.104 = (bf16[8,4736]{1,0:T(8,128)(2,1)S(1)}, bf16[8,4736]{1,0:T(8,128)(2,1)S(1)}, bf16[8,4736]{1,0:T(8,128)(2,1)S(1)}, bf16[8,4736]{1,0:T(8,128)(2,1)S(1)}, f32[16,128]{1,0:T(8,128)S(1)}) custom-call(s32[2,6]{1,0:T(2,128)} %bitcast.9, s32[2,6]{1,0:T(2,128)} %bitcast.11, s32[2,6]{1,0:T(2,128)} %bitcast.12, bf16[6,3072]{1,0:T(8,128)(2,1)} %tok.3, ...), custom_call_target="tpu_custom_call" | custom-call | tf_op jit(solution)/shard_map/pallas_call | solution.py:282
  1.9 3.1 %collective-permute-start = (bf16[8,4736]{1,0:T(8,128)(2,1)S(1)}, bf16[8,4736]{1,0:T(8,128)(2,1)S(1)}, u32[]{:S(2)}, u32[]{:S(2)}) collective-permute-start(bf16[8,4736]{1,0:T(8,128)(2,1)S(1)} %get-tuple-element.24), channel_id=1, source_target_pairs={{0,4},{4,0},{8,12},{12,8},{1,5},{5,1},{9,13},{13,9},{2,6},{6,2},{1... | collective-permute-start | bytes 227336 | tf_op jit(solution)/shard_map/ppermute | solution.py:303
  5.0 2.6 %collective-permute-start.1 = (bf16[8,4736]{1,0:T(8,128)(2,1)S(1)}, bf16[8,4736]{1,0:T(8,128)(2,1)S(1)}, u32[]{:S(2)}, u32[]{:S(2)}) collective-permute-start(bf16[8,4736]{1,0:T(8,128)(2,1)S(1)} %get-tuple-element.25), channel_id=1, source_target_pairs={{0,8},{4,12},{8,0},{12,4},{1,9},{5,13},{9,1},{13,5},{2,10},{6,14},... | collective-permute-start | bytes 227336 | tf_op jit(solution)/shard_map/ppermute | solution.py:303
  7.6 5.5 %shard_map.105 = (bf16[3072,2560]{1,0:T(8,128)(2,1)S(1)}, f32[8,128]{1,0:T(8,128)S(1)}) custom-call(f32[16,128]{1,0:T(8,128)S(1)} %get-tuple-element.21.after.gates, bf16[1,3072,4096]{2,1,0:T(8,128)(2,1)} %weight.3), custom_call_target="tpu_custom_call" | custom-call | bytes 31457280 | tf_op jit(solution)/shard_map/pallas_call | solution.py:319
  13.1 0.8 %collective-permute-done.2.refs_3_ = bf16[8,4736]{1,0:T(8,128)(2,1)S(1)} collective-permute-done((bf16[8,4736]{1,0:T(8,128)(2,1)S(1)}, bf16[8,4736]{1,0:T(8,128)(2,1)S(1)}, u32[]{:S(2)}, u32[]{:S(2)}) %collective-permute-start.2) | collective-permute-done | bytes 75808 | tf_op jit(solution)/shard_map/ppermute | solution.py:303
  13.9 0.3 shard_map.106
  14.1 1.6 %collective-permute-start.4 = (bf16[32,3072]{1,0:T(8,128)(2,1)S(1)}, bf16[32,3072]{1,0:T(8,128)(2,1)S(1)}, u32[]{:S(2)}, u32[]{:S(2)}) collective-permute-start(bf16[32,3072]{1,0:T(8,128)(2,1)S(1)} %get-tuple-element.27.refs_0_), channel_id=1, source_target_pairs={{0,2},{1,3},{2,0},{3,1},{4,6},{5,7},{6,4},{7,5},{8,10},{9,11},{10,... | collective-permute-start | bytes 589832 | tf_op jit(solution)/shard_map/ppermute | solution.py:303
  15.7 3.7 %shard_map.107 = (bf16[3072,1536]{1,0:T(8,128)(2,1)S(1)}, f32[8,128]{1,0:T(8,128)S(1)}) custom-call(f32[32,128]{1,0:T(8,128)S(1)} %get-tuple-element.28.after.refs_3_, bf16[1,3072,4096]{2,1,0:T(8,128)(2,1)} %weight.3), custom_call_target="tpu_custom_call" | custom-call | bytes 18874368 | tf_op jit(solution)/shard_map/pallas_call | solution.py:319
  19.4 0.4 collective-permute-done.4.rows
  20.0 1.4 %collective-permute-done.5.refs_3_ = bf16[32,3072]{1,0:T(8,128)(2,1)S(1)} collective-permute-done((bf16[32,3072]{1,0:T(8,128)(2,1)S(1)}, bf16[32,3072]{1,0:T(8,128)(2,1)S(1)}, u32[]{:S(2)}, u32[]{:S(2)}) %collective-permute-start.5) | collective-permute-done | bytes 196640 | tf_op jit(solution)/shard_map/ppermute | solution.py:303
  21.4 18.2 %shard_map.109 = (bf16[3072,2560]{1,0:T(8,128)(2,1)S(1)}, bf16[3072,1536]{1,0:T(8,128)(2,1)S(1)}, bf16[32,3072]{1,0:T(8,128)(2,1)S(1)}, bf16[32,3072]{1,0:T(8,12...) custom-call(bf16[32,3072]{1,0:T(8,128)(2,1)S(1)} %get-tuple-element., ...), custom_call_target="tpu_custom_call", output_to_operand_aliasing={{0}: (4, {}), {1}: (5, {})} | custom-call | tf_op jit(solution)/shard_map/pallas_call | solution.py:357
  39.7 0.2 collective-permute-start.7
  39.9 0.4 collective-permute-start.6
  40.3 0.9 %collective-permute-done.7 = bf16[32,3072]{1,0:T(8,128)(2,1)S(1)} collective-permute-done((bf16[32,3072]{1,0:T(8,128)(2,1)S(1)}, bf16[32,3072]{1,0:T(8,128)(2,1)S(1)}, u32[]{:S(2)}, u32[]{:S(2)}) %collective-permute-start.7) | collective-permute-done | bytes 196640 | tf_op jit(solution)/shard_map/ppermute | solution.py:303
  41.2 1.6 %collective-permute-start.8 = (bf16[32,3072]{1,0:T(8,128)(2,1)S(1)}, bf16[32,3072]{1,0:T(8,128)(2,1)S(1)}, u32[]{:S(2)}, u32[]{:S(2)}) collective-permute-start(bf16[32,3072]{1,0:T(8,128)(2,1)S(1)} %add_convert_fusion), channel_id=1, source_target_pairs={{0,2},{1,3},{2,0},{3,1},{4,6},{5,7},{6,4},{7,5},{8,10},{9,11},{10,... | collective-permute-start | bytes 589832 | tf_op jit(solution)/shard_map/ppermute | solution.py:303
  42.8 5.4 %collective-permute-done.8.refs_2_ = bf16[32,3072]{1,0:T(8,128)(2,1)S(1)} collective-permute-done((bf16[32,3072]{1,0:T(8,128)(2,1)S(1)}, bf16[32,3072]{1,0:T(8,128)(2,1)S(1)}, u32[]{:S(2)}, u32[]{:S(2)}) %collective-permute-start.8) | collective-permute-done | bytes 196640 | tf_op jit(solution)/shard_map/ppermute | solution.py:303
  48.2 0.4 shard_map.110
  48.6 1.3 %collective-permute-start.9 = (bf16[8,4608]{1,0:T(8,128)(2,1)S(1)}, bf16[8,4608]{1,0:T(8,128)(2,1)S(1)}, u32[]{:S(2)}, u32[]{:S(2)}) collective-permute-start(bf16[8,4608]{1,0:T(8,128)(2,1)S(1)} %get-tuple-element.37), channel_id=1, source_target_pairs={{0,4},{4,0},{8,12},{12,8},{1,5},{5,1},{9,13},{13,9},{2,6},{6,2},{1... | collective-permute-start | bytes 221192 | tf_op jit(solution)/shard_map/ppermute | solution.py:303
  49.9 2.5 %collective-permute-start.10 = (bf16[8,4608]{1,0:T(8,128)(2,1)S(1)}, bf16[8,4608]{1,0:T(8,128)(2,1)S(1)}, u32[]{:S(2)}, u32[]{:S(2)}) collective-permute-start(bf16[8,4608]{1,0:T(8,128)(2,1)S(1)} %get-tuple-element.38), channel_id=1, source_target_pairs={{0,8},{4,12},{8,0},{12,4},{1,9},{5,13},{9,1},{13,5},{2,10},{6,14},... | collective-permute-start | bytes 221192 | tf_op jit(solution)/shard_map/ppermute | solution.py:303
  52.4 0.6 %collective-permute-start.11 = (bf16[8,4608]{1,0:T(8,128)(2,1)S(1)}, bf16[8,4608]{1,0:T(8,128)(2,1)S(1)}, u32[]{:S(2)}, u32[]{:S(2)}) collective-permute-start(bf16[8,4608]{1,0:T(8,128)(2,1)S(1)} %get-tuple-element.39), channel_id=1, source_target_pairs={{0,12},{4,8},{8,4},{12,0},{1,13},{5,9},{9,5},{13,1},{2,14},{6,10},... | collective-permute-start | bytes 221192 | tf_op jit(solution)/shard_map/ppermute | solution.py:303
  53.1 0.7 %collective-permute-done.9.refs_1_ = bf16[8,4608]{1,0:T(8,128)(2,1)S(1)} collective-permute-done((bf16[8,4608]{1,0:T(8,128)(2,1)S(1)}, bf16[8,4608]{1,0:T(8,128)(2,1)S(1)}, u32[]{:S(2)}, u32[]{:S(2)}) %collective-permute-start.9) | collective-permute-done | bytes 73760 | tf_op jit(solution)/shard_map/ppermute | solution.py:303
  53.8 3.4 %collective-permute-done.10.refs_2_ = bf16[8,4608]{1,0:T(8,128)(2,1)S(1)} collective-permute-done((bf16[8,4608]{1,0:T(8,128)(2,1)S(1)}, bf16[8,4608]{1,0:T(8,128)(2,1)S(1)}, u32[]{:S(2)}, u32[]{:S(2)}) %collective-permute-start.10) | collective-permute-done | bytes 73760 | tf_op jit(solution)/shard_map/ppermute | solution.py:303
  57.2 1.5 %collective-permute-done.11.refs_3_ = bf16[8,4608]{1,0:T(8,128)(2,1)S(1)} collective-permute-done((bf16[8,4608]{1,0:T(8,128)(2,1)S(1)}, bf16[8,4608]{1,0:T(8,128)(2,1)S(1)}, u32[]{:S(2)}, u32[]{:S(2)}) %collective-permute-start.11) | collective-permute-done | bytes 73760 | tf_op jit(solution)/shard_map/ppermute | solution.py:303
  58.7 1.6 %shard_map.111 = (bf16[6,3072]{1,0:T(8,128)(2,1)}, bf16[6,3072]{1,0:T(8,128)(2,1)}) custom-call(s32[2,6]{1,0:T(2,128)S(1)} %bitcast.10, bf16[6,3072]{1,0:T(8,128)(2,1)S(1)} %copy-done, bf16[6,3072]{1,0:T(8,128)(2,1)S(1)} %copy-done.1, f32[1,3072]{1,0:T(1,128)S(1)} %bitcast.8, bf16[4,3072]{1,0:T(4,128)(2,1)S(1)} %bitcast.6, ...), custom_call_target="tpu_custom_call" | custom-call | tf_op jit(solution)/shard_map/pallas_call | solution.py:282
  (19 shorter events, 0.2 us)
Async XLA Ops:
  1.9 11.2 %collective-permute-start = (bf16[8,4736]{1,0:T(8,128)(2,1)S(1)}, bf16[8,4736]{1,0:T(8,128)(2,1)S(1)}, u32[]{:S(2)}, u32[]{:S(2)}) collective-permute-start(bf16[8,4736]{1,0:T(8,128)(2,1)S(1)} %get-tuple-element.24), channel_id=1, source_target_pairs={{0,4},{4,0},{8,12},{12,8},{1,5},{5,1},{9,13},{13,9},{2,6},{6,2},{1... | collective-permute-start | bytes 227336 | tf_op jit(solution)/shard_map/ppermute | solution.py:303
  5.0 8.1 %collective-permute-start.1 = (bf16[8,4736]{1,0:T(8,128)(2,1)S(1)}, bf16[8,4736]{1,0:T(8,128)(2,1)S(1)}, u32[]{:S(2)}, u32[]{:S(2)}) collective-permute-start(bf16[8,4736]{1,0:T(8,128)(2,1)S(1)} %get-tuple-element.25), channel_id=1, source_target_pairs={{0,8},{4,12},{8,0},{12,4},{1,9},{5,13},{9,1},{13,5},{2,10},{6,14},... | collective-permute-start | bytes 227336 | tf_op jit(solution)/shard_map/ppermute | solution.py:303
  7.6 6.3 %collective-permute-start.2 = (bf16[8,4736]{1,0:T(8,128)(2,1)S(1)}, bf16[8,4736]{1,0:T(8,128)(2,1)S(1)}, u32[]{:S(2)}, u32[]{:S(2)}) collective-permute-start(bf16[8,4736]{1,0:T(8,128)(2,1)S(1)} %get-tuple-element.26), channel_id=1, source_target_pairs={{0,12},{4,8},{8,4},{12,0},{1,13},{5,9},{9,5},{13,1},{2,14},{6,10},... | collective-permute-start | bytes 227336 | tf_op jit(solution)/shard_map/ppermute | solution.py:303
  14.1 5.7 %collective-permute-start.4 = (bf16[32,3072]{1,0:T(8,128)(2,1)S(1)}, bf16[32,3072]{1,0:T(8,128)(2,1)S(1)}, u32[]{:S(2)}, u32[]{:S(2)}) collective-permute-start(bf16[32,3072]{1,0:T(8,128)(2,1)S(1)} %get-tuple-element.27.refs_0_), channel_id=1, source_target_pairs={{0,2},{1,3},{2,0},{3,1},{4,6},{5,7},{6,4},{7,5},{8,10},{9,11},{10,... | collective-permute-start | bytes 589832 | tf_op jit(solution)/shard_map/ppermute | solution.py:303
  15.7 4.3 %collective-permute-start.3 = (bf16[32,3072]{1,0:T(8,128)(2,1)S(1)}, bf16[32,3072]{1,0:T(8,128)(2,1)S(1)}, u32[]{:S(2)}, u32[]{:S(2)}) collective-permute-start(bf16[32,3072]{1,0:T(8,128)(2,1)S(1)} %get-tuple-element.27.refs_0_), channel_id=1, source_target_pairs={{0,1},{1,0},{2,3},{3,2},{4,5},{5,4},{6,7},{7,6},{8,9},{9,8},{10,11... | collective-permute-start | bytes 589832 | tf_op jit(solution)/shard_map/ppermute | solution.py:303
  19.9 1.5 %collective-permute-start.5 = (bf16[32,3072]{1,0:T(8,128)(2,1)S(1)}, bf16[32,3072]{1,0:T(8,128)(2,1)S(1)}, u32[]{:S(2)}, u32[]{:S(2)}) collective-permute-start(bf16[32,3072]{1,0:T(8,128)(2,1)S(1)} %shard_map.108.refs_2_), channel_id=1, source_target_pairs={{0,1},{1,0},{2,3},{3,2},{4,5},{5,4},{6,7},{7,6},{8,9},{9,8},{10,11... | collective-permute-start | bytes 589832 | tf_op jit(solution)/shard_map/ppermute | solution.py:303
  21.4 37.3 %copy-start = (bf16[6,3072]{1,0:T(8,128)(2,1)S(1)}, bf16[6,3072]{1,0:T(8,128)(2,1)}, u32[]{:S(2)}) copy-start(bf16[6,3072]{1,0:T(8,128)(2,1)} %tok.3) | copy-start | bytes 110596
  21.4 37.3 %copy-start.1 = (bf16[6,3072]{1,0:T(8,128)(2,1)S(1)}, bf16[6,3072]{1,0:T(8,128)(2,1)}, u32[]{:S(2)}) copy-start(bf16[6,3072]{1,0:T(8,128)(2,1)} %grad.3) | copy-start | bytes 110596
  21.4 37.3 %copy-start.2 = (bf16[3072,4]{0,1:T(4,128)(2,1)S(1)}, bf16[3072,4]{0,1:T(4,128)(2,1)}, u32[]{:S(2)}) copy-start(bf16[3072,4]{0,1:T(4,128)(2,1)} %param.11) | copy-start | bytes 73732
  21.4 37.3 %copy-start.3 = (f32[3072]{0:T(1024)S(1)}, f32[3072]{0:T(1024)}, u32[]{:S(2)}) copy-start(f32[3072]{0:T(1024)} %param.10) | copy-start | bytes 36868
  21.4 37.3 %copy-start.4 = (s32[6,2]{0,1:T(2,128)S(1)}, s32[6,2]{0,1:T(2,128)}, u32[]{:S(2)}) copy-start(s32[6,2]{0,1:T(2,128)} %param.14) | copy-start | bytes 148
  39.7 1.5 %collective-permute-start.7 = (bf16[32,3072]{1,0:T(8,128)(2,1)S(1)}, bf16[32,3072]{1,0:T(8,128)(2,1)S(1)}, u32[]{:S(2)}, u32[]{:S(2)}) collective-permute-start(bf16[32,3072]{1,0:T(8,128)(2,1)S(1)} %get-tuple-element.35), channel_id=1, source_target_pairs={{0,1},{1,0},{2,3},{3,2},{4,5},{5,4},{6,7},{7,6},{8,9},{9,8},{10,11... | collective-permute-start | bytes 589832 | tf_op jit(solution)/shard_map/ppermute | solution.py:303
  39.9 3.0 %collective-permute-start.6 = (bf16[32,3072]{1,0:T(8,128)(2,1)S(1)}, bf16[32,3072]{1,0:T(8,128)(2,1)S(1)}, u32[]{:S(2)}, u32[]{:S(2)}) collective-permute-start(bf16[32,3072]{1,0:T(8,128)(2,1)S(1)} %get-tuple-element.33), channel_id=1, source_target_pairs={{0,1},{1,0},{2,3},{3,2},{4,5},{5,4},{6,7},{7,6},{8,9},{9,8},{10,11... | collective-permute-start | bytes 589832 | tf_op jit(solution)/shard_map/ppermute | solution.py:303
  41.2 7.0 %collective-permute-start.8 = (bf16[32,3072]{1,0:T(8,128)(2,1)S(1)}, bf16[32,3072]{1,0:T(8,128)(2,1)S(1)}, u32[]{:S(2)}, u32[]{:S(2)}) collective-permute-start(bf16[32,3072]{1,0:T(8,128)(2,1)S(1)} %add_convert_fusion), channel_id=1, source_target_pairs={{0,2},{1,3},{2,0},{3,1},{4,6},{5,7},{6,4},{7,5},{8,10},{9,11},{10,... | collective-permute-start | bytes 589832 | tf_op jit(solution)/shard_map/ppermute | solution.py:303
  48.6 5.2 %collective-permute-start.9 = (bf16[8,4608]{1,0:T(8,128)(2,1)S(1)}, bf16[8,4608]{1,0:T(8,128)(2,1)S(1)}, u32[]{:S(2)}, u32[]{:S(2)}) collective-permute-start(bf16[8,4608]{1,0:T(8,128)(2,1)S(1)} %get-tuple-element.37), channel_id=1, source_target_pairs={{0,4},{4,0},{8,12},{12,8},{1,5},{5,1},{9,13},{13,9},{2,6},{6,2},{1... | collective-permute-start | bytes 221192 | tf_op jit(solution)/shard_map/ppermute | solution.py:303
  49.9 7.3 %collective-permute-start.10 = (bf16[8,4608]{1,0:T(8,128)(2,1)S(1)}, bf16[8,4608]{1,0:T(8,128)(2,1)S(1)}, u32[]{:S(2)}, u32[]{:S(2)}) collective-permute-start(bf16[8,4608]{1,0:T(8,128)(2,1)S(1)} %get-tuple-element.38), channel_id=1, source_target_pairs={{0,8},{4,12},{8,0},{12,4},{1,9},{5,13},{9,1},{13,5},{2,10},{6,14},... | collective-permute-start | bytes 221192 | tf_op jit(solution)/shard_map/ppermute | solution.py:303
  52.4 6.3 %collective-permute-start.11 = (bf16[8,4608]{1,0:T(8,128)(2,1)S(1)}, bf16[8,4608]{1,0:T(8,128)(2,1)S(1)}, u32[]{:S(2)}, u32[]{:S(2)}) collective-permute-start(bf16[8,4608]{1,0:T(8,128)(2,1)S(1)} %get-tuple-element.39), channel_id=1, source_target_pairs={{0,12},{4,8},{8,4},{12,0},{1,13},{5,9},{9,5},{13,1},{2,14},{6,10},... | collective-permute-start | bytes 221192 | tf_op jit(solution)/shard_map/ppermute | solution.py:303

commit v5 on v4

--- a/solution.py
+++ b/solution.py
@@ -48,7 +48,7 @@
 
 
 def pack_kernel(ids, slots, kept, tok, grad, gain, router, *outs):
-    messages, gates_ref = outs[:-1], outs[-1]
+    messages, (gates_ref, tok_out, grad_out, gain_out, router_out) = outs[:-5], outs[-5:]
     rows, width = tok.shape
     experts = router.shape[0]
     pieces, tail, head = layout(rows, width)
@@ -68,8 +68,13 @@
     gate0 = 1.0 / (1.0 + jnp.exp(pick1 - pick0))
     gate1 = 1.0 / (1.0 + jnp.exp(pick0 - pick1))
     gates_ref[...] = jnp.zeros_like(gates_ref)
-    gates_ref[0:rows, :] = gate0
-    gates_ref[PAD : PAD + rows, :] = gate1
+    kept_for_later = (gate0, gate1, id0.astype(jnp.float32), id1.astype(jnp.float32), inverse)
+    for i, entry in enumerate(kept_for_later):
+        gates_ref[i * PAD : i * PAD + rows, :] = jnp.broadcast_to(entry, (rows, LANES))
+    tok_out[...] = tok[...]
+    grad_out[...] = grad[...]
+    gain_out[...] = gain[...]
+    router_out[...] = router[...]
     row = lax.broadcasted_iota(jnp.int32, (PAD, LANES), 0)
     field = lax.broadcasted_iota(jnp.int32, (PAD, LANES), 1) // FIELD
     for k, out in enumerate(messages):
@@ -116,6 +121,33 @@
     bins[SLOTS : 2 * SLOTS, width - tail :] = rest.astype(jnp.bfloat16)
 
 
+def later(gates, i, rows):
+    return gates[i * PAD : i * PAD + rows, 0:1]
+
+
+def prepare_kernel(start, gates, tok, gain, router, weight, out, done, *refs):
+    scale, along, share, fixed, mean, sem = refs
+    copy = pltpu.make_async_copy(weight.at[0, :, pl.ds(start, out.shape[1])], out, sem)
+    copy.start()
+    done[...] = gates[0:8, :]
+    rows, width = tok.shape
+    id0, id1, inverse = (later(gates, i, rows) for i in (2, 3, 4))
+    x = tok[...].astype(jnp.float32)
+    line = jnp.zeros((rows, width), jnp.float32)
+    for e in range(router.shape[0]):
+        sign = jnp.where(id0 == e, 1.0, 0.0) - jnp.where(id1 == e, 1.0, 0.0)
+        line = line + sign * router[e : e + 1, :].astype(jnp.float32)
+    scaled = gain[...] * inverse
+    weighted = gain[...] * x
+    scale[...] = scaled
+    along[...] = x * inverse * inverse * inverse
+    share[...] = weighted
+    fixed[...] = line * scaled
+    total = jnp.mean(line * weighted, axis=1, keepdims=True)
+    mean[...] = jnp.broadcast_to(total, mean.shape)
+    copy.wait()
+
+
 def load_kernel(start, after, weight, out, done, sem):
     copy = pltpu.make_async_copy(weight.at[0, :, pl.ds(start, out.shape[1])], out, sem)
     copy.start()
@@ -232,22 +264,17 @@
             out[:, at] = spread[k * PAD : (k + 1) * PAD].astype(jnp.bfloat16)
 
 
-def finish_kernel(ids, tok, grad, gain, router, gates, *refs):
+def finish_kernel(grad, gates, scale, along, share, fixed, fixed_mean, *refs):
     replies, (mixed, grad_tokens) = refs[:-2], refs[-2:]
-    rows, width = tok.shape
-    experts = router.shape[0]
+    rows, width = grad.shape
     pieces, tail, head = layout(rows, width)
     me = lax.axis_index("expert")
-    x = tok[...].astype(jnp.float32)
-    g = grad[...].astype(jnp.float32)
-    inverse = lax.rsqrt(jnp.mean(x * x, axis=1, keepdims=True) + 1e-06)
-    id0, id1 = column(ids, 0, rows)[:, 0:1], column(ids, 1, rows)[:, 0:1]
-    gate0, gate1 = gates[0:rows, 0:1], gates[PAD : PAD + rows, 0:1]
+    gate0, gate1, id0, id1 = (later(gates, i, rows) for i in range(4))
     chosen0 = jnp.zeros((rows, width), jnp.float32)
     chosen1 = jnp.zeros((rows, width), jnp.float32)
     back = jnp.zeros((PAD, head), jnp.float32)
     for k, reply in enumerate(replies):
-        expert = me ^ k
+        expert = (me ^ k).astype(jnp.float32)
         answer = reply[...].astype(jnp.float32)
         chosen0 = jnp.where(id0 == expert, answer[:rows, :width], chosen0)
         chosen1 = jnp.where(id1 == expert, answer[:rows, :width], chosen1)
@@ -258,16 +285,12 @@
         rest.append(back[rows + r // pieces : rows + r // pieces + 1, p * tail : (p + 1) * tail])
     back = jnp.concatenate([back[:rows, width:], jnp.concatenate(rest, axis=0)], axis=1)
     mixed[...] = (gate0 * chosen0 + gate1 * chosen1).astype(jnp.bfloat16)
-    grad0 = jnp.sum(g * chosen0, axis=1, keepdims=True)
-    grad1 = jnp.sum(g * chosen1, axis=1, keepdims=True)
-    spread = gate0 * gate1 * (grad0 - grad1)
-    for e in range(experts):
-        line = router[e : e + 1, :].astype(jnp.float32)
-        weight = jnp.where(id0 == e, spread, 0.0) - jnp.where(id1 == e, spread, 0.0)
-        back = back + weight * line
-    upstream = back * gain[...]
-    mean = jnp.mean(upstream * x, axis=1, keepdims=True)
-    grad_tokens[...] = (inverse * (upstream - x * inverse * inverse * mean)).astype(jnp.bfloat16)
+    g = grad[...].astype(jnp.float32)
+    spread = gate0 * gate1 * jnp.sum(g * (chosen0 - chosen1), axis=1, keepdims=True)
+    mean = jnp.mean(back * share[...], axis=1, keepdims=True) + spread * fixed_mean[:, 0:1]
+    grad_tokens[...] = (
+        back * scale[...] + spread * fixed[...] - along[...] * mean
+    ).astype(jnp.bfloat16)
 
 
 def near(array):
@@ -305,31 +328,39 @@
     ids, slots, kept = expert_ids.T, bin_slots.T, kept_mask.T
     gain, lines = norm_gain.reshape(1, width), router.T
 
-    *messages, gates = call(
+    *messages, gates, tokens, grad_out, gain, lines = call(
         pack_kernel,
         [pltpu.VMEM((PAD, head + LANES), bf16)] * experts
-        + [pltpu.VMEM((2 * PAD, LANES), f32)],
+        + [pltpu.VMEM((5 * PAD, LANES), f32)]
+        + [pltpu.VMEM(a.shape, a.dtype) for a in (tokens, grad_out, gain, lines)],
         [SM] * 3 + [VM] * 4,
         (ids, slots, kept, tokens, grad_out, gain, lines),
         limit=None,
     )
     arrived = [messages[0]] + [swap(messages[k], "expert", k) for k in range(1, experts)]
 
-    def load(start, stop, after):
+    def load(body, start, stop, given, more):
         return pl.pallas_call(
-            functools.partial(load_kernel, start),
-            out_shape=[pltpu.VMEM((width, stop - start), bf16), pltpu.VMEM((8, LANES), f32)],
-            in_specs=[VM, FAR],
-            out_specs=[VM, VM],
+            functools.partial(body, start),
+            out_shape=[pltpu.VMEM((width, stop - start), bf16), pltpu.VMEM((8, LANES), f32)]
+            + more,
+            in_specs=[VM] * len(given) + [FAR],
+            out_specs=[VM] * (2 + len(more)),
             scratch_shapes=[pltpu.SemaphoreType.DMA],
             compiler_params=pltpu.CompilerParams(vmem_limit_bytes=2**20),
             cost_estimate=pl.CostEstimate(
                 flops=0, bytes_accessed=width * (stop - start) * 4, transcendentals=0
             ),
-        )(after, far(up_weight))
+        )(*[near(a) for a in given], far(up_weight))
 
     early = max(STEP, hidden * 5 // 8 // STEP * STEP)
-    up_a, done = load(0, early, near(gates))
+    up_a, done, *factors = load(
+        prepare_kernel,
+        0,
+        early,
+        (gates, tokens, gain, lines),
+        [pltpu.VMEM((rows, width), f32)] * 4 + [pltpu.VMEM((rows, LANES), f32)],
+    )
 
     own, placed = call(
         functools.partial(bin_kernel, rows, width),
@@ -337,7 +368,7 @@
         [VM] * (1 + experts),
         [near(a) for a in (done, *arrived)],
     )
-    up_b, done = load(early, hidden, near(placed))
+    up_b, done = load(load_kernel, early, hidden, (placed,), [])
 
     mask = groups // 2
     far_rows = call(
@@ -402,8 +433,8 @@
     mixed, grad_tokens = call(
         finish_kernel,
         [result, result],
-        [SM] + [VM] * (5 + experts),
-        (ids, tokens, grad_out, gain, lines, near(gates), *[near(a) for a in answers]),
+        [VM] * (7 + experts),
+        [near(a) for a in (grad_out, gates, *factors, *answers)],
     )
     return mixed, grad_tokens
 

time: 60.6 us -> 59.9 us (0.988)
    pallas_call x5, Pallas kernels: 3.5 us -> 2.84 us  [call(): pl.pallas_call(body, out_shape=out_shape, in_specs=in_specs, out_specs=[V...]
where the time goes in v5:
time: 59.9 us; the launch traced here: 59.6 us
  Pallas kernels  30.3 us (51%)
  waiting for transfers between devices  14.6 us (24%)
  starting transfers between devices  14 us (23%)
  between operations  0.71 us (1%)
    pallas_call x1, Pallas kernels, shards(): pl.pallas_call(functools.partial(expert_kernel, groups), out_shape=[pltpu...  18.2 us
    ppermute x12, waiting for transfers between devices, swap(): return lax.ppermute(array, axis, [(i, i ^ mask) for i in range(n)])  14.6 us
    ppermute x12, starting transfers between devices, swap(): return lax.ppermute(array, axis, [(i, i ^ mask) for i in range(n)])  14 us
    pallas_call x2, Pallas kernels, load(): pl.pallas_call(functools.partial(body, start), out_shape=[pltpu.VMEM((wid...  9.2 us
    pallas_call x5, Pallas kernels, call(): pl.pallas_call(body, out_shape=out_shape, in_specs=in_specs, out_specs=[V...  2.84 us
  transfers between devices with their start and end apart: 12, of which 8 were waited for; matrix products, arithmetic and copies ran while one was open for 0% of the time, Pallas kernels for 15%

profile of v5, /device:TPU:0, one launch (start us, length us, event | category | flops | bytes accessed | tf_op | source)
XLA Modules:
  0.0 59.6 jit_solution(13375465994194788854)
XLA Ops:
  0.6 1.3 %shard_map.104 = (bf16[8,4736]{1,0:T(8,128)(2,1)S(1)}, bf16[8,4736]{1,0:T(8,128)(2,1)S(1)}, bf16[8,4736]{1,0:T(8,128)(2,1)S(1)}, bf16[8,4736]{1,0:T(8,128)(2,1)S...) custom-call(s32[2,6]{1,0:T(2,128)} %bitcast.7, ...), custom_call_target="tpu_custom_call" | custom-call | tf_op jit(solution)/shard_map/pallas_call | solution.py:305
  1.9 3.1 %collective-permute-start = (bf16[8,4736]{1,0:T(8,128)(2,1)S(1)}, bf16[8,4736]{1,0:T(8,128)(2,1)S(1)}, u32[]{:S(2)}, u32[]{:S(2)}) collective-permute-start(bf16[8,4736]{1,0:T(8,128)(2,1)S(1)} %get-tuple-element.42), channel_id=1, source_target_pairs={{0,4},{4,0},{8,12},{12,8},{1,5},{5,1},{9,13},{13,9},{2,6},{6,2},{1... | collective-permute-start | bytes 227336 | tf_op jit(solution)/shard_map/ppermute | solution.py:326
  5.0 2.6 %collective-permute-start.1 = (bf16[8,4736]{1,0:T(8,128)(2,1)S(1)}, bf16[8,4736]{1,0:T(8,128)(2,1)S(1)}, u32[]{:S(2)}, u32[]{:S(2)}) collective-permute-start(bf16[8,4736]{1,0:T(8,128)(2,1)S(1)} %get-tuple-element.43), channel_id=1, source_target_pairs={{0,8},{4,12},{8,0},{12,4},{1,9},{5,13},{9,1},{13,5},{2,10},{6,14},... | collective-permute-start | bytes 227336 | tf_op jit(solution)/shard_map/ppermute | solution.py:326
  7.6 5.5 %shard_map.105 = (bf16[3072,2560]{1,0:T(8,128)(2,1)S(1)}, f32[8,128]{1,0:T(8,128)S(1)}, f32[6,3072]{1,0:T(8,128)S(1)}, f32[6,3072]{1,0:T(8,128)S(1)}, f32[6,3072...) custom-call(f32[40,128]{1,0:T(8,128)S(1)} %get-tuple-element.31.gates, ...), custom_call_target="tpu_custom_call" | custom-call | bytes 31457280 | tf_op jit(solution)/shard_map/pallas_call | solution.py:343
  13.1 0.7 %collective-permute-done.2.refs_3_ = bf16[8,4736]{1,0:T(8,128)(2,1)S(1)} collective-permute-done((bf16[8,4736]{1,0:T(8,128)(2,1)S(1)}, bf16[8,4736]{1,0:T(8,128)(2,1)S(1)}, u32[]{:S(2)}, u32[]{:S(2)}) %collective-permute-start.2) | collective-permute-done | bytes 75808 | tf_op jit(solution)/shard_map/ppermute | solution.py:326
  13.9 0.3 shard_map.106
  14.1 1.6 %collective-permute-start.4 = (bf16[32,3072]{1,0:T(8,128)(2,1)S(1)}, bf16[32,3072]{1,0:T(8,128)(2,1)S(1)}, u32[]{:S(2)}, u32[]{:S(2)}) collective-permute-start(bf16[32,3072]{1,0:T(8,128)(2,1)S(1)} %get-tuple-element.45.refs_0_), channel_id=1, source_target_pairs={{0,2},{1,3},{2,0},{3,1},{4,6},{5,7},{6,4},{7,5},{8,10},{9,11},{10,... | collective-permute-start | bytes 589832 | tf_op jit(solution)/shard_map/ppermute | solution.py:326
  15.7 3.7 %shard_map.107 = (bf16[3072,1536]{1,0:T(8,128)(2,1)S(1)}, f32[8,128]{1,0:T(8,128)S(1)}) custom-call(f32[32,128]{1,0:T(8,128)S(1)} %get-tuple-element.46.after.refs_3_, bf16[1,3072,4096]{2,1,0:T(8,128)(2,1)} %weight.3), custom_call_target="tpu_custom_call" | custom-call | bytes 18874368 | tf_op jit(solution)/shard_map/pallas_call | solution.py:343
  19.4 0.5 collective-permute-done.4.rows
  20.0 1.4 %collective-permute-done.5.refs_3_ = bf16[32,3072]{1,0:T(8,128)(2,1)S(1)} collective-permute-done((bf16[32,3072]{1,0:T(8,128)(2,1)S(1)}, bf16[32,3072]{1,0:T(8,128)(2,1)S(1)}, u32[]{:S(2)}, u32[]{:S(2)}) %collective-permute-start.5) | collective-permute-done | bytes 196640 | tf_op jit(solution)/shard_map/ppermute | solution.py:326
  21.4 18.2 %shard_map.109 = (bf16[3072,2560]{1,0:T(8,128)(2,1)S(1)}, bf16[3072,1536]{1,0:T(8,128)(2,1)S(1)}, bf16[32,3072]{1,0:T(8,128)(2,1)S(1)}, bf16[32,3072]{1,0:T(8,12...) custom-call(bf16[32,3072]{1,0:T(8,128)(2,1)S(1)} %get-tuple-element., ...), custom_call_target="tpu_custom_call", output_to_operand_aliasing={{0}: (4, {}), {1}: (5, {})} | custom-call | tf_op jit(solution)/shard_map/pallas_call | solution.py:388
  39.7 0.2 collective-permute-start.7
  39.8 0.4 collective-permute-start.6
  40.2 0.9 %collective-permute-done.7 = bf16[32,3072]{1,0:T(8,128)(2,1)S(1)} collective-permute-done((bf16[32,3072]{1,0:T(8,128)(2,1)S(1)}, bf16[32,3072]{1,0:T(8,128)(2,1)S(1)}, u32[]{:S(2)}, u32[]{:S(2)}) %collective-permute-start.7) | collective-permute-done | bytes 196640 | tf_op jit(solution)/shard_map/ppermute | solution.py:326
  41.2 1.6 %collective-permute-start.8 = (bf16[32,3072]{1,0:T(8,128)(2,1)S(1)}, bf16[32,3072]{1,0:T(8,128)(2,1)S(1)}, u32[]{:S(2)}, u32[]{:S(2)}) collective-permute-start(bf16[32,3072]{1,0:T(8,128)(2,1)S(1)} %add_convert_fusion), channel_id=1, source_target_pairs={{0,2},{1,3},{2,0},{3,1},{4,6},{5,7},{6,4},{7,5},{8,10},{9,11},{10,... | collective-permute-start | bytes 589832 | tf_op jit(solution)/shard_map/ppermute | solution.py:326
  42.8 5.4 %collective-permute-done.8.refs_2_ = bf16[32,3072]{1,0:T(8,128)(2,1)S(1)} collective-permute-done((bf16[32,3072]{1,0:T(8,128)(2,1)S(1)}, bf16[32,3072]{1,0:T(8,128)(2,1)S(1)}, u32[]{:S(2)}, u32[]{:S(2)}) %collective-permute-start.8) | collective-permute-done | bytes 196640 | tf_op jit(solution)/shard_map/ppermute | solution.py:326
  48.2 0.4 shard_map.110
  48.6 1.3 %collective-permute-start.9 = (bf16[8,4608]{1,0:T(8,128)(2,1)S(1)}, bf16[8,4608]{1,0:T(8,128)(2,1)S(1)}, u32[]{:S(2)}, u32[]{:S(2)}) collective-permute-start(bf16[8,4608]{1,0:T(8,128)(2,1)S(1)} %get-tuple-element.55), channel_id=1, source_target_pairs={{0,4},{4,0},{8,12},{12,8},{1,5},{5,1},{9,13},{13,9},{2,6},{6,2},{1... | collective-permute-start | bytes 221192 | tf_op jit(solution)/shard_map/ppermute | solution.py:326
  49.9 2.5 %collective-permute-start.10 = (bf16[8,4608]{1,0:T(8,128)(2,1)S(1)}, bf16[8,4608]{1,0:T(8,128)(2,1)S(1)}, u32[]{:S(2)}, u32[]{:S(2)}) collective-permute-start(bf16[8,4608]{1,0:T(8,128)(2,1)S(1)} %get-tuple-element.56), channel_id=1, source_target_pairs={{0,8},{4,12},{8,0},{12,4},{1,9},{5,13},{9,1},{13,5},{2,10},{6,14},... | collective-permute-start | bytes 221192 | tf_op jit(solution)/shard_map/ppermute | solution.py:326
  52.4 0.6 %collective-permute-start.11 = (bf16[8,4608]{1,0:T(8,128)(2,1)S(1)}, bf16[8,4608]{1,0:T(8,128)(2,1)S(1)}, u32[]{:S(2)}, u32[]{:S(2)}) collective-permute-start(bf16[8,4608]{1,0:T(8,128)(2,1)S(1)} %get-tuple-element.57), channel_id=1, source_target_pairs={{0,12},{4,8},{8,4},{12,0},{1,13},{5,9},{9,5},{13,1},{2,14},{6,10},... | collective-permute-start | bytes 221192 | tf_op jit(solution)/shard_map/ppermute | solution.py:326
  53.0 0.7 %collective-permute-done.9.refs_1_ = bf16[8,4608]{1,0:T(8,128)(2,1)S(1)} collective-permute-done((bf16[8,4608]{1,0:T(8,128)(2,1)S(1)}, bf16[8,4608]{1,0:T(8,128)(2,1)S(1)}, u32[]{:S(2)}, u32[]{:S(2)}) %collective-permute-start.9) | collective-permute-done | bytes 73760 | tf_op jit(solution)/shard_map/ppermute | solution.py:326
  53.7 3.5 %collective-permute-done.10.refs_2_ = bf16[8,4608]{1,0:T(8,128)(2,1)S(1)} collective-permute-done((bf16[8,4608]{1,0:T(8,128)(2,1)S(1)}, bf16[8,4608]{1,0:T(8,128)(2,1)S(1)}, u32[]{:S(2)}, u32[]{:S(2)}) %collective-permute-start.10) | collective-permute-done | bytes 73760 | tf_op jit(solution)/shard_map/ppermute | solution.py:326
  57.2 1.5 %collective-permute-done.11.refs_3_ = bf16[8,4608]{1,0:T(8,128)(2,1)S(1)} collective-permute-done((bf16[8,4608]{1,0:T(8,128)(2,1)S(1)}, bf16[8,4608]{1,0:T(8,128)(2,1)S(1)}, u32[]{:S(2)}, u32[]{:S(2)}) %collective-permute-start.11) | collective-permute-done | bytes 73760 | tf_op jit(solution)/shard_map/ppermute | solution.py:326
  58.7 0.9 %shard_map.111 = (bf16[6,3072]{1,0:T(8,128)(2,1)}, bf16[6,3072]{1,0:T(8,128)(2,1)}) custom-call(bf16[6,3072]{1,0:T(8,128)(2,1)S(1)} %get-tuple-element.30.grad, f32[40,128]{1,0:T(8,128)S(1)} %get-tuple-element.31.gates, f32[6,3072]{1,0:T(8,128)S(1)} %get-tuple-element.35.scale, f32[6,3072]{1,0:T(8,128)S(1)} %get-tuple-element.36.along, ...), custom_call_target="tpu_custom_call" | custom-call | tf_op jit(solution)/shard_map/pallas_call | solution.py:305
  (9 shorter events, 0.2 us)
Async XLA Ops:
  1.9 11.2 %collective-permute-start = (bf16[8,4736]{1,0:T(8,128)(2,1)S(1)}, bf16[8,4736]{1,0:T(8,128)(2,1)S(1)}, u32[]{:S(2)}, u32[]{:S(2)}) collective-permute-start(bf16[8,4736]{1,0:T(8,128)(2,1)S(1)} %get-tuple-element.42), channel_id=1, source_target_pairs={{0,4},{4,0},{8,12},{12,8},{1,5},{5,1},{9,13},{13,9},{2,6},{6,2},{1... | collective-permute-start | bytes 227336 | tf_op jit(solution)/shard_map/ppermute | solution.py:326
  5.0 8.1 %collective-permute-start.1 = (bf16[8,4736]{1,0:T(8,128)(2,1)S(1)}, bf16[8,4736]{1,0:T(8,128)(2,1)S(1)}, u32[]{:S(2)}, u32[]{:S(2)}) collective-permute-start(bf16[8,4736]{1,0:T(8,128)(2,1)S(1)} %get-tuple-element.43), channel_id=1, source_target_pairs={{0,8},{4,12},{8,0},{12,4},{1,9},{5,13},{9,1},{13,5},{2,10},{6,14},... | collective-permute-start | bytes 227336 | tf_op jit(solution)/shard_map/ppermute | solution.py:326
  7.6 6.3 %collective-permute-start.2 = (bf16[8,4736]{1,0:T(8,128)(2,1)S(1)}, bf16[8,4736]{1,0:T(8,128)(2,1)S(1)}, u32[]{:S(2)}, u32[]{:S(2)}) collective-permute-start(bf16[8,4736]{1,0:T(8,128)(2,1)S(1)} %get-tuple-element.44), channel_id=1, source_target_pairs={{0,12},{4,8},{8,4},{12,0},{1,13},{5,9},{9,5},{13,1},{2,14},{6,10},... | collective-permute-start | bytes 227336 | tf_op jit(solution)/shard_map/ppermute | solution.py:326
  14.1 5.7 %collective-permute-start.4 = (bf16[32,3072]{1,0:T(8,128)(2,1)S(1)}, bf16[32,3072]{1,0:T(8,128)(2,1)S(1)}, u32[]{:S(2)}, u32[]{:S(2)}) collective-permute-start(bf16[32,3072]{1,0:T(8,128)(2,1)S(1)} %get-tuple-element.45.refs_0_), channel_id=1, source_target_pairs={{0,2},{1,3},{2,0},{3,1},{4,6},{5,7},{6,4},{7,5},{8,10},{9,11},{10,... | collective-permute-start | bytes 589832 | tf_op jit(solution)/shard_map/ppermute | solution.py:326
  15.7 4.3 %collective-permute-start.3 = (bf16[32,3072]{1,0:T(8,128)(2,1)S(1)}, bf16[32,3072]{1,0:T(8,128)(2,1)S(1)}, u32[]{:S(2)}, u32[]{:S(2)}) collective-permute-start(bf16[32,3072]{1,0:T(8,128)(2,1)S(1)} %get-tuple-element.45.refs_0_), channel_id=1, source_target_pairs={{0,1},{1,0},{2,3},{3,2},{4,5},{5,4},{6,7},{7,6},{8,9},{9,8},{10,11... | collective-permute-start | bytes 589832 | tf_op jit(solution)/shard_map/ppermute | solution.py:326
  19.9 1.5 %collective-permute-start.5 = (bf16[32,3072]{1,0:T(8,128)(2,1)S(1)}, bf16[32,3072]{1,0:T(8,128)(2,1)S(1)}, u32[]{:S(2)}, u32[]{:S(2)}) collective-permute-start(bf16[32,3072]{1,0:T(8,128)(2,1)S(1)} %shard_map.108.refs_2_), channel_id=1, source_target_pairs={{0,1},{1,0},{2,3},{3,2},{4,5},{5,4},{6,7},{7,6},{8,9},{9,8},{10,11... | collective-permute-start | bytes 589832 | tf_op jit(solution)/shard_map/ppermute | solution.py:326
  39.7 1.5 %collective-permute-start.7 = (bf16[32,3072]{1,0:T(8,128)(2,1)S(1)}, bf16[32,3072]{1,0:T(8,128)(2,1)S(1)}, u32[]{:S(2)}, u32[]{:S(2)}) collective-permute-start(bf16[32,3072]{1,0:T(8,128)(2,1)S(1)} %get-tuple-element.53), channel_id=1, source_target_pairs={{0,1},{1,0},{2,3},{3,2},{4,5},{5,4},{6,7},{7,6},{8,9},{9,8},{10,11... | collective-permute-start | bytes 589832 | tf_op jit(solution)/shard_map/ppermute | solution.py:326
  39.8 2.9 %collective-permute-start.6 = (bf16[32,3072]{1,0:T(8,128)(2,1)S(1)}, bf16[32,3072]{1,0:T(8,128)(2,1)S(1)}, u32[]{:S(2)}, u32[]{:S(2)}) collective-permute-start(bf16[32,3072]{1,0:T(8,128)(2,1)S(1)} %get-tuple-element.51), channel_id=1, source_target_pairs={{0,1},{1,0},{2,3},{3,2},{4,5},{5,4},{6,7},{7,6},{8,9},{9,8},{10,11... | collective-permute-start | bytes 589832 | tf_op jit(solution)/shard_map/ppermute | solution.py:326
  41.2 7.0 %collective-permute-start.8 = (bf16[32,3072]{1,0:T(8,128)(2,1)S(1)}, bf16[32,3072]{1,0:T(8,128)(2,1)S(1)}, u32[]{:S(2)}, u32[]{:S(2)}) collective-permute-start(bf16[32,3072]{1,0:T(8,128)(2,1)S(1)} %add_convert_fusion), channel_id=1, source_target_pairs={{0,2},{1,3},{2,0},{3,1},{4,6},{5,7},{6,4},{7,5},{8,10},{9,11},{10,... | collective-permute-start | bytes 589832 | tf_op jit(solution)/shard_map/ppermute | solution.py:326
  48.6 5.1 %collective-permute-start.9 = (bf16[8,4608]{1,0:T(8,128)(2,1)S(1)}, bf16[8,4608]{1,0:T(8,128)(2,1)S(1)}, u32[]{:S(2)}, u32[]{:S(2)}) collective-permute-start(bf16[8,4608]{1,0:T(8,128)(2,1)S(1)} %get-tuple-element.55), channel_id=1, source_target_pairs={{0,4},{4,0},{8,12},{12,8},{1,5},{5,1},{9,13},{13,9},{2,6},{6,2},{1... | collective-permute-start | bytes 221192 | tf_op jit(solution)/shard_map/ppermute | solution.py:326
  49.9 7.3 %collective-permute-start.10 = (bf16[8,4608]{1,0:T(8,128)(2,1)S(1)}, bf16[8,4608]{1,0:T(8,128)(2,1)S(1)}, u32[]{:S(2)}, u32[]{:S(2)}) collective-permute-start(bf16[8,4608]{1,0:T(8,128)(2,1)S(1)} %get-tuple-element.56), channel_id=1, source_target_pairs={{0,8},{4,12},{8,0},{12,4},{1,9},{5,13},{9,1},{13,5},{2,10},{6,14},... | collective-permute-start | bytes 221192 | tf_op jit(solution)/shard_map/ppermute | solution.py:326
  52.4 6.3 %collective-permute-start.11 = (bf16[8,4608]{1,0:T(8,128)(2,1)S(1)}, bf16[8,4608]{1,0:T(8,128)(2,1)S(1)}, u32[]{:S(2)}, u32[]{:S(2)}) collective-permute-start(bf16[8,4608]{1,0:T(8,128)(2,1)S(1)} %get-tuple-element.57), channel_id=1, source_target_pairs={{0,12},{4,8},{8,4},{12,0},{1,13},{5,9},{9,5},{13,1},{2,14},{6,10},... | collective-permute-start | bytes 221192 | tf_op jit(solution)/shard_map/ppermute | solution.py:326

commit v6 on v5

--- a/solution.py
+++ b/solution.py
@@ -209,11 +209,11 @@
         def _(i=i):
             fetch(i).wait()
             for d in range(edges[i], edges[i + 1], STEP):
+                turn(share)
                 total = lax.dot_general(
                     down[d : d + STEP, :], active[...], over, preferred_element_type=jnp.float32
                 )
                 deliver(total.T.astype(jnp.bfloat16), slice(d, d + STEP), 0)
-                turn(share)
 
     @pl.when(taken)
     def _():

time: 59.9 us -> 59.9 us (level)
  no operation moved by 1% of the time
where the time goes in v6:
time: 59.9 us; the launch traced here: 59.6 us
  Pallas kernels  30.3 us (51%)
  waiting for transfers between devices  14.6 us (24%)
  starting transfers between devices  14 us (23%)
  between operations  0.71 us (1%)
    pallas_call x1, Pallas kernels, shards(): pl.pallas_call(functools.partial(expert_kernel, groups), out_shape=[pltpu...  18.2 us
    ppermute x12, waiting for transfers between devices, swap(): return lax.ppermute(array, axis, [(i, i ^ mask) for i in range(n)])  14.6 us
    ppermute x12, starting transfers between devices, swap(): return lax.ppermute(array, axis, [(i, i ^ mask) for i in range(n)])  14 us
    pallas_call x2, Pallas kernels, load(): pl.pallas_call(functools.partial(body, start), out_shape=[pltpu.VMEM((wid...  9.2 us
    pallas_call x5, Pallas kernels, call(): pl.pallas_call(body, out_shape=out_shape, in_specs=in_specs, out_specs=[V...  2.84 us
  transfers between devices with their start and end apart: 12, of which 8 were waited for; matrix products, arithmetic and copies ran while one was open for 0% of the time, Pallas kernels for 15%

profile of v6, /device:TPU:0, one launch (start us, length us, event | category | flops | bytes accessed | tf_op | source)
XLA Modules:
  0.0 59.6 jit_solution(14308683473541859539)
XLA Ops:
  0.6 1.3 %shard_map.104 = (bf16[8,4736]{1,0:T(8,128)(2,1)S(1)}, bf16[8,4736]{1,0:T(8,128)(2,1)S(1)}, bf16[8,4736]{1,0:T(8,128)(2,1)S(1)}, bf16[8,4736]{1,0:T(8,128)(2,1)S...) custom-call(s32[2,6]{1,0:T(2,128)} %bitcast.7, ...), custom_call_target="tpu_custom_call" | custom-call | tf_op jit(solution)/shard_map/pallas_call | solution.py:305
  1.9 3.1 %collective-permute-start = (bf16[8,4736]{1,0:T(8,128)(2,1)S(1)}, bf16[8,4736]{1,0:T(8,128)(2,1)S(1)}, u32[]{:S(2)}, u32[]{:S(2)}) collective-permute-start(bf16[8,4736]{1,0:T(8,128)(2,1)S(1)} %get-tuple-element.42), channel_id=1, source_target_pairs={{0,4},{4,0},{8,12},{12,8},{1,5},{5,1},{9,13},{13,9},{2,6},{6,2},{1... | collective-permute-start | bytes 227336 | tf_op jit(solution)/shard_map/ppermute | solution.py:326
  5.0 2.6 %collective-permute-start.1 = (bf16[8,4736]{1,0:T(8,128)(2,1)S(1)}, bf16[8,4736]{1,0:T(8,128)(2,1)S(1)}, u32[]{:S(2)}, u32[]{:S(2)}) collective-permute-start(bf16[8,4736]{1,0:T(8,128)(2,1)S(1)} %get-tuple-element.43), channel_id=1, source_target_pairs={{0,8},{4,12},{8,0},{12,4},{1,9},{5,13},{9,1},{13,5},{2,10},{6,14},... | collective-permute-start | bytes 227336 | tf_op jit(solution)/shard_map/ppermute | solution.py:326
  7.6 5.5 %shard_map.105 = (bf16[3072,2560]{1,0:T(8,128)(2,1)S(1)}, f32[8,128]{1,0:T(8,128)S(1)}, f32[6,3072]{1,0:T(8,128)S(1)}, f32[6,3072]{1,0:T(8,128)S(1)}, f32[6,3072...) custom-call(f32[40,128]{1,0:T(8,128)S(1)} %get-tuple-element.31.gates, ...), custom_call_target="tpu_custom_call" | custom-call | bytes 31457280 | tf_op jit(solution)/shard_map/pallas_call | solution.py:343
  13.1 0.7 %collective-permute-done.2.refs_3_ = bf16[8,4736]{1,0:T(8,128)(2,1)S(1)} collective-permute-done((bf16[8,4736]{1,0:T(8,128)(2,1)S(1)}, bf16[8,4736]{1,0:T(8,128)(2,1)S(1)}, u32[]{:S(2)}, u32[]{:S(2)}) %collective-permute-start.2) | collective-permute-done | bytes 75808 | tf_op jit(solution)/shard_map/ppermute | solution.py:326
  13.9 0.3 shard_map.106
  14.1 1.6 %collective-permute-start.4 = (bf16[32,3072]{1,0:T(8,128)(2,1)S(1)}, bf16[32,3072]{1,0:T(8,128)(2,1)S(1)}, u32[]{:S(2)}, u32[]{:S(2)}) collective-permute-start(bf16[32,3072]{1,0:T(8,128)(2,1)S(1)} %get-tuple-element.45.refs_0_), channel_id=1, source_target_pairs={{0,2},{1,3},{2,0},{3,1},{4,6},{5,7},{6,4},{7,5},{8,10},{9,11},{10,... | collective-permute-start | bytes 589832 | tf_op jit(solution)/shard_map/ppermute | solution.py:326
  15.7 3.7 %shard_map.107 = (bf16[3072,1536]{1,0:T(8,128)(2,1)S(1)}, f32[8,128]{1,0:T(8,128)S(1)}) custom-call(f32[32,128]{1,0:T(8,128)S(1)} %get-tuple-element.46.after.refs_3_, bf16[1,3072,4096]{2,1,0:T(8,128)(2,1)} %weight.3), custom_call_target="tpu_custom_call" | custom-call | bytes 18874368 | tf_op jit(solution)/shard_map/pallas_call | solution.py:343
  19.4 0.5 collective-permute-done.4.rows
  20.0 1.4 %collective-permute-done.5.refs_3_ = bf16[32,3072]{1,0:T(8,128)(2,1)S(1)} collective-permute-done((bf16[32,3072]{1,0:T(8,128)(2,1)S(1)}, bf16[32,3072]{1,0:T(8,128)(2,1)S(1)}, u32[]{:S(2)}, u32[]{:S(2)}) %collective-permute-start.5) | collective-permute-done | bytes 196640 | tf_op jit(solution)/shard_map/ppermute | solution.py:326
  21.4 18.2 %shard_map.109 = (bf16[3072,2560]{1,0:T(8,128)(2,1)S(1)}, bf16[3072,1536]{1,0:T(8,128)(2,1)S(1)}, bf16[32,3072]{1,0:T(8,128)(2,1)S(1)}, bf16[32,3072]{1,0:T(8,12...) custom-call(bf16[32,3072]{1,0:T(8,128)(2,1)S(1)} %get-tuple-element., ...), custom_call_target="tpu_custom_call", output_to_operand_aliasing={{0}: (4, {}), {1}: (5, {})} | custom-call | tf_op jit(solution)/shard_map/pallas_call | solution.py:388
  39.7 0.2 collective-permute-start.7
  39.8 0.4 collective-permute-start.6
  40.2 0.9 %collective-permute-done.7 = bf16[32,3072]{1,0:T(8,128)(2,1)S(1)} collective-permute-done((bf16[32,3072]{1,0:T(8,128)(2,1)S(1)}, bf16[32,3072]{1,0:T(8,128)(2,1)S(1)}, u32[]{:S(2)}, u32[]{:S(2)}) %collective-permute-start.7) | collective-permute-done | bytes 196640 | tf_op jit(solution)/shard_map/ppermute | solution.py:326
  41.2 1.6 %collective-permute-start.8 = (bf16[32,3072]{1,0:T(8,128)(2,1)S(1)}, bf16[32,3072]{1,0:T(8,128)(2,1)S(1)}, u32[]{:S(2)}, u32[]{:S(2)}) collective-permute-start(bf16[32,3072]{1,0:T(8,128)(2,1)S(1)} %add_convert_fusion), channel_id=1, source_target_pairs={{0,2},{1,3},{2,0},{3,1},{4,6},{5,7},{6,4},{7,5},{8,10},{9,11},{10,... | collective-permute-start | bytes 589832 | tf_op jit(solution)/shard_map/ppermute | solution.py:326
  42.8 5.4 %collective-permute-done.8.refs_2_ = bf16[32,3072]{1,0:T(8,128)(2,1)S(1)} collective-permute-done((bf16[32,3072]{1,0:T(8,128)(2,1)S(1)}, bf16[32,3072]{1,0:T(8,128)(2,1)S(1)}, u32[]{:S(2)}, u32[]{:S(2)}) %collective-permute-start.8) | collective-permute-done | bytes 196640 | tf_op jit(solution)/shard_map/ppermute | solution.py:326
  48.2 0.4 shard_map.110
  48.6 1.3 %collective-permute-start.9 = (bf16[8,4608]{1,0:T(8,128)(2,1)S(1)}, bf16[8,4608]{1,0:T(8,128)(2,1)S(1)}, u32[]{:S(2)}, u32[]{:S(2)}) collective-permute-start(bf16[8,4608]{1,0:T(8,128)(2,1)S(1)} %get-tuple-element.55), channel_id=1, source_target_pairs={{0,4},{4,0},{8,12},{12,8},{1,5},{5,1},{9,13},{13,9},{2,6},{6,2},{1... | collective-permute-start | bytes 221192 | tf_op jit(solution)/shard_map/ppermute | solution.py:326
  49.9 2.5 %collective-permute-start.10 = (bf16[8,4608]{1,0:T(8,128)(2,1)S(1)}, bf16[8,4608]{1,0:T(8,128)(2,1)S(1)}, u32[]{:S(2)}, u32[]{:S(2)}) collective-permute-start(bf16[8,4608]{1,0:T(8,128)(2,1)S(1)} %get-tuple-element.56), channel_id=1, source_target_pairs={{0,8},{4,12},{8,0},{12,4},{1,9},{5,13},{9,1},{13,5},{2,10},{6,14},... | collective-permute-start | bytes 221192 | tf_op jit(solution)/shard_map/ppermute | solution.py:326
  52.4 0.6 %collective-permute-start.11 = (bf16[8,4608]{1,0:T(8,128)(2,1)S(1)}, bf16[8,4608]{1,0:T(8,128)(2,1)S(1)}, u32[]{:S(2)}, u32[]{:S(2)}) collective-permute-start(bf16[8,4608]{1,0:T(8,128)(2,1)S(1)} %get-tuple-element.57), channel_id=1, source_target_pairs={{0,12},{4,8},{8,4},{12,0},{1,13},{5,9},{9,5},{13,1},{2,14},{6,10},... | collective-permute-start | bytes 221192 | tf_op jit(solution)/shard_map/ppermute | solution.py:326
  53.0 0.7 %collective-permute-done.9.refs_1_ = bf16[8,4608]{1,0:T(8,128)(2,1)S(1)} collective-permute-done((bf16[8,4608]{1,0:T(8,128)(2,1)S(1)}, bf16[8,4608]{1,0:T(8,128)(2,1)S(1)}, u32[]{:S(2)}, u32[]{:S(2)}) %collective-permute-start.9) | collective-permute-done | bytes 73760 | tf_op jit(solution)/shard_map/ppermute | solution.py:326
  53.7 3.5 %collective-permute-done.10.refs_2_ = bf16[8,4608]{1,0:T(8,128)(2,1)S(1)} collective-permute-done((bf16[8,4608]{1,0:T(8,128)(2,1)S(1)}, bf16[8,4608]{1,0:T(8,128)(2,1)S(1)}, u32[]{:S(2)}, u32[]{:S(2)}) %collective-permute-start.10) | collective-permute-done | bytes 73760 | tf_op jit(solution)/shard_map/ppermute | solution.py:326
  57.2 1.5 %collective-permute-done.11.refs_3_ = bf16[8,4608]{1,0:T(8,128)(2,1)S(1)} collective-permute-done((bf16[8,4608]{1,0:T(8,128)(2,1)S(1)}, bf16[8,4608]{1,0:T(8,128)(2,1)S(1)}, u32[]{:S(2)}, u32[]{:S(2)}) %collective-permute-start.11) | collective-permute-done | bytes 73760 | tf_op jit(solution)/shard_map/ppermute | solution.py:326
  58.7 0.9 %shard_map.111 = (bf16[6,3072]{1,0:T(8,128)(2,1)}, bf16[6,3072]{1,0:T(8,128)(2,1)}) custom-call(bf16[6,3072]{1,0:T(8,128)(2,1)S(1)} %get-tuple-element.30.grad, f32[40,128]{1,0:T(8,128)S(1)} %get-tuple-element.31.gates, f32[6,3072]{1,0:T(8,128)S(1)} %get-tuple-element.35.scale, f32[6,3072]{1,0:T(8,128)S(1)} %get-tuple-element.36.along, ...), custom_call_target="tpu_custom_call" | custom-call | tf_op jit(solution)/shard_map/pallas_call | solution.py:305
  (9 shorter events, 0.2 us)
Async XLA Ops:
  1.9 11.2 %collective-permute-start = (bf16[8,4736]{1,0:T(8,128)(2,1)S(1)}, bf16[8,4736]{1,0:T(8,128)(2,1)S(1)}, u32[]{:S(2)}, u32[]{:S(2)}) collective-permute-start(bf16[8,4736]{1,0:T(8,128)(2,1)S(1)} %get-tuple-element.42), channel_id=1, source_target_pairs={{0,4},{4,0},{8,12},{12,8},{1,5},{5,1},{9,13},{13,9},{2,6},{6,2},{1... | collective-permute-start | bytes 227336 | tf_op jit(solution)/shard_map/ppermute | solution.py:326
  5.0 8.1 %collective-permute-start.1 = (bf16[8,4736]{1,0:T(8,128)(2,1)S(1)}, bf16[8,4736]{1,0:T(8,128)(2,1)S(1)}, u32[]{:S(2)}, u32[]{:S(2)}) collective-permute-start(bf16[8,4736]{1,0:T(8,128)(2,1)S(1)} %get-tuple-element.43), channel_id=1, source_target_pairs={{0,8},{4,12},{8,0},{12,4},{1,9},{5,13},{9,1},{13,5},{2,10},{6,14},... | collective-permute-start | bytes 227336 | tf_op jit(solution)/shard_map/ppermute | solution.py:326
  7.6 6.3 %collective-permute-start.2 = (bf16[8,4736]{1,0:T(8,128)(2,1)S(1)}, bf16[8,4736]{1,0:T(8,128)(2,1)S(1)}, u32[]{:S(2)}, u32[]{:S(2)}) collective-permute-start(bf16[8,4736]{1,0:T(8,128)(2,1)S(1)} %get-tuple-element.44), channel_id=1, source_target_pairs={{0,12},{4,8},{8,4},{12,0},{1,13},{5,9},{9,5},{13,1},{2,14},{6,10},... | collective-permute-start | bytes 227336 | tf_op jit(solution)/shard_map/ppermute | solution.py:326
  14.1 5.7 %collective-permute-start.4 = (bf16[32,3072]{1,0:T(8,128)(2,1)S(1)}, bf16[32,3072]{1,0:T(8,128)(2,1)S(1)}, u32[]{:S(2)}, u32[]{:S(2)}) collective-permute-start(bf16[32,3072]{1,0:T(8,128)(2,1)S(1)} %get-tuple-element.45.refs_0_), channel_id=1, source_target_pairs={{0,2},{1,3},{2,0},{3,1},{4,6},{5,7},{6,4},{7,5},{8,10},{9,11},{10,... | collective-permute-start | bytes 589832 | tf_op jit(solution)/shard_map/ppermute | solution.py:326
  15.7 4.3 %collective-permute-start.3 = (bf16[32,3072]{1,0:T(8,128)(2,1)S(1)}, bf16[32,3072]{1,0:T(8,128)(2,1)S(1)}, u32[]{:S(2)}, u32[]{:S(2)}) collective-permute-start(bf16[32,3072]{1,0:T(8,128)(2,1)S(1)} %get-tuple-element.45.refs_0_), channel_id=1, source_target_pairs={{0,1},{1,0},{2,3},{3,2},{4,5},{5,4},{6,7},{7,6},{8,9},{9,8},{10,11... | collective-permute-start | bytes 589832 | tf_op jit(solution)/shard_map/ppermute | solution.py:326
  19.9 1.5 %collective-permute-start.5 = (bf16[32,3072]{1,0:T(8,128)(2,1)S(1)}, bf16[32,3072]{1,0:T(8,128)(2,1)S(1)}, u32[]{:S(2)}, u32[]{:S(2)}) collective-permute-start(bf16[32,3072]{1,0:T(8,128)(2,1)S(1)} %shard_map.108.refs_2_), channel_id=1, source_target_pairs={{0,1},{1,0},{2,3},{3,2},{4,5},{5,4},{6,7},{7,6},{8,9},{9,8},{10,11... | collective-permute-start | bytes 589832 | tf_op jit(solution)/shard_map/ppermute | solution.py:326
  39.7 1.5 %collective-permute-start.7 = (bf16[32,3072]{1,0:T(8,128)(2,1)S(1)}, bf16[32,3072]{1,0:T(8,128)(2,1)S(1)}, u32[]{:S(2)}, u32[]{:S(2)}) collective-permute-start(bf16[32,3072]{1,0:T(8,128)(2,1)S(1)} %get-tuple-element.53), channel_id=1, source_target_pairs={{0,1},{1,0},{2,3},{3,2},{4,5},{5,4},{6,7},{7,6},{8,9},{9,8},{10,11... | collective-permute-start | bytes 589832 | tf_op jit(solution)/shard_map/ppermute | solution.py:326
  39.8 2.9 %collective-permute-start.6 = (bf16[32,3072]{1,0:T(8,128)(2,1)S(1)}, bf16[32,3072]{1,0:T(8,128)(2,1)S(1)}, u32[]{:S(2)}, u32[]{:S(2)}) collective-permute-start(bf16[32,3072]{1,0:T(8,128)(2,1)S(1)} %get-tuple-element.51), channel_id=1, source_target_pairs={{0,1},{1,0},{2,3},{3,2},{4,5},{5,4},{6,7},{7,6},{8,9},{9,8},{10,11... | collective-permute-start | bytes 589832 | tf_op jit(solution)/shard_map/ppermute | solution.py:326
  41.2 7.0 %collective-permute-start.8 = (bf16[32,3072]{1,0:T(8,128)(2,1)S(1)}, bf16[32,3072]{1,0:T(8,128)(2,1)S(1)}, u32[]{:S(2)}, u32[]{:S(2)}) collective-permute-start(bf16[32,3072]{1,0:T(8,128)(2,1)S(1)} %add_convert_fusion), channel_id=1, source_target_pairs={{0,2},{1,3},{2,0},{3,1},{4,6},{5,7},{6,4},{7,5},{8,10},{9,11},{10,... | collective-permute-start | bytes 589832 | tf_op jit(solution)/shard_map/ppermute | solution.py:326
  48.6 5.1 %collective-permute-start.9 = (bf16[8,4608]{1,0:T(8,128)(2,1)S(1)}, bf16[8,4608]{1,0:T(8,128)(2,1)S(1)}, u32[]{:S(2)}, u32[]{:S(2)}) collective-permute-start(bf16[8,4608]{1,0:T(8,128)(2,1)S(1)} %get-tuple-element.55), channel_id=1, source_target_pairs={{0,4},{4,0},{8,12},{12,8},{1,5},{5,1},{9,13},{13,9},{2,6},{6,2},{1... | collective-permute-start | bytes 221192 | tf_op jit(solution)/shard_map/ppermute | solution.py:326
  49.9 7.3 %collective-permute-start.10 = (bf16[8,4608]{1,0:T(8,128)(2,1)S(1)}, bf16[8,4608]{1,0:T(8,128)(2,1)S(1)}, u32[]{:S(2)}, u32[]{:S(2)}) collective-permute-start(bf16[8,4608]{1,0:T(8,128)(2,1)S(1)} %get-tuple-element.56), channel_id=1, source_target_pairs={{0,8},{4,12},{8,0},{12,4},{1,9},{5,13},{9,1},{13,5},{2,10},{6,14},... | collective-permute-start | bytes 221192 | tf_op jit(solution)/shard_map/ppermute | solution.py:326
  52.4 6.3 %collective-permute-start.11 = (bf16[8,4608]{1,0:T(8,128)(2,1)S(1)}, bf16[8,4608]{1,0:T(8,128)(2,1)S(1)}, u32[]{:S(2)}, u32[]{:S(2)}) collective-permute-start(bf16[8,4608]{1,0:T(8,128)(2,1)S(1)} %get-tuple-element.57), channel_id=1, source_target_pairs={{0,12},{4,8},{8,4},{12,0},{1,13},{5,9},{9,5},{13,1},{2,14},{6,10},... | collective-permute-start | bytes 221192 | tf_op jit(solution)/shard_map/ppermute | solution.py:326
